TPU v7x, 256 devices: a whole 4x4x8 slice. The times are simulated.
256 devices in a mesh: seq: 16 (over y_lo, x, core), grp: 16 (over z, y_hi).
Axes of the slice: x: 4, y: 4 (y_hi: 2, y_lo: 2; y = y_hi * 2 + y_lo), z: 8, core: 2. Of those that a mesh axis runs over, the one named last changes fastest.
Arguments:
- query_in: bfloat16 [32768, 8192], P('seq', 'grp'), may hold values from -6 to 6
- key_in: bfloat16 [32768, 8192], P('seq', 'grp'), may hold values from -6 to 6
- value_in: bfloat16 [32768, 8192], P('seq', 'grp'), may hold values from -6 to 6
- gate_in: bfloat16 [32768, 8192], P('seq', 'grp'), may hold values from -6 to 6
- norm_gain: float32 [8192], P('grp'), may hold values from 0.1 to 1.9
- head_owner: int32 [16], replicated, may hold values from 0 to 15, each once
Outputs:
- attn_out: bfloat16 [32768, 8192], P('seq', 'grp')
- decode_state: float32 [64, 128, 128], P('grp', 'seq')
Inputs may be any that keep to these rules, and one draw needn't show every extreme that they name: head_owner is a permutation of the head groups.
All inputs are finite; a program needn't handle non-finite values.
Results may differ from a plain program's by a relative error of at most 0.0095.
Values sent between devices are 32-bit elements; how exact they have to be, the bound alone decides.
No kernel may reach another device: no remote copies, remote signals or barrier semaphores. Data moves between devices by JAX's collectives and lax.ppermute only.
A program may use at most 128 MiB of HBM per device.

v0:
```python
import jax
import jax.numpy as jnp
from jax import lax
from jax.sharding import PartitionSpec as P

DH = 128


def carried_in(part, axis, combine, identity):
    place = lax.axis_index(axis)
    gathered = lax.all_gather(part, axis)
    state = jnp.zeros_like(part) + jnp.asarray(identity, part.dtype)

    def one(hop, state):
        return combine(state, lax.dynamic_index_in_dim(gathered, hop, 0, False))

    return lax.fori_loop(0, place, one, state)


def activate(arr):
    return jax.nn.silu(arr.astype(jnp.float32)).astype(jnp.bfloat16)


def body(query_in, key_in, value_in, gate_in, norm_gain, head_owner):
    seq_len, feature_width = query_in.shape
    head_count = feature_width // DH
    block_len = min(256, seq_len)
    block_count = seq_len // block_len
    highest = lax.Precision.HIGHEST
    q_act = activate(query_in).reshape(block_count, block_len, head_count, DH)
    k_act = activate(key_in).reshape(block_count, block_len, head_count, DH)
    v_act = activate(value_in).reshape(block_count, block_len, head_count, DH)
    kv_block = jnp.einsum("nbhd,nbhe->nhde", k_act, v_act, preferred_element_type=jnp.float32)
    local_state = jnp.sum(kv_block, axis=0)
    before = carried_in(local_state, "seq", jnp.add, jnp.zeros_like(local_state))
    total_rows = lax.psum_scatter(local_state, "seq", scatter_dimension=1, tiled=True)
    running = jnp.concatenate(
        [jnp.zeros_like(kv_block[:1]), jnp.cumsum(kv_block[:-1], axis=0)], axis=0
    )
    starts = before[None] + running
    starts_hi = starts.astype(jnp.bfloat16)
    starts_lo = (starts - starts_hi.astype(jnp.float32)).astype(jnp.bfloat16)
    causal = (
        jnp.arange(block_len, dtype=jnp.int32)[:, None]
        >= jnp.arange(block_len, dtype=jnp.int32)[None, :]
    ).astype(jnp.float32)
    scores = (
        jnp.einsum("nbhd,nchd->nhbc", q_act, k_act, preferred_element_type=jnp.float32) * causal
    ).astype(jnp.bfloat16)
    inside = jnp.einsum("nhbc,nche->nbhe", scores, v_act, preferred_element_type=jnp.float32)
    carried = jnp.einsum("nbhd,nhde->nbhe", q_act, starts_hi, preferred_element_type=jnp.float32)
    carried = carried + jnp.einsum(
        "nbhd,nhde->nbhe", q_act, starts_lo, preferred_element_type=jnp.float32
    )
    attn = (inside + carried).reshape(seq_len, feature_width)
    squares = lax.psum(jnp.sum(attn * attn, axis=-1), "grp")
    scale = lax.rsqrt(squares / (feature_width * lax.axis_size("grp")) + 1e-06)
    normed = attn * scale[:, None] * norm_gain * jax.nn.sigmoid(gate_in.astype(jnp.float32))
    attn_out = normed.astype(jnp.bfloat16)
    grp_index = lax.axis_index("grp")
    chosen = (head_owner == grp_index).astype(jnp.float32)
    decode_state = jnp.tensordot(
        chosen, lax.all_gather(total_rows[None], "grp", axis=0, tiled=True), 1, precision=highest
    )
    return (attn_out, decode_state)


def solution(mesh):
    return jax.shard_map(
        body,
        mesh=mesh,
        in_specs=(
            P("seq", "grp"),
            P("seq", "grp"),
            P("seq", "grp"),
            P("seq", "grp"),
            P("grp"),
            P(),
        ),
        out_specs=(P("seq", "grp"), P("grp", "seq", None)),
        check_vma=False,
    )
```

profile of v0, /device:TPU:14, one launch (start us, length us, event | category | flops | bytes accessed | tf_op | source)
XLA Modules:
  0.0 230.9 jit_solution(5158493496886420242)
XLA Ops:
  7.2 0.0 reduce-scatter.2.cloned.1.call-start
  7.2 2.9 %copy.28 = bf16[2048,512]{0,1:T(8,128)(2,1)S(1)} copy(bf16[2048,512]{1,0:T(8,128)(2,1)} %param.10) | data formatting | bytes 4194304 | tf_op args[2]
  10.2 1.2 fusion.3
  11.4 2.0 copy.48
  13.4 3.4 %copy.35 = bf16[8,256,4,128]{3,1,2,0:T(8,128)(2,1)S(1)} copy(bf16[8,256,4,128]{1,0,3,2:T(8,128)(2,1)} %bitcast.47) | data formatting | bytes 4194304 | tf_op jit(solution)/shard_map/reshape | solution.py:32
  16.8 4.5 %copy.30 = bf16[2048,512]{0,1:T(8,128)(2,1)} copy(bf16[2048,512]{1,0:T(8,128)(2,1)} %param.9) | data formatting | bytes 4194304 | tf_op args[1]
  21.4 2.8 %fusion.11 = bf16[2048,512]{0,1:T(8,128)(2,1)S(1)} fusion(bf16[2048,512]{0,1:T(8,128)(2,1)} %copy.30), kind=kLoop, calls=%fused_computation.19 | loop fusion | flops 6291456 | bytes 4194304 | tf_op jit(solution)/shard_map/convert_element_type | solution.py:21
  24.2 0.7 copy.50
  24.9 3.1 %fusion.36 = (f32[4,128,128]{2,1,0:T(8,128)}, f32[8,4,128,128]{3,2,1,0:T(8,128)}) fusion(bf16[8,256,4,128]{3,1,2,0:T(8,128)(2,1)S(1)} %copy.35, bf16[8,256,4,128]{1,0,3,2:T(8,128)(2,1)S(1)} %bitcast.42), kind=kOutput, calls=%fused_computation.48 | convolution fusion | flops 268894208 | bytes 6553600 | tf_op jit(solution)/shard_map/nbhd,nbhe->nhde/dot_general | solution.py:33
  28.0 0.0 reduce-scatter.2.cloned.1.call-update
  28.0 0.0 all-gather.4.cloned.1.call-start
  28.1 0.7 all-gather.4.cloned.1.call-update
  28.8 2.9 %copy.29 = bf16[2048,512]{0,1:T(8,128)(2,1)S(1)} copy(bf16[2048,512]{1,0:T(8,128)(2,1)} %param.8) | data formatting | bytes 4194304 | tf_op args[0]
  31.7 1.2 fusion.7
  33.0 2.0 copy.49
  35.0 3.4 %copy.31 = bf16[8,256,4,128]{3,1,2,0:T(8,128)(2,1)S(1)} copy(bf16[8,256,4,128]{1,0,3,2:T(8,128)(2,1)} %bitcast.50) | data formatting | bytes 4194304 | tf_op jit(solution)/shard_map/reshape | solution.py:30
  38.4 3.9 %copy.41 = bf16[2048,512]{0,1:T(8,128)(2,1)} copy(bf16[2048,512]{1,0:T(8,128)(2,1)} %param.11) | data formatting | bytes 4194304 | tf_op args[3]
  42.4 2.9 %fusion.21 = f32[7,4,128,128]{3,2,1,0:T(8,128)} fusion(f32[8,4,128,128]{3,2,1,0:T(8,128)} %get-tuple-element.39), kind=kOutput, calls=%fused_computation.32 | output fusion | flops 2752512 | bytes 3670016 | tf_op jit(solution)/shard_map/jit(cumsum)/reduce_window_sum | solution.py:38
  45.3 44.6 %reduce-scatter.2.cloned.1.call-done = f32[4,8,128]{2,1,0:T(8,128)} async-done(((f32[4,128,128]{2,1,0:T(8,128)}), f32[4,8,128]{2,1,0:T(8,128)}) %reduce-scatter.2.cloned.1.call-update) | async-done | bytes 16400 | tf_op jit(solution)/shard_map/reduce_scatter | solution.py:36
  89.9 42.5 %all-gather.1 = f32[64,8,128]{2,1,0:T(8,128)S(1)} all-gather(f32[4,8,128]{2,1,0:T(8,128)} %reduce-scatter.2.cloned.1.call-done), channel_id=3, replica_groups=mesh['seq'=16,'grp'=16] {'grp'}, dimensions={0}, use_global_device_ids=true | all-gather | bytes 278528 | tf_op jit(solution)/shard_map/all_gather | solution.py:63
  132.3 0.0 copy-done.5
  132.3 1.0 fusion.28
  133.3 0.4 all-gather.4.cloned.1.call-done
  133.8 14.7 %while.10 = (s32[]{:T(128)}, f32[4,128,128]{2,1,0:T(8,128)S(1)}, s32[]{:T(128)}, f32[16,4,128,128]{3,2,1,0:T(8,128)}, s32[]{:T(128)}, /*index=5*/s32[]{:T(128)}, s32[]{:T(128)}) while((s32[]{:T(128)}, f32[4,128,128]{2,1,0:T(8,128)S(1)}, s32[]{:T(128)}, f32[16,4,128,128]{3,2,1,0:T(8,128)}, s32[]{:T(128)}, /*index=5*/s32[]{:T(128)}, ...), condition=%wide.region_2.3_spmd, body=%wide.region_1.2_spmd.sunk | while | flops 65541 | bytes 786547 | solution.py:17
  133.8 1.0 bitcast_add_fusion.2
  134.8 1.0 bitcast_add_fusion.2
  135.9 1.0 bitcast_add_fusion.2
  136.9 1.0 bitcast_add_fusion.2
  138.0 1.0 bitcast_add_fusion.2
  139.0 1.0 bitcast_add_fusion.2
  140.0 1.0 bitcast_add_fusion.2
  141.1 1.0 bitcast_add_fusion.2
  142.1 1.0 bitcast_add_fusion.2
  143.1 1.0 bitcast_add_fusion.2
  144.2 1.0 bitcast_add_fusion.2
  145.2 1.0 bitcast_add_fusion.2
  146.3 1.0 bitcast_add_fusion.2
  147.3 1.0 bitcast_add_fusion.2
  148.5 4.3 %fusion.25 = f32[8,4,128,256]{3,2,1,0:T(8,128)} fusion(bf16[8,256,4,128]{3,1,2,0:T(8,128)(2,1)S(1)} %copy.31, f32[7,4,128,128]{3,2,1,0:T(8,128)} %fusion.21, f32[4,128,128]{2,1,0:T(8,128)S(1)} %get-tuple-element.25), kind=kOutput, calls=%fused_computation.35 | convolution fusion | flops 271056896 | bytes 8388608 | tf_op jit(solution)/shard_map/nbhd,nhde->nbhe/dot_general | solution.py:52
  152.8 2.7 %fusion.23 = f32[8,4,128,256]{3,2,1,0:T(8,128)} fusion(bf16[8,256,4,128]{3,1,2,0:T(8,128)(2,1)S(1)} %copy.31, f32[7,4,128,128]{3,2,1,0:T(8,128)S(1)} %copy-done.2, f32[4,128,128]{2,1,0:T(8,128)S(1)} %get-tuple-element.25), kind=kOutput, calls=%fused_computation.34 | convolution fusion | flops 269484032 | bytes 8388608 | tf_op jit(solution)/shard_map/nbhd,nhde->nbhe/dot_general | solution.py:51
  155.6 9.5 %multiply_reduce_fusion = (f32[8,256]{1,0:T(8,128)S(1)}, f32[8,256,4,128]{1,3,2,0:T(8,128)}) fusion(f32[8,4,128,256]{3,2,1,0:T(8,128)} %fusion.23, f32[8,4,128,256]{3,2,1,0:T(8,128)} %fusion.25, bf16[8,256,4,128]{3,1,2,0:T(8,128)(2,1)} %copy-done, f32[256,256]{1,0:T(8,128)S(1)} %fusion.30, bf16[8,256,4,128]{3,1,2,0:T(8,128)(2,1)S(1)} %copy.31, ...), kind=kOutput, calls=%fused_computation.22 | convolution fusion | flops 1082128384 | bytes 19144704 | tf_op jit(solution)/shard_map/nhbc,nche->nbhe/dot_general | solution.py:50
  165.0 4.6 %copy.40 = f32[8,256,4,128]{1,0,3,2:T(8,128)S(1)} copy(f32[8,256,4,128]{1,3,2,0:T(8,128)} %get-tuple-element.41) | data formatting | bytes 8388608 | tf_op jit(solution)/shard_map/add | solution.py:55
  169.6 0.0 copy-start.3
  169.7 0.0 copy-start.4
  169.7 3.9 %copy.51 = f32[64,8,8,256]{3,1,2,0:T(8,128)} copy(f32[64,8,8,256]{3,2,1,0:T(8,128)S(1)} %bitcast.45) | data formatting | bytes 8388608
  173.6 41.8 %psum.7 = f32[2048]{0:T(1024)S(1)} all-reduce(f32[2048]{0:T(1024)S(1)} %bitcast.54), channel_id=1, replica_groups=mesh['seq'=16,'grp'=16] {'grp'}, use_global_device_ids=true, to_apply=%region_5.6 | all-reduce | flops 2048 | bytes 16384 | tf_op jit(solution)/shard_map/psum | solution.py:56
  215.4 4.8 %multiply_convert_fusion.2 = bf16[2048,512]{0,1:T(8,128)(2,1)} fusion(bf16[2048,512]{0,1:T(8,128)(2,1)S(1)} %copy-done.3, f32[2048,512]{0,1:T(8,128)} %bitcast.44, f32[512]{0:T(512)S(1)} %copy-done.4, f32[2048]{0:T(1024)S(1)} %add_rsqrt_fusion), kind=kLoop, calls=%fused_computation.21 | loop fusion | flops 8388608 | bytes 8398848 | tf_op jit(solution)/shard_map/convert_element_type | solution.py:59
  220.2 3.9 %copy.42 = bf16[2048,512]{1,0:T(8,128)(2,1)} copy(bf16[2048,512]{0,1:T(8,128)(2,1)} %multiply_convert_fusion.2) | data formatting | bytes 4194304
  (13 shorter events, 0.1 us)
Async XLA Ops:
  7.2 82.7 %reduce-scatter.2.cloned.1.call-start = ((), (), s32[]{:S(2)}) async-start(), calls=%async_computation.1 | async-start | bytes 278528 | tf_op jit(solution)/shard_map/reduce_scatter | solution.py:36
  16.8 8.1 %copy-start = (bf16[8,256,4,128]{3,1,2,0:T(8,128)(2,1)}, bf16[8,256,4,128]{3,1,2,0:T(8,128)(2,1)S(1)}, u32[]{:S(2)}) copy-start(bf16[8,256,4,128]{3,1,2,0:T(8,128)(2,1)S(1)} %copy.35) | copy-start | bytes 6291460
  24.9 3.1 %copy-start.1 = (bf16[64,8,8,256]{3,2,1,0:T(8,128)(2,1)}, bf16[64,8,8,256]{3,2,1,0:T(8,128)(2,1)S(1)}, u32[]{:S(2)}) copy-start(bf16[64,8,8,256]{3,2,1,0:T(8,128)(2,1)S(1)} %copy.50) | copy-start | bytes 6291460
  28.0 105.7 %all-gather.4.cloned.1.call-start = ((), (), s32[]{:S(2)}) async-start(), calls=%async_computation.2 | async-start | bytes 4456448 | tf_op jit(solution)/shard_map/all_gather | solution.py:11
  42.3 90.0 %copy-start.5 = (s32[16]{0:T(128)S(1)}, s32[16]{0:T(128)}, u32[]{:S(2)}) copy-start(s32[16]{0:T(128)} %param.13) | copy-start | bytes 196
  148.5 4.3 %copy-start.2 = (f32[7,4,128,128]{3,2,1,0:T(8,128)S(1)}, f32[7,4,128,128]{3,2,1,0:T(8,128)}, u32[]{:S(2)}) copy-start(f32[7,4,128,128]{3,2,1,0:T(8,128)} %fusion.21) | copy-start | bytes 5505028
  169.6 45.8 %copy-start.3 = (bf16[2048,512]{0,1:T(8,128)(2,1)S(1)}, bf16[2048,512]{0,1:T(8,128)(2,1)}, u32[]{:S(2)}) copy-start(bf16[2048,512]{0,1:T(8,128)(2,1)} %copy.41) | copy-start | bytes 6291460
  169.7 45.8 %copy-start.4 = (f32[512]{0:T(512)S(1)}, f32[512]{0:T(512)}, u32[]{:S(2)}) copy-start(f32[512]{0:T(512)} %param.12) | copy-start | bytes 6148
Sparse Core Ops, SparseCore 0:
  28.2 61.6 reduce-scatter.1
  91.9 41.8 all-gather.3
where the time goes:
time: 232 us; the launch traced here: 231 us
  blocking collectives  84.3 us (36%)
  waiting for transfers between devices  45.7 us (20%)
  local copies, waits for them, and re-layouts  38.4 us (17%)
  other arithmetic  27.1 us (12%)
  matrix products  20.6 us (9%)
  between operations  14.2 us (6%)
    reduce_scatter x1, waiting for transfers between devices, body(): lax.psum_scatter(local_state, 'seq', scatter_dimension=1, tiled=True)  44.6 us
    all_gather x1, blocking collectives, body(): lax.all_gather(total_rows[None], 'grp', axis=0, tiled=True)  42.5 us
    psum x1, blocking collectives, body(): squares = lax.psum(jnp.sum(attn * attn, axis=-1), 'grp')  41.8 us
    unnamed x22, local copies, waits for them, and re-layouts  26.9 us
    add x14, other arithmetic, one(): return combine(state, lax.dynamic_index_in_dim(gathered, hop, 0, False))  14.1 us
    dot_general x1, matrix products, body(): jnp.einsum('nhbc,nche->nbhe', scores, v_act, preferred_element_type=jnp.f...  9.46 us
    convert_element_type x3, other arithmetic, activate(): return jax.nn.silu(arr.astype(jnp.float32)).astype(jnp.bfloat16)  5.22 us
    convert_element_type x1, other arithmetic, body(): attn_out = normed.astype(jnp.bfloat16)  4.76 us
  transfers between devices with their start and end apart: 2, of which 2 were waited for; matrix products, arithmetic and copies ran while one was open for 8% of the time, Pallas kernels for 0%

commit v1 on v0

v1 whole, which is shorter than its diff:
```python
import functools

import jax
import jax.numpy as jnp
from jax import lax
from jax.experimental import pallas as pl
from jax.experimental.pallas import tpu as pltpu
from jax.sharding import PartitionSpec as P

DH = 128
F32 = jnp.float32
BF16 = jnp.bfloat16
MIB = 1 << 20


def dot(a, b, dims):
    return lax.dot_general(a, b, (dims, ((), ())), preferred_element_type=F32)


def silu(x):
    half = x.astype(F32) * 0.5
    return (half + half * jnp.tanh(half)).astype(BF16)


def params(mib):
    return pltpu.CompilerParams(vmem_limit_bytes=mib * MIB)


def cost(flops, nbytes, trans=0):
    return pl.CostEstimate(flops=flops, bytes_accessed=nbytes, transcendentals=trans)


def state_kernel(heads, shards, k_ref, v_ref, out_ref, acc):
    step = pl.program_id(0)

    @pl.when(step == 0)
    def _():
        acc[...] = jnp.zeros_like(acc)

    for h in range(heads):
        cols = slice(h * DH, (h + 1) * DH)
        k = silu(k_ref[:, cols])
        v = silu(v_ref[:, cols])
        acc[h] += dot(k, v, ((0,), (0,)))

    @pl.when(step == pl.num_programs(0) - 1)
    def _():
        rows = DH // shards
        for j in range(shards):
            for h in range(heads):
                out_ref[j, h] = acc[h, j * rows : (j + 1) * rows]


def prefix_kernel(shards, part_ref, before_ref, total_ref):
    run = jnp.zeros(part_ref.shape[1:], F32)
    for j in range(shards):
        before_ref[j] = run
        run = run + part_ref[j]
    total_ref[...] = run


def inside_kernel(heads, q_ref, k_ref, v_ref, base_ref, qa_ref, run):
    step = pl.program_id(0)

    @pl.when(step == 0)
    def _():
        run[...] = jnp.zeros_like(run)

    n = q_ref.shape[0]
    causal = lax.broadcasted_iota(jnp.int32, (n, n), 0) >= lax.broadcasted_iota(
        jnp.int32, (n, n), 1
    )
    for h in range(heads):
        cols = slice(h * DH, (h + 1) * DH)
        q = silu(q_ref[:, cols])
        k = silu(k_ref[:, cols])
        v = silu(v_ref[:, cols])
        scores = jnp.where(causal, dot(q, k, ((1,), (1,))), 0.0).astype(BF16)
        state = run[h]
        hi = state.astype(BF16)
        lo = (state - hi.astype(F32)).astype(BF16)
        left = jnp.concatenate([scores, q, q], axis=1)
        right = jnp.concatenate([v, hi, lo], axis=0)
        base_ref[:, cols] = dot(left, right, ((1,), (0,)))
        qa_ref[:, cols] = q
        run[h] = state + dot(k, v, ((0,), (0,)))


def carry_kernel(
    heads, shards, owner_ref, base0_ref, base1_ref, qa0_ref, qa1_ref, before_ref, total_ref,
    attn_ref, send_ref, states, squares,
):
    step = pl.program_id(0)
    groups = send_ref.shape[0]
    half = heads // 2

    @pl.when(step == 0)
    def _():
        for h in range(heads):
            state = before_ref[:, h].reshape(DH, DH)
            hi = state.astype(BF16)
            states[h, :DH] = hi
            states[h, DH:] = (state - hi.astype(F32)).astype(BF16)

    sums = None
    for h in range(heads):
        cols = slice((h % half) * DH, (h % half + 1) * DH)
        base_ref, qa_ref = (base0_ref, qa0_ref) if h < half else (base1_ref, qa1_ref)
        q = qa_ref[:, cols]
        attn = base_ref[:, cols] + dot(
            jnp.concatenate([q, q], axis=1), states[h], ((1,), (0,))
        )
        attn_ref[:, h * DH : (h + 1) * DH] = attn
        sums = attn * attn if sums is None else sums + attn * attn
    tokens = sums.shape[0]
    for c in range(tokens // DH):
        column = jnp.sum(sums[c * DH : (c + 1) * DH], axis=1, keepdims=True)
        row = jnp.transpose(jnp.broadcast_to(column, (DH, DH)))[:1]
        squares[pl.ds(step * (tokens // DH) + c, 1), :] = row

    @pl.when(step == pl.num_programs(0) - 1)
    def _():
        token_rows = squares.shape[0]
        owner = owner_ref[lax.axis_index("grp")]
        mine = squares[...]
        rows = total_ref.shape[1]
        for g in range(groups):
            send_ref[g, :token_rows] = mine
            for h in range(heads):
                at = token_rows + h * rows
                send_ref[g, at : at + rows] = jnp.where(owner == g, total_ref[h], 0.0)


def gate_kernel(attn_ref, gate_ref, gain_ref, out_ref):
    sigmoid = 0.5 + 0.5 * jnp.tanh(gate_ref[...].astype(F32) * 0.5)
    out_ref[...] = attn_ref[...] * (gain_ref[...] * sigmoid)


def norm_kernel(heads, features, got_ref, gated_ref, out_ref, state_ref, scales):
    step = pl.program_id(0)
    groups = got_ref.shape[0]

    @pl.when(step == 0)
    def _():
        total = got_ref[0]
        for g in range(1, groups):
            total = total + got_ref[g]
        token_rows = scales.shape[0]
        scales[...] = lax.rsqrt(total[:token_rows] / features + 1e-6)
        rows = state_ref.shape[1]
        for h in range(heads):
            at = token_rows + h * rows
            state_ref[h] = total[at : at + rows]

    tokens = gated_ref.shape[0]
    for c in range(tokens // DH):
        row = scales[pl.ds(step * (tokens // DH) + c, 1), :]
        column = jnp.transpose(jnp.broadcast_to(row, (DH, DH)))[:, :1]
        part = slice(c * DH, (c + 1) * DH)
        out_ref[part, :] = (gated_ref[part, :] * column).astype(BF16)


def body(query_in, key_in, value_in, gate_in, norm_gain, head_owner):
    tokens, width = query_in.shape
    heads = width // DH
    half = heads // 2
    shards = lax.axis_size("seq")
    groups = lax.axis_size("grp")
    block = min(256, tokens)
    blocks = tokens // block
    rows = DH // shards
    token_rows = tokens // DH
    whole = lambda *shape: pl.BlockSpec(shape, lambda i: (0,) * len(shape))

    big = 2 * block
    part = pl.pallas_call(
        functools.partial(state_kernel, heads, shards),
        grid=(tokens // big,),
        in_specs=[pl.BlockSpec((big, width), lambda i: (i, 0))] * 2,
        out_specs=whole(shards, heads, rows, DH),
        out_shape=jax.ShapeDtypeStruct((shards, heads, rows, DH), F32),
        scratch_shapes=[pltpu.VMEM((heads, DH, DH), F32)],
        compiler_params=params(56),
        cost_estimate=cost(2 * tokens * width * DH, 4 * tokens * width),
        name="local_state",
    )(key_in, value_in)

    gathered = lax.all_to_all(part, "seq", 0, 0, tiled=True)

    def inside(pair):
        spec = pl.BlockSpec((block, half * DH), lambda i: (i, pair))
        out = pl.BlockSpec((block, half * DH), lambda i: (i, 0))
        return pl.pallas_call(
            functools.partial(inside_kernel, half),
            grid=(blocks,),
            in_specs=[spec] * 3,
            out_specs=[out] * 2,
            out_shape=[
                jax.ShapeDtypeStruct((tokens, half * DH), F32),
                jax.ShapeDtypeStruct((tokens, half * DH), BF16),
            ],
            scratch_shapes=[pltpu.VMEM((half, DH, DH), F32)],
            compiler_params=params(56),
            cost_estimate=cost(
                2 * tokens * half * DH * (2 * block + 3 * DH), 12 * tokens * half * DH
            ),
            name="inside%d" % pair,
        )(query_in, key_in, value_in)

    base0, qa0 = inside(0)
    base1, qa1 = inside(1)

    before_all, total = pl.pallas_call(
        functools.partial(prefix_kernel, shards),
        in_specs=[pl.BlockSpec(memory_space=pltpu.VMEM)],
        out_specs=[pl.BlockSpec(memory_space=pltpu.VMEM)] * 2,
        out_shape=[
            jax.ShapeDtypeStruct((shards, heads, rows, DH), F32),
            jax.ShapeDtypeStruct((heads, rows, DH), F32),
        ],
        compiler_params=params(4),
        name="prefix",
    )(gathered)
    before = lax.all_to_all(before_all, "seq", 0, 0, tiled=True)

    pair_spec = pl.BlockSpec((big, half * DH), lambda i: (i, 0))
    payload = token_rows + heads * rows
    attn, send = pl.pallas_call(
        functools.partial(carry_kernel, heads, shards),
        grid=(tokens // big,),
        in_specs=[
            pl.BlockSpec(memory_space=pltpu.SMEM),
            pair_spec, pair_spec, pair_spec, pair_spec,
            whole(shards, heads, rows, DH),
            whole(heads, rows, DH),
        ],
        out_specs=[
            pl.BlockSpec((big, width), lambda i: (i, 0)),
            whole(groups, payload, DH),
        ],
        out_shape=[
            jax.ShapeDtypeStruct((tokens, width), F32),
            jax.ShapeDtypeStruct((groups, payload, DH), F32),
        ],
        scratch_shapes=[
            pltpu.VMEM((heads, 2 * DH, DH), BF16),
            pltpu.VMEM((token_rows, DH), F32),
        ],
        compiler_params=params(56),
        cost_estimate=cost(4 * tokens * width * DH, 10 * tokens * width),
        name="carry",
    )(head_owner, base0, base1, qa0, qa1, before, total)

    got = lax.all_to_all(send, "grp", 0, 0, tiled=True)

    row_spec = pl.BlockSpec((big, width), lambda i: (i, 0))
    gated = pl.pallas_call(
        gate_kernel,
        grid=(tokens // big,),
        in_specs=[row_spec, row_spec, whole(1, width)],
        out_specs=row_spec,
        out_shape=jax.ShapeDtypeStruct((tokens, width), F32),
        compiler_params=params(56),
        cost_estimate=cost(4 * tokens * width, 10 * tokens * width),
        name="gate",
    )(attn, gate_in, norm_gain.reshape(1, width))

    attn_out, decode_state = pl.pallas_call(
        functools.partial(norm_kernel, heads, float(width * groups)),
        grid=(tokens // big,),
        in_specs=[whole(groups, payload, DH), row_spec],
        out_specs=[row_spec, whole(heads, rows, DH)],
        out_shape=[
            jax.ShapeDtypeStruct((tokens, width), BF16),
            jax.ShapeDtypeStruct((heads, rows, DH), F32),
        ],
        scratch_shapes=[pltpu.VMEM((token_rows, DH), F32)],
        compiler_params=params(56),
        cost_estimate=cost(2 * tokens * width, 6 * tokens * width),
        name="norm",
    )(got, gated)
    return attn_out, decode_state


def solution(mesh):
    return jax.shard_map(
        body,
        mesh=mesh,
        in_specs=(
            P("seq", "grp"),
            P("seq", "grp"),
            P("seq", "grp"),
            P("seq", "grp"),
            P("grp"),
            P(),
        ),
        out_specs=(P("seq", "grp"), P("grp", "seq", None)),
        check_vma=False,
    )
```

time: 232 us -> 81 us (0.35)
  the two profiles are of different devices: /device:TPU:14 before, /device:TPU:1 now
where the time goes in v1:
time: 81 us; the launch traced here: 79.4 us
  Pallas kernels  38.4 us (47%)
  starting transfers between devices  14.7 us (18%)
  blocking collectives  14 us (17%)
  waiting for transfers between devices  9.6 us (12%)
  local copies, waits for them, and re-layouts  2.06 us (3%)
    pallas_call x2, Pallas kernels, inside(): pl.pallas_call(functools.partial(inside_kernel, half), grid=(blocks,), in...  15.7 us
    all_to_all x1, blocking collectives, body(): gathered = lax.all_to_all(part, 'seq', 0, 0, tiled=True)  14 us
    all_to_all x1, starting transfers between devices, body(): got = lax.all_to_all(send, 'grp', 0, 0, tiled=True)  10.6 us
    all_to_all x1, waiting for transfers between devices, body(): got = lax.all_to_all(send, 'grp', 0, 0, tiled=True)  9.59 us
    pallas_call x1, Pallas kernels, body(): pl.pallas_call(functools.partial(carry_kernel, heads, shards), grid=(toke...  6.63 us
    pallas_call x1, Pallas kernels, body(): pl.pallas_call(gate_kernel, grid=(tokens // big,), in_specs=[row_spec, ro...  5.51 us
    pallas_call x1, Pallas kernels, body(): pl.pallas_call(functools.partial(state_kernel, heads, shards), grid=(toke...  5.04 us
    pallas_call x1, Pallas kernels, body(): pl.pallas_call(functools.partial(norm_kernel, heads, float(width * groups...  4.77 us
  transfers between devices with their start and end apart: 2, of which 1 were waited for; matrix products, arithmetic and copies ran while one was open for 0% of the time, Pallas kernels for 27%

profile of v1, /device:TPU:1, one launch (start us, length us, event | category | flops | bytes accessed | tf_op | source)
XLA Modules:
  0.0 79.4 jit_solution(12684949407043070882)
XLA Ops:
  0.6 5.0 %local_state.1 = f32[16,4,8,128]{3,2,1,0:T(8,128)} custom-call(bf16[2048,512]{1,0:T(8,128)(2,1)} %k_ref.5, bf16[2048,512]{1,0:T(8,128)(2,1)} %v_ref.5), custom_call_target="tpu_custom_call" | custom-call | flops 268435456 | bytes 4194304 | tf_op jit(solution)/shard_map/local_state/pallas_call | solution.py:176
  5.7 14.0 %all_to_all.15.part_ref = f32[16,4,8,128]{3,2,1,0:T(8,128)S(1)} all-to-all(f32[16,4,8,128]{3,2,1,0:T(8,128)} %local_state.1), channel_id=1, replica_groups=mesh['seq'=16,'grp'=16] {'seq'}, dimensions={0} | all-to-all | bytes 524288 | tf_op jit(solution)/shard_map/all_to_all | solution.py:188
  19.7 0.7 prefix.1
  20.4 0.0 copy-start
  20.4 0.6 copy-done
  21.0 4.1 %all-to-all-start.1 = ((f32[16,4,8,128]{3,2,1,0:T(8,128)}), f32[16,4,8,128]{3,2,1,0:T(8,128)S(1)}, u32[]{:S(2)}, u32[]{:S(2)}) async-start(f32[16,4,8,128]{3,2,1,0:T(8,128)} %get-tuple-element.14), calls=%async_computation.1 | async-start | bytes 524288 | tf_op jit(solution)/shard_map/all_to_all | solution.py:224
  25.1 7.9 %inside1.1 = (f32[2048,256]{1,0:T(8,128)}, bf16[2048,256]{1,0:T(8,128)(2,1)}) custom-call(bf16[2048,512]{1,0:T(8,128)(2,1)} %q_ref.3, bf16[2048,512]{1,0:T(8,128)(2,1)} %k_ref.5, bf16[2048,512]{1,0:T(8,128)(2,1)} %v_ref.5), custom_call_target="tpu_custom_call" | custom-call | flops 939524096 | bytes 6291456 | tf_op jit(solution)/shard_map/inside1/pallas_call | solution.py:193
  33.0 7.8 %inside0.1 = (f32[2048,256]{1,0:T(8,128)}, bf16[2048,256]{1,0:T(8,128)(2,1)}) custom-call(bf16[2048,512]{1,0:T(8,128)(2,1)} %q_ref.3, bf16[2048,512]{1,0:T(8,128)(2,1)} %k_ref.5, bf16[2048,512]{1,0:T(8,128)(2,1)} %v_ref.5), custom_call_target="tpu_custom_call" | custom-call | flops 939524096 | bytes 6291456 | tf_op jit(solution)/shard_map/inside0/pallas_call | solution.py:193
  40.8 0.0 all-to-all-done.1.before_ref
  40.8 0.0 copy-start.2
  40.8 0.7 copy-done.2
  41.5 6.6 %carry.1 = (f32[2048,512]{1,0:T(8,128)}, f32[16,48,128]{2,1,0:T(8,128)}) custom-call(s32[16]{0:T(128)} %owner_ref.1, f32[2048,256]{1,0:T(8,128)} %get-tuple-element.10.base0_ref, f32[2048,256]{1,0:T(8,128)} %get-tuple-element.11.base1_ref, bf16[2048,256]{1,0:T(8,128)(2,1)} %get-tuple-element.12.qa0_ref, bf16[2048,256]{1,0:T(8,128)(2,1)} %get-tuple-element.13.qa1_ref, ...), custom_call_target="tpu_custom_call" | custom-call | flops 536870912 | bytes 10485760 | tf_op jit(solution)/shard_map/carry/pallas_call | solution.py:228
  48.2 10.6 %all-to-all-start.2 = ((f32[16,48,128]{2,1,0:T(8,128)}), f32[16,48,128]{2,1,0:T(8,128)S(1)}, u32[]{:S(2)}, u32[]{:S(2)}) async-start(f32[16,48,128]{2,1,0:T(8,128)} %get-tuple-element.16), calls=%async_computation.2 | async-start | bytes 786432 | tf_op jit(solution)/shard_map/all_to_all | solution.py:254
  58.8 5.5 %gate.1.gated_ref = f32[2048,512]{1,0:T(8,128)} custom-call(f32[2048,512]{1,0:T(8,128)} %get-tuple-element.17.attn_ref, bf16[2048,512]{1,0:T(8,128)(2,1)} %gate_ref.1, f32[1,512]{1,0:T(1,128)} %bitcast.1), custom_call_target="tpu_custom_call" | custom-call | flops 4194304 | bytes 10485760 | tf_op jit(solution)/shard_map/gate/pallas_call | solution.py:257
  64.3 9.6 %all-to-all-done.2.got_ref = f32[16,48,128]{2,1,0:T(8,128)S(1)} async-done(((f32[16,48,128]{2,1,0:T(8,128)}), f32[16,48,128]{2,1,0:T(8,128)S(1)}, u32[]{:S(2)}, u32[]{:S(2)}) %all-to-all-start.2) | async-done | bytes 393248 | tf_op jit(solution)/shard_map/all_to_all | solution.py:254
  73.9 0.0 copy-start.1
  73.9 0.7 copy-done.1
  74.7 4.8 %norm.1 = (bf16[2048,512]{1,0:T(8,128)(2,1)}, f32[4,8,128]{2,1,0:T(8,128)}) custom-call(f32[16,48,128]{2,1,0:T(8,128)} %copy-done.1, f32[2048,512]{1,0:T(8,128)} %gate.1.gated_ref), custom_call_target="tpu_custom_call" | custom-call | flops 2097152 | bytes 6291456 | tf_op jit(solution)/shard_map/norm/pallas_call | solution.py:268
Async XLA Ops:
  20.4 0.6 copy-start
  21.0 19.8 %all-to-all-start.1 = ((f32[16,4,8,128]{3,2,1,0:T(8,128)}), f32[16,4,8,128]{3,2,1,0:T(8,128)S(1)}, u32[]{:S(2)}, u32[]{:S(2)}) async-start(f32[16,4,8,128]{3,2,1,0:T(8,128)} %get-tuple-element.14), calls=%async_computation.1 | async-start | bytes 524288 | tf_op jit(solution)/shard_map/all_to_all | solution.py:224
  40.8 0.7 copy-start.2
  48.2 25.7 %all-to-all-start.2 = ((f32[16,48,128]{2,1,0:T(8,128)}), f32[16,48,128]{2,1,0:T(8,128)S(1)}, u32[]{:S(2)}, u32[]{:S(2)}) async-start(f32[16,48,128]{2,1,0:T(8,128)} %get-tuple-element.16), calls=%async_computation.2 | async-start | bytes 786432 | tf_op jit(solution)/shard_map/all_to_all | solution.py:254
  73.9 0.7 copy-start.1

commit v2 on v0

v2 whole, which is shorter than its diff:
```python
import functools

import jax
import jax.numpy as jnp
from jax import lax
from jax.experimental import pallas as pl
from jax.experimental.pallas import tpu as pltpu
from jax.sharding import PartitionSpec as P

DH = 128
F32 = jnp.float32
BF16 = jnp.bfloat16
MIB = 1 << 20
VMEM = pl.BlockSpec(memory_space=pltpu.VMEM)
SMEM = pl.BlockSpec(memory_space=pltpu.SMEM)
HBM = pl.BlockSpec(memory_space=pltpu.HBM)


def dot(a, b, dims):
    return lax.dot_general(a, b, (dims, ((), ())), preferred_element_type=F32)


def silu(x):
    half = x.astype(F32) * 0.5
    return (half + half * jnp.tanh(half)).astype(BF16)


def params(mib):
    return pltpu.CompilerParams(vmem_limit_bytes=mib * MIB)


def cost(flops, nbytes, trans=0):
    return pl.CostEstimate(flops=flops, bytes_accessed=nbytes, transcendentals=trans)


def in_hbm(x):
    return pltpu.with_memory_space_constraint(x, pltpu.HBM)


def cols_of(h):
    return slice(h * DH, (h + 1) * DH)


def state_kernel(heads, chunk, k_hbm, v_hbm, ka_ref, va_ref, give_ref, mine_ref, k_in, v_in, acc, sems):
    count = k_in.shape[0] // chunk
    copies = []
    for c in range(count):
        part = pl.ds(c * chunk, chunk)
        pair = [
            pltpu.make_async_copy(k_hbm.at[part], k_in.at[part], sems.at[0, c]),
            pltpu.make_async_copy(v_hbm.at[part], v_in.at[part], sems.at[1, c]),
        ]
        for copy in pair:
            copy.start()
        copies.append(pair)
    for c in range(count):
        part = slice(c * chunk, (c + 1) * chunk)
        for copy in copies[c]:
            copy.wait()
        for h in range(heads):
            k = silu(k_in[part, cols_of(h)])
            v = silu(v_in[part, cols_of(h)])
            ka_ref[part, cols_of(h)] = k
            va_ref[part, cols_of(h)] = v
            new = dot(k, v, ((0,), (0,)))
            acc[h] = new if c == 0 else acc[h] + new
    half = heads // 2
    core = lax.rem(lax.axis_index("seq"), 2)
    for i in range(half):
        give_ref[i] = acc[(1 - core) * half + i]
        mine_ref[i] = acc[core * half + i]


def pair_kernel(mine_ref, other_ref, out_ref):
    out_ref[...] = mine_ref[...] + other_ref[...]


def along_x_kernel(chips, own_ref, *refs):
    got, (before_ref, all_ref) = refs[: chips - 1], refs[chips - 1 :]
    x = lax.rem(lax.div(lax.axis_index("seq"), 2), chips)
    total = own_ref[...]
    before = jnp.zeros_like(total)
    for back in range(1, chips):
        part = got[back - 1][...]
        total = total + part
        before = before + jnp.where(x >= back, part, 0.0)
    before_ref[...] = before
    all_ref[...] = total


def along_y_kernel(chips, before_ref, all_ref, over_ref, mine_ref, other_ref, keep_ref, send_ref):
    at = lax.axis_index("seq")
    core = lax.rem(at, 2)
    y = lax.div(at, 2 * chips)
    before = before_ref[...] + jnp.where(y > 0, over_ref[...], 0.0)
    keep_ref[:, :DH] = before + jnp.where(core > 0, other_ref[...], 0.0)
    send_ref[:, :DH] = before + jnp.where(core > 0, 0.0, mine_ref[...])
    rows = keep_ref.shape[1] - DH
    partner = at + 1 - 2 * core
    for i in range(keep_ref.shape[0]):
        for ref, place in ((keep_ref, at), (send_ref, partner)):
            some = pl.ds(pl.multiple_of(place * rows, 8), rows)
            ref[i, DH:] = all_ref[i, some] + over_ref[i, some]


def inside_kernel(first, heads, block, q_hbm, ka_ref, va_ref, run_in, base_ref, qa_ref, run_ref, q_in, sems):
    count = q_in.shape[0] // block

    def copy(n):
        return pltpu.make_async_copy(
            q_hbm.at[pl.ds((first + n) * block, block)], q_in.at[pl.ds(n * block, block)], sems.at[n]
        )

    for n in range(count):
        copy(n).start()
    run_ref[...] = run_in[...]
    causal = lax.broadcasted_iota(jnp.int32, (block, block), 0) >= lax.broadcasted_iota(
        jnp.int32, (block, block), 1
    )

    @pl.loop(0, count)
    def _(n):
        copy(n).wait()
        part = pl.ds(pl.multiple_of(n * block, block), block)
        whole = pl.ds(pl.multiple_of((first + n) * block, block), block)
        for h in range(heads):
            q = silu(q_in[part, cols_of(h)])
            k = ka_ref[whole, cols_of(h)]
            v = va_ref[whole, cols_of(h)]
            scores = jnp.where(causal, dot(q, k, ((1,), (1,))), 0.0).astype(BF16)
            state = run_ref[h]
            hi = state.astype(BF16)
            lo = (state - hi.astype(F32)).astype(BF16)
            left = jnp.concatenate([scores, q, q], axis=1)
            right = jnp.concatenate([v, hi, lo], axis=0)
            base_ref[part, cols_of(h)] = dot(left, right, ((1,), (0,)))
            qa_ref[part, cols_of(h)] = q
            run_ref[h] = state + dot(k, v, ((0,), (0,)))


def gate_kernel(block, gate_hbm, gain_ref, out_ref, gate_in, sems):
    tokens = gate_in.shape[0]
    count = tokens // block

    def copy(n):
        part = pl.ds(n * block, block)
        return pltpu.make_async_copy(gate_hbm.at[part], gate_in.at[part], sems.at[n])

    for n in range(count):
        copy(n).start()

    @pl.loop(0, count)
    def _(n):
        copy(n).wait()
        part = pl.ds(pl.multiple_of(n * block, block), block)
        sigmoid = 0.5 + 0.5 * jnp.tanh(gate_in[part].astype(F32) * 0.5)
        out_ref[part] = gain_ref[...] * sigmoid


def carry_kernel(
    heads, block, owner_ref, base0_ref, base1_ref, qa0_ref, qa1_ref, keep_ref, got_ref, gate_ref,
    gated_ref, send_ref, states, squares,
):
    half = heads // 2
    core = lax.rem(lax.axis_index("seq"), 2)
    for i in range(half):
        for ref, h in ((keep_ref, core * half + i), (got_ref, (1 - core) * half + i)):
            state = ref[i, :DH]
            hi = state.astype(BF16)
            states[h, :DH] = hi
            states[h, DH:] = (state - hi.astype(F32)).astype(BF16)
    ones = jnp.ones((16, 2 * DH), BF16)
    per = block // DH
    first = 0
    for base_ref, qa_ref in ((base0_ref, qa0_ref), (base1_ref, qa1_ref)):

        @pl.loop(0, base_ref.shape[0] // block)
        def _(n):
            part = pl.ds(pl.multiple_of(n * block, block), block)
            whole = pl.ds(pl.multiple_of((first + n) * block, block), block)
            sums = None
            for h in range(heads):
                q = qa_ref[part, cols_of(h)]
                attn = base_ref[part, cols_of(h)] + dot(
                    jnp.concatenate([q, q], axis=1), states[h], ((1,), (0,))
                )
                gated_ref[whole, cols_of(h)] = attn * gate_ref[whole, cols_of(h)]
                sums = attn * attn if sums is None else sums + attn * attn
            hi = sums.astype(BF16)
            lo = (sums - hi.astype(F32)).astype(BF16)
            across = dot(ones, jnp.concatenate([hi, lo], axis=1), ((1,), (1,)))
            for c in range(per):
                squares[pl.ds((first + n) * per + c, 1), :] = across[:1, c * DH : (c + 1) * DH]

        first += base_ref.shape[0] // block

    token_rows = squares.shape[0]
    owner = owner_ref[lax.axis_index("grp")]
    mine = squares[...]
    rows = keep_ref.shape[1] - DH
    low = [jnp.where(core == 0, keep_ref[i, DH:], got_ref[i, DH:]) for i in range(half)]
    high = [jnp.where(core == 0, got_ref[i, DH:], keep_ref[i, DH:]) for i in range(half)]
    for g in range(send_ref.shape[0]):
        send_ref[g, :token_rows] = mine
        for h, final in enumerate(low + high):
            at = token_rows + h * rows
            send_ref[g, at : at + rows] = jnp.where(owner == g, final, 0.0)


def norm_kernel(heads, features, block, got_ref, gated_ref, out_hbm, state_ref, out, scales, sems):
    total = got_ref[0]
    for g in range(1, got_ref.shape[0]):
        total = total + got_ref[g]
    rows = state_ref.shape[1]
    tokens = out.shape[0]
    token_rows = tokens // DH
    scales[...] = jnp.zeros_like(scales)
    scales[:token_rows] = lax.rsqrt(total[:token_rows] / features + 1e-6)
    columns = jnp.transpose(scales[...])
    copies = []
    for n in range(tokens // block):
        for c in range(n * block // DH, (n + 1) * block // DH):
            part = slice(c * DH, (c + 1) * DH)
            out[part] = (gated_ref[part] * columns[:, c : c + 1]).astype(BF16)
        part = pl.ds(n * block, block)
        copies.append(pltpu.make_async_copy(out.at[part], out_hbm.at[part], sems.at[n]))
        copies[-1].start()
    for h in range(heads):
        at = token_rows + h * rows
        state_ref[h] = total[at : at + rows]
    for copy in copies:
        copy.wait()


def body(query_in, key_in, value_in, gate_in, norm_gain, head_owner):
    tokens, width = query_in.shape
    heads = width // DH
    half = heads // 2
    shards = lax.axis_size("seq")
    groups = lax.axis_size("grp")
    chips = 4
    block = min(256, tokens)
    count = tokens // block
    chunk = 2 * block
    rows = DH // shards
    token_rows = tokens // DH
    pair_state = pltpu.VMEM((half, DH, DH), F32)
    dma = lambda *shape: pltpu.SemaphoreType.DMA(shape)
    limit = params(24)

    ka, va, give, mine = pl.pallas_call(
        functools.partial(state_kernel, heads, chunk),
        in_specs=[HBM, HBM],
        out_specs=[VMEM] * 4,
        out_shape=[pltpu.VMEM((tokens, width), BF16)] * 2 + [pair_state] * 2,
        scratch_shapes=[
            pltpu.VMEM((tokens, width), BF16),
            pltpu.VMEM((tokens, width), BF16),
            pltpu.VMEM((heads, DH, DH), F32),
            dma(2, tokens // chunk),
        ],
        compiler_params=limit,
        cost_estimate=cost(2 * tokens * width * DH, 4 * tokens * width),
        name="local_state",
    )(in_hbm(key_in), in_hbm(value_in))

    def swap(x, bit):
        return lax.ppermute(x, "seq", [(i, i ^ bit) for i in range(shards)])

    def on_x(x, k):
        place = lambda i: i - i % (2 * chips) + (i + 2 * k) % (2 * chips)
        return lax.ppermute(x, "seq", [(i, place(i)) for i in range(shards)])

    def inside(first, blocks, q, ka, va, run):
        part = blocks * block
        return pl.pallas_call(
            functools.partial(inside_kernel, first, heads, block),
            in_specs=[HBM, VMEM, VMEM, VMEM],
            out_specs=[VMEM] * 3,
            out_shape=[
                pltpu.VMEM((part, width), F32),
                pltpu.VMEM((part, width), BF16),
                pltpu.VMEM((heads, DH, DH), F32),
            ],
            scratch_shapes=[pltpu.VMEM((part, width), BF16), dma(blocks)],
            compiler_params=limit,
            cost_estimate=cost(2 * part * width * (2 * block + 3 * DH), 12 * part * width),
            name="inside%d" % first,
        )(in_hbm(q), ka, va, run)

    cut = 5 * count // 8
    other = swap(give, 1)
    pair = pl.pallas_call(
        pair_kernel, in_specs=[VMEM] * 2, out_specs=VMEM, out_shape=pair_state,
        compiler_params=limit, name="pair",
    )(mine, other)
    around = [on_x(pair, k) for k in range(1, chips)]
    ka, va, _ = lax.optimization_barrier((ka, va, pair))
    base0, qa0, run = inside(0, cut, query_in, ka, va, jnp.zeros((heads, DH, DH), F32))
    base0, *around = lax.optimization_barrier((base0, *around))
    before_x, all_x = pl.pallas_call(
        functools.partial(along_x_kernel, chips),
        in_specs=[VMEM] * chips, out_specs=[VMEM] * 2, out_shape=[pair_state] * 2,
        compiler_params=limit, name="along_x",
    )(pair, *around)
    over = swap(all_x, 2 * chips)
    run, _ = lax.optimization_barrier((run, all_x))
    base1, qa1, _ = inside(cut, count - cut, query_in, ka, va, run)
    base1, over = lax.optimization_barrier((base1, over))
    keep, send_core = pl.pallas_call(
        functools.partial(along_y_kernel, chips),
        in_specs=[VMEM] * 5, out_specs=[VMEM] * 2,
        out_shape=[pltpu.VMEM((half, DH + rows, DH), F32)] * 2,
        compiler_params=limit, name="along_y",
    )(before_x, all_x, over, mine, other)
    got_core = swap(send_core, 1)

    gate = pl.pallas_call(
        functools.partial(gate_kernel, block),
        in_specs=[HBM, VMEM],
        out_specs=VMEM,
        out_shape=pltpu.VMEM((tokens, width), F32),
        scratch_shapes=[pltpu.VMEM((tokens, width), BF16), dma(count)],
        compiler_params=limit,
        cost_estimate=cost(4 * tokens * width, 6 * tokens * width),
        name="gate",
    )(in_hbm(gate_in), norm_gain.reshape(1, width))

    payload = token_rows + heads * rows
    gated, send = pl.pallas_call(
        functools.partial(carry_kernel, heads, block),
        in_specs=[SMEM] + [VMEM] * 7,
        out_specs=[VMEM] * 2,
        out_shape=[
            pltpu.VMEM((tokens, width), F32),
            pltpu.VMEM((groups, payload, DH), F32),
        ],
        scratch_shapes=[
            pltpu.VMEM((heads, 2 * DH, DH), BF16),
            pltpu.VMEM((token_rows, DH), F32),
        ],
        compiler_params=limit,
        cost_estimate=cost(4 * tokens * width * DH, 10 * tokens * width),
        name="carry",
    )(head_owner, base0, base1, qa0, qa1, keep, got_core, gate)

    got = lax.all_to_all(send, "grp", 0, 0, tiled=True)

    attn_out, decode_state = pl.pallas_call(
        functools.partial(norm_kernel, heads, float(width * groups), block),
        in_specs=[VMEM, VMEM],
        out_specs=[HBM, VMEM],
        out_shape=[
            jax.ShapeDtypeStruct((tokens, width), BF16),
            jax.ShapeDtypeStruct((heads, rows, DH), F32),
        ],
        scratch_shapes=[
            pltpu.VMEM((tokens, width), BF16),
            pltpu.VMEM((DH, DH), F32),
            dma(count),
        ],
        compiler_params=limit,
        cost_estimate=cost(2 * tokens * width, 6 * tokens * width),
        name="norm",
    )(got, gated)
    return attn_out, decode_state


def solution(mesh):
    return jax.shard_map(
        body,
        mesh=mesh,
        in_specs=(
            P("seq", "grp"),
            P("seq", "grp"),
            P("seq", "grp"),
            P("seq", "grp"),
            P("grp"),
            P(),
        ),
        out_specs=(P("seq", "grp"), P("grp", "seq", None)),
        check_vma=False,
    )
```

time: 232 us -> 59.7 us (0.26)
  the two profiles are of different devices: /device:TPU:14 before, /device:TPU:1 now
where the time goes in v2:
time: 59.7 us; the launch traced here: 59.6 us
  blocking collectives  25.8 us (43%)
  Pallas kernels  22.5 us (38%)
  starting transfers between devices  9.32 us (16%)
  waiting for transfers between devices  1.12 us (2%)
  between operations  0.74 us (1%)
    all_to_all x1, blocking collectives, body(): got = lax.all_to_all(send, 'grp', 0, 0, tiled=True)  25.8 us
    pallas_call x2, Pallas kernels, inside(): pl.pallas_call(functools.partial(inside_kernel, first, heads, block), in_...  10.3 us
    ppermute x3, starting transfers between devices, swap(): return lax.ppermute(x, 'seq', [(i, i ^ bit) for i in range(shards)])  6.18 us
    pallas_call x1, Pallas kernels, body(): pl.pallas_call(functools.partial(state_kernel, heads, chunk), in_specs=[H...  3.99 us
    pallas_call x1, Pallas kernels, body(): pl.pallas_call(functools.partial(carry_kernel, heads, block), in_specs=[S...  3.94 us
    ppermute x3, starting transfers between devices, on_x(): return lax.ppermute(x, 'seq', [(i, place(i)) for i in range(shards)])  3.15 us
    pallas_call x1, Pallas kernels, body(): pl.pallas_call(functools.partial(norm_kernel, heads, float(width * groups...  2.28 us
    pallas_call x1, Pallas kernels, body(): pl.pallas_call(functools.partial(gate_kernel, block), in_specs=[HBM, VMEM...  1.91 us
  transfers between devices with their start and end apart: 6, of which 2 were waited for; matrix products, arithmetic and copies ran while one was open for 0% of the time, Pallas kernels for 20%

profile of v2, /device:TPU:1, one launch (start us, length us, event | category | flops | bytes accessed | tf_op | source)
XLA Modules:
  0.0 59.6 jit_solution(3645554570563179719)
XLA Ops:
  0.6 4.0 %local_state.1 = (bf16[2048,512]{1,0:T(8,128)(2,1)S(1)}, bf16[2048,512]{1,0:T(8,128)(2,1)S(1)}, f32[2,128,128]{2,1,0:T(8,128)S(1)}, f32[2,128,128]{2,1,0:T(8,128)S(1)}) custom-call(bf16[2048,512]{1,0:T(8,128)(2,1)} %k_hbm.1, bf16[2048,512]{1,0:T(8,128)(2,1)} %v_hbm.1), custom_call_target="tpu_custom_call" | custom-call | flops 268435456 | bytes 4194304 | tf_op jit(solution)/shard_map/local_state/pallas_call | solution.py:251
  4.6 3.3 %collective-permute-start = (f32[2,128,128]{2,1,0:T(8,128)S(1)}, f32[2,128,128]{2,1,0:T(8,128)S(1)}, u32[]{:S(2)}, u32[]{:S(2)}) collective-permute-start(f32[2,128,128]{2,1,0:T(8,128)S(1)} %get-tuple-element.29), channel_id=1, source_target_pairs={{0,16},{16,0},{32,48},{48,32},{64,80},{80,64},{96,112},{112,96},{1... | collective-permute-start | bytes 393224 | tf_op jit(solution)/shard_map/ppermute | solution.py:268
  8.0 1.0 %collective-permute-done.other_ref = f32[2,128,128]{2,1,0:T(8,128)S(1)} collective-permute-done((f32[2,128,128]{2,1,0:T(8,128)S(1)}, f32[2,128,128]{2,1,0:T(8,128)S(1)}, u32[]{:S(2)}, u32[]{:S(2)}) %collective-permute-start) | collective-permute-done | bytes 131104 | tf_op jit(solution)/shard_map/ppermute | solution.py:268
  9.0 0.1 collective-permute-start.1
  9.1 1.9 %collective-permute-start.2 = (f32[2,128,128]{2,1,0:T(8,128)S(1)}, f32[2,128,128]{2,1,0:T(8,128)S(1)}, u32[]{:S(2)}, u32[]{:S(2)}) collective-permute-start(f32[2,128,128]{2,1,0:T(8,128)S(1)} %pair.1.own_ref), channel_id=1, source_target_pairs={{0,64},{16,80},{32,96},{48,112},{64,0},{80,16},{96,32},{112,48},{1... | collective-permute-start | bytes 393224 | tf_op jit(solution)/shard_map/ppermute | solution.py:272
  11.0 1.2 %collective-permute-start.3 = (f32[2,128,128]{2,1,0:T(8,128)S(1)}, f32[2,128,128]{2,1,0:T(8,128)S(1)}, u32[]{:S(2)}, u32[]{:S(2)}) collective-permute-start(f32[2,128,128]{2,1,0:T(8,128)S(1)} %pair.1.own_ref), channel_id=1, source_target_pairs={{0,96},{16,112},{32,0},{48,16},{64,32},{80,48},{96,64},{112,80},{1... | collective-permute-start | bytes 393224 | tf_op jit(solution)/shard_map/ppermute | solution.py:272
  12.1 5.8 %inside0.1 = (f32[1280,512]{1,0:T(8,128)S(1)}, bf16[1280,512]{1,0:T(8,128)(2,1)S(1)}, f32[4,128,128]{2,1,0:T(8,128)S(1)}) custom-call(bf16[2048,512]{1,0:T(8,128)(2,1)} %q_hbm.3, bf16[2048,512]{1,0:T(8,128)(2,1)S(1)} %get-tuple-element.30.ka_ref, bf16[2048,512]{1,0:T(8,128)(2,1)S(1)} %get-tuple-element.31.va_ref, f32[4,128,128]{2,1,0:T(8,128)S(1)} %broadcast_in_dim.3.run_in), custom_call_target="tpu_custom_call" | custom-call | flops 1174405120 | bytes 7864320 | tf_op jit(solution)/shard_map/inside0/pallas_call | solution.py:276
  17.9 0.0 collective-permute-done.1.refs_0_
  17.9 0.0 collective-permute-done.2.refs_1_
  17.9 0.1 collective-permute-done.3.refs_2_
  18.1 1.3 %collective-permute-start.4 = (f32[2,128,128]{2,1,0:T(8,128)S(1)}, f32[2,128,128]{2,1,0:T(8,128)S(1)}, u32[]{:S(2)}, u32[]{:S(2)}) collective-permute-start(f32[2,128,128]{2,1,0:T(8,128)S(1)} %get-tuple-element.38.all_ref), channel_id=1, source_target_pairs={{0,128},{16,144},{32,160},{48,176},{64,192},{80,208},{96,224},{112... | collective-permute-start | bytes 393224 | tf_op jit(solution)/shard_map/ppermute | solution.py:268
  19.4 0.0 copy-start
  19.4 4.5 %inside5.1 = (f32[768,512]{1,0:T(8,128)S(1)}, bf16[768,512]{1,0:T(8,128)(2,1)S(1)}, f32[4,128,128]{2,1,0:T(8,128)}) custom-call(bf16[2048,512]{1,0:T(8,128)(2,1)} %q_hbm.3, bf16[2048,512]{1,0:T(8,128)(2,1)S(1)} %get-tuple-element.30.ka_ref, bf16[2048,512]{1,0:T(8,128)(2,1)S(1)} %get-tuple-element.31.va_ref, f32[4,128,128]{2,1,0:T(8,128)S(1)} %get-tuple-element.39.run_in), custom_call_target="tpu_custom_call" | custom-call | flops 704643072 | bytes 4718592 | tf_op jit(solution)/shard_map/inside5/pallas_call | solution.py:276
  23.9 0.0 collective-permute-done.4.over_ref
  24.0 0.1 along_y.1
  24.0 1.6 %collective-permute-start.5 = (f32[2,136,128]{2,1,0:T(8,128)S(1)}, f32[2,136,128]{2,1,0:T(8,128)S(1)}, u32[]{:S(2)}, u32[]{:S(2)}) collective-permute-start(f32[2,136,128]{2,1,0:T(8,128)S(1)} %get-tuple-element.47), channel_id=1, source_target_pairs={{0,16},{16,0},{32,48},{48,32},{64,80},{80,64},{96,112},{112,96},{1... | collective-permute-start | bytes 417800 | tf_op jit(solution)/shard_map/ppermute | solution.py:268
  25.6 0.0 copy-done
  25.6 0.0 copy-start.1
  25.6 1.9 %gate.1.gate_ref = f32[2048,512]{1,0:T(8,128)S(1)} custom-call(bf16[2048,512]{1,0:T(8,128)(2,1)} %gate_hbm.1, f32[1,512]{1,0:T(1,128)S(1)} %bitcast.1), custom_call_target="tpu_custom_call" | custom-call | flops 4194304 | bytes 6291456 | tf_op jit(solution)/shard_map/gate/pallas_call | solution.py:318
  27.5 0.0 collective-permute-done.5.got_ref
  27.5 0.0 copy-done.1
  27.5 3.9 %carry.1 = (f32[2048,512]{1,0:T(8,128)S(1)}, f32[16,48,128]{2,1,0:T(8,128)S(1)}) custom-call(s32[16]{0:T(128)S(1)} %copy-done.1, f32[1280,512]{1,0:T(8,128)S(1)} %get-tuple-element.33.base0_ref, f32[768,512]{1,0:T(8,128)S(1)} %get-tuple-element.41.base1_ref, bf16[1280,512]{1,0:T(8,128)(2,1)S(1)} %get-tuple-element.42.qa0_ref, ...), custom_call_target="tpu_custom_call" | custom-call | flops 536870912 | bytes 10485760 | tf_op jit(solution)/shard_map/carry/pallas_call | solution.py:330
  31.5 25.8 %all_to_all.5.got_ref = f32[16,48,128]{2,1,0:T(8,128)S(1)} all-to-all(f32[16,48,128]{2,1,0:T(8,128)S(1)} %get-tuple-element.48), channel_id=1, replica_groups=mesh['seq'=16,'grp'=16] {'grp'}, dimensions={0} | all-to-all | bytes 786432 | tf_op jit(solution)/shard_map/all_to_all | solution.py:347
  57.3 2.3 %norm.1 = (bf16[2048,512]{1,0:T(8,128)(2,1)}, f32[4,8,128]{2,1,0:T(8,128)}) custom-call(f32[16,48,128]{2,1,0:T(8,128)S(1)} %all_to_all.5.got_ref, f32[2048,512]{1,0:T(8,128)S(1)} %get-tuple-element.49.gated_ref), custom_call_target="tpu_custom_call" | custom-call | flops 2097152 | bytes 6291456 | tf_op jit(solution)/shard_map/norm/pallas_call | solution.py:349
  (3 shorter events, 0.1 us)
Async XLA Ops:
  4.6 4.3 %collective-permute-start = (f32[2,128,128]{2,1,0:T(8,128)S(1)}, f32[2,128,128]{2,1,0:T(8,128)S(1)}, u32[]{:S(2)}, u32[]{:S(2)}) collective-permute-start(f32[2,128,128]{2,1,0:T(8,128)S(1)} %get-tuple-element.29), channel_id=1, source_target_pairs={{0,16},{16,0},{32,48},{48,32},{64,80},{80,64},{96,112},{112,96},{1... | collective-permute-start | bytes 393224 | tf_op jit(solution)/shard_map/ppermute | solution.py:268
  9.0 8.9 %collective-permute-start.1 = (f32[2,128,128]{2,1,0:T(8,128)S(1)}, f32[2,128,128]{2,1,0:T(8,128)S(1)}, u32[]{:S(2)}, u32[]{:S(2)}) collective-permute-start(f32[2,128,128]{2,1,0:T(8,128)S(1)} %pair.1.own_ref), channel_id=1, source_target_pairs={{0,32},{16,48},{32,64},{48,80},{64,96},{80,112},{96,0},{112,16},{1... | collective-permute-start | bytes 393224 | tf_op jit(solution)/shard_map/ppermute | solution.py:272
  9.1 8.9 %collective-permute-start.2 = (f32[2,128,128]{2,1,0:T(8,128)S(1)}, f32[2,128,128]{2,1,0:T(8,128)S(1)}, u32[]{:S(2)}, u32[]{:S(2)}) collective-permute-start(f32[2,128,128]{2,1,0:T(8,128)S(1)} %pair.1.own_ref), channel_id=1, source_target_pairs={{0,64},{16,80},{32,96},{48,112},{64,0},{80,16},{96,32},{112,48},{1... | collective-permute-start | bytes 393224 | tf_op jit(solution)/shard_map/ppermute | solution.py:272
  11.0 7.1 %collective-permute-start.3 = (f32[2,128,128]{2,1,0:T(8,128)S(1)}, f32[2,128,128]{2,1,0:T(8,128)S(1)}, u32[]{:S(2)}, u32[]{:S(2)}) collective-permute-start(f32[2,128,128]{2,1,0:T(8,128)S(1)} %pair.1.own_ref), channel_id=1, source_target_pairs={{0,96},{16,112},{32,0},{48,16},{64,32},{80,48},{96,64},{112,80},{1... | collective-permute-start | bytes 393224 | tf_op jit(solution)/shard_map/ppermute | solution.py:272
  18.1 5.8 %collective-permute-start.4 = (f32[2,128,128]{2,1,0:T(8,128)S(1)}, f32[2,128,128]{2,1,0:T(8,128)S(1)}, u32[]{:S(2)}, u32[]{:S(2)}) collective-permute-start(f32[2,128,128]{2,1,0:T(8,128)S(1)} %get-tuple-element.38.all_ref), channel_id=1, source_target_pairs={{0,128},{16,144},{32,160},{48,176},{64,192},{80,208},{96,224},{112... | collective-permute-start | bytes 393224 | tf_op jit(solution)/shard_map/ppermute | solution.py:268
  19.4 6.2 %copy-start = (f32[512]{0:T(512)S(1)}, f32[512]{0:T(512)}, u32[]{:S(2)}) copy-start(f32[512]{0:T(512)} %param.10) | copy-start | bytes 6148
  24.0 3.5 %collective-permute-start.5 = (f32[2,136,128]{2,1,0:T(8,128)S(1)}, f32[2,136,128]{2,1,0:T(8,128)S(1)}, u32[]{:S(2)}, u32[]{:S(2)}) collective-permute-start(f32[2,136,128]{2,1,0:T(8,128)S(1)} %get-tuple-element.47), channel_id=1, source_target_pairs={{0,16},{16,0},{32,48},{48,32},{64,80},{80,64},{96,112},{112,96},{1... | collective-permute-start | bytes 417800 | tf_op jit(solution)/shard_map/ppermute | solution.py:268
  25.6 1.9 %copy-start.1 = (s32[16]{0:T(128)S(1)}, s32[16]{0:T(128)}, u32[]{:S(2)}) copy-start(s32[16]{0:T(128)} %owner_ref.1) | copy-start | bytes 196

commit v3 on v2

v3 whole, which is shorter than its diff:
```python
import functools

import jax
import jax.numpy as jnp
from jax import lax
from jax.experimental import pallas as pl
from jax.experimental.pallas import tpu as pltpu
from jax.sharding import PartitionSpec as P

DH = 128
F32 = jnp.float32
BF16 = jnp.bfloat16
MIB = 1 << 20
VMEM = pl.BlockSpec(memory_space=pltpu.VMEM)
HBM = pl.BlockSpec(memory_space=pltpu.HBM)


def places(groups):
    return list(range(groups))[::-1]


def dot(a, b, dims):
    return lax.dot_general(a, b, (dims, ((), ())), preferred_element_type=F32)


def silu(x):
    half = x.astype(F32) * 0.5
    return (half + half * jnp.tanh(half)).astype(BF16)


def params(mib):
    return pltpu.CompilerParams(vmem_limit_bytes=mib * MIB)


def cost(flops, nbytes, trans=0):
    return pl.CostEstimate(flops=flops, bytes_accessed=nbytes, transcendentals=trans)


def in_hbm(x):
    return pltpu.with_memory_space_constraint(x, pltpu.HBM)


def cols_of(h):
    return slice(h * DH, (h + 1) * DH)


def state_kernel(
    heads, chunk, k_hbm, v_hbm, q_hbm, gate_hbm, owner_hbm,
    ka_ref, va_ref, give_ref, mine_ref, q_ref, gate_ref, owners_ref, k_in, v_in, acc, owner, sems, late,
):
    count = k_in.shape[0] // chunk

    def pair(c):
        part = pl.ds(c * chunk, chunk)
        return [
            pltpu.make_async_copy(k_hbm.at[part], k_in.at[part], sems.at[0, c]),
            pltpu.make_async_copy(v_hbm.at[part], v_in.at[part], sems.at[1, c]),
        ]

    later = [
        pltpu.make_async_copy(q_hbm, q_ref, late.at[0]),
        pltpu.make_async_copy(gate_hbm, gate_ref, late.at[1]),
        pltpu.make_async_copy(owner_hbm, owner, late.at[2]),
    ]
    for c in range(count):
        for copy in pair(c):
            copy.start()
    for copy in later:
        copy.start()
    acc[...] = jnp.zeros_like(acc)

    @pl.loop(0, count)
    def _(c):
        for copy in pair(c):
            copy.wait()
        part = pl.ds(pl.multiple_of(c * chunk, chunk), chunk)
        for h in range(heads):
            k = silu(k_in[part, cols_of(h)])
            v = silu(v_in[part, cols_of(h)])
            ka_ref[part, cols_of(h)] = k
            va_ref[part, cols_of(h)] = v
            acc[h] += dot(k, v, ((0,), (0,)))

    half = heads // 2
    core = lax.rem(lax.axis_index("seq"), 2)
    for i in range(half):
        give_ref[i] = acc[(1 - core) * half + i]
        mine_ref[i] = acc[core * half + i]
    for copy in later:
        copy.wait()
    group = lax.axis_index("grp")
    for at, g in enumerate((group, group + 1 - 2 * lax.rem(group, 2))):
        owners_ref[at] = jnp.full(owners_ref.shape[1:], owner[g], jnp.int32)


def pair_kernel(mine_ref, other_ref, out_ref):
    out_ref[...] = mine_ref[...] + other_ref[...]


def along_x_kernel(chips, own_ref, *refs):
    got, (before_ref, all_ref) = refs[: chips - 1], refs[chips - 1 :]
    x = lax.rem(lax.div(lax.axis_index("seq"), 2), chips)
    total = own_ref[...]
    before = jnp.zeros_like(total)
    for back in range(1, chips):
        part = got[back - 1][...]
        total = total + part
        before = before + jnp.where(x >= back, part, 0.0)
    before_ref[...] = before
    all_ref[...] = total


def along_y_kernel(chips, before_ref, all_ref, over_ref, mine_ref, other_ref, keep_ref, send_ref, hand_ref):
    at = lax.axis_index("seq")
    core = lax.rem(at, 2)
    y = lax.div(at, 2 * chips)
    before = before_ref[...] + jnp.where(y > 0, over_ref[...], 0.0)
    keep_ref[:, :DH] = before + jnp.where(core > 0, other_ref[...], 0.0)
    send_ref[:, :DH] = before + jnp.where(core > 0, 0.0, mine_ref[...])
    rows = keep_ref.shape[1] - DH
    partner = at + 1 - 2 * core
    side = lax.rem(lax.axis_index("grp"), 2)
    for i in range(keep_ref.shape[0]):
        finals = []
        for ref, place in ((keep_ref, at), (send_ref, partner)):
            some = pl.ds(pl.multiple_of(place * rows, 8), rows)
            finals.append(all_ref[i, some] + over_ref[i, some])
            ref[i, DH:] = finals[-1]
        hand_ref[i] = jnp.where(side == 0, finals[1], finals[0])


def inside_kernel(first, heads, block, q_ref, ka_ref, va_ref, run_in, base_ref, qa_ref, run_ref):
    count = qa_ref.shape[0] // block
    run_ref[...] = run_in[...]
    causal = lax.broadcasted_iota(jnp.int32, (block, block), 0) >= lax.broadcasted_iota(
        jnp.int32, (block, block), 1
    )

    @pl.loop(0, count, unroll=2)
    def _(n):
        part = pl.ds(pl.multiple_of(n * block, block), block)
        whole = pl.ds(pl.multiple_of((first + n) * block, block), block)
        for h in range(heads):
            q = silu(q_ref[whole, cols_of(h)])
            k = ka_ref[whole, cols_of(h)]
            v = va_ref[whole, cols_of(h)]
            scores = jnp.where(causal, dot(q, k, ((1,), (1,))), 0.0).astype(BF16)
            state = run_ref[h]
            hi = state.astype(BF16)
            lo = (state - hi.astype(F32)).astype(BF16)
            left = jnp.concatenate([scores, q, q], axis=1)
            right = jnp.concatenate([v, hi, lo], axis=0)
            base_ref[part, cols_of(h)] = dot(left, right, ((1,), (0,)))
            qa_ref[part, cols_of(h)] = q
            run_ref[h] = state + dot(k, v, ((0,), (0,)))


def gate_kernel(gate_ref, gain_ref, out_ref):
    sigmoid = 0.5 + 0.5 * jnp.tanh(gate_ref[...].astype(F32) * 0.5)
    out_ref[...] = gain_ref[...] * sigmoid


def carry_kernel(
    heads, block, base0_ref, base1_ref, qa0_ref, qa1_ref, keep_ref, got_ref, gate_ref,
    gated_ref, mine_ref, states, squares,
):
    half = heads // 2
    core = lax.rem(lax.axis_index("seq"), 2)
    for i in range(half):
        for ref, h in ((keep_ref, core * half + i), (got_ref, (1 - core) * half + i)):
            state = ref[i, :DH]
            hi = state.astype(BF16)
            states[h, :DH] = hi
            states[h, DH:] = (state - hi.astype(F32)).astype(BF16)
    first = 0
    for base_ref, qa_ref in ((base0_ref, qa0_ref), (base1_ref, qa1_ref)):

        @pl.loop(0, base_ref.shape[0] // block, unroll=2)
        def _(n):
            part = pl.ds(pl.multiple_of(n * block, block), block)
            whole = pl.ds(pl.multiple_of((first + n) * block, block), block)
            sums = None
            for h in range(heads):
                q = qa_ref[part, cols_of(h)]
                attn = base_ref[part, cols_of(h)] + dot(
                    jnp.concatenate([q, q], axis=1), states[h], ((1,), (0,))
                )
                gated_ref[whole, cols_of(h)] = attn * gate_ref[whole, cols_of(h)]
                sums = attn * attn if sums is None else sums + attn * attn
            hi = sums.astype(BF16)
            squares[whole, :DH] = hi
            squares[whole, DH:] = (sums - hi.astype(F32)).astype(BF16)

        first += base_ref.shape[0] // block

    across = dot(jnp.ones((16, 2 * DH), BF16), squares[...], ((1,), (1,)))
    for c in range(squares.shape[0] // DH):
        mine_ref[c : c + 1] = across[:1, cols_of(c)]


def pack_kernel(owners_ref, squares_ref, keep_ref, got_ref, handed_ref, send_ref):
    side = lax.rem(lax.axis_index("grp"), 2)
    token_rows = squares_ref.shape[0]
    half, rows, _ = handed_ref.shape
    own, other = owners_ref[0], owners_ref[1]
    for place, g in enumerate(places(send_ref.shape[0])):
        send_ref[place, :token_rows] = squares_ref[...]
        for i in range(half):
            at = token_rows + i * rows
            final = jnp.where(side == 0, keep_ref[i, DH:], got_ref[i, DH:])
            send_ref[place, at : at + rows] = jnp.where(
                own == g, final, jnp.where(other == g, handed_ref[i], 0.0)
            )


def norm_kernel(heads, features, block, got_ref, gated_ref, out_hbm, state_ref, out, scales, sems):
    sums = [None, None]
    for place, g in enumerate(places(got_ref.shape[0])):
        sums[g % 2] = got_ref[place] if sums[g % 2] is None else sums[g % 2] + got_ref[place]
    even, odd = sums
    rows = state_ref.shape[1]
    tokens = out.shape[0]
    token_rows = tokens // DH
    scales[...] = jnp.zeros_like(scales)
    scales[:token_rows] = lax.rsqrt(
        (even[:token_rows] + odd[:token_rows]) / features + 1e-6
    )
    columns = jnp.transpose(scales[...])
    copies = []
    for n in range(tokens // block):
        for c in range(n * block // DH, (n + 1) * block // DH):
            part = slice(c * DH, (c + 1) * DH)
            out[part] = (gated_ref[part] * columns[:, c : c + 1]).astype(BF16)
        part = pl.ds(n * block, block)
        copies.append(pltpu.make_async_copy(out.at[part], out_hbm.at[part], sems.at[n]))
        copies[-1].start()
    half = heads // 2
    core = lax.rem(lax.axis_index("seq"), 2)
    for i in range(half):
        at = token_rows + i * rows
        state_ref[core * half + i] = even[at : at + rows]
        state_ref[(1 - core) * half + i] = odd[at : at + rows]
    for copy in copies:
        copy.wait()


def body(query_in, key_in, value_in, gate_in, norm_gain, head_owner):
    tokens, width = query_in.shape
    heads = width // DH
    half = heads // 2
    shards = lax.axis_size("seq")
    groups = lax.axis_size("grp")
    chips = 4
    block = min(256, tokens)
    count = tokens // block
    chunk = 2 * block
    rows = DH // shards
    token_rows = tokens // DH
    wide = pltpu.VMEM((tokens, width), BF16)
    pair_state = pltpu.VMEM((half, DH, DH), F32)
    dma = lambda *shape: pltpu.SemaphoreType.DMA(shape)
    limit = params(24)

    ka, va, give, mine, query, gate, owners = pl.pallas_call(
        functools.partial(state_kernel, heads, chunk),
        in_specs=[HBM] * 5,
        out_specs=[VMEM] * 7,
        out_shape=[wide] * 2 + [pair_state] * 2 + [wide] * 2
        + [pltpu.VMEM((2, rows, DH), jnp.int32)],
        scratch_shapes=[
            pltpu.VMEM((tokens, width), BF16),
            pltpu.VMEM((tokens, width), BF16),
            pltpu.VMEM((heads, DH, DH), F32),
            pltpu.SMEM(head_owner.shape, jnp.int32),
            dma(2, tokens // chunk),
            dma(3),
        ],
        compiler_params=limit,
        cost_estimate=cost(2 * tokens * width * DH, 4 * tokens * width),
        name="local_state",
    )(in_hbm(key_in), in_hbm(value_in), in_hbm(query_in), in_hbm(gate_in), in_hbm(head_owner))

    def swap(x, bit):
        return lax.ppermute(x, "seq", [(i, i ^ bit) for i in range(shards)])

    def on_x(x, k):
        place = lambda i: i - i % (2 * chips) + (i + 2 * k) % (2 * chips)
        return lax.ppermute(x, "seq", [(i, place(i)) for i in range(shards)])

    def inside(first, blocks, q, ka, va, run):
        part = blocks * block
        return pl.pallas_call(
            functools.partial(inside_kernel, first, heads, block),
            in_specs=[VMEM] * 4,
            out_specs=[VMEM] * 3,
            out_shape=[
                pltpu.VMEM((part, width), F32),
                pltpu.VMEM((part, width), BF16),
                pltpu.VMEM((heads, DH, DH), F32),
            ],
            compiler_params=limit,
            cost_estimate=cost(2 * part * width * (2 * block + 3 * DH), 12 * part * width),
            name="inside%d" % first,
        )(q, ka, va, run)

    cut = 6 * count // 8
    other = swap(give, 1)
    pair = pl.pallas_call(
        pair_kernel, in_specs=[VMEM] * 2, out_specs=VMEM, out_shape=pair_state,
        compiler_params=limit, name="pair",
    )(mine, other)
    around = [on_x(pair, k) for k in range(1, chips)]
    ka, va, _ = lax.optimization_barrier((ka, va, pair))
    base0, qa0, run = inside(0, cut, query, ka, va, jnp.zeros((heads, DH, DH), F32))
    base0, *around = lax.optimization_barrier((base0, *around))
    before_x, all_x = pl.pallas_call(
        functools.partial(along_x_kernel, chips),
        in_specs=[VMEM] * chips, out_specs=[VMEM] * 2, out_shape=[pair_state] * 2,
        compiler_params=limit, name="along_x",
    )(pair, *around)
    over = swap(all_x, 2 * chips)
    run, _ = lax.optimization_barrier((run, all_x))
    base1, qa1, _ = inside(cut, count - cut, query, ka, va, run)
    gate, _ = lax.optimization_barrier((gate, all_x))
    gate = pl.pallas_call(
        gate_kernel,
        in_specs=[VMEM, VMEM],
        out_specs=VMEM,
        out_shape=pltpu.VMEM((tokens, width), F32),
        compiler_params=limit,
        cost_estimate=cost(4 * tokens * width, 6 * tokens * width),
        name="gate",
    )(gate, norm_gain.reshape(1, width))

    base1, gate, over = lax.optimization_barrier((base1, gate, over))
    keep, send_core, hand = pl.pallas_call(
        functools.partial(along_y_kernel, chips),
        in_specs=[VMEM] * 5, out_specs=[VMEM] * 3,
        out_shape=[pltpu.VMEM((half, DH + rows, DH), F32)] * 2
        + [pltpu.VMEM((half, rows, DH), F32)],
        compiler_params=limit, name="along_y",
    )(before_x, all_x, over, mine, other)
    got_core = swap(send_core, 1)
    crossing = [
        (i * groups + g, (i if g % 2 else i ^ 1) * groups + (g ^ 1))
        for i in range(shards)
        for g in range(groups)
    ]
    handed = lax.ppermute(hand, ("seq", "grp"), crossing)

    payload = token_rows + half * rows
    gated, squares = pl.pallas_call(
        functools.partial(carry_kernel, heads, block),
        in_specs=[VMEM] * 7,
        out_specs=[VMEM] * 2,
        out_shape=[
            pltpu.VMEM((tokens, width), F32),
            pltpu.VMEM((token_rows, DH), F32),
        ],
        scratch_shapes=[
            pltpu.VMEM((heads, 2 * DH, DH), BF16),
            pltpu.VMEM((tokens, 2 * DH), BF16),
        ],
        compiler_params=limit,
        cost_estimate=cost(4 * tokens * width * DH, 10 * tokens * width),
        name="carry",
    )(base0, base1, qa0, qa1, keep, got_core, gate)

    send = pl.pallas_call(
        pack_kernel,
        in_specs=[VMEM] * 5,
        out_specs=VMEM,
        out_shape=pltpu.VMEM((groups, payload, DH), F32),
        compiler_params=limit,
        name="pack",
    )(owners, squares, keep, got_core, handed)

    got = lax.all_to_all(
        send, "grp", 0, 0, tiled=True, axis_index_groups=[places(groups)]
    )

    attn_out, decode_state = pl.pallas_call(
        functools.partial(norm_kernel, heads, float(width * groups), block),
        in_specs=[VMEM, VMEM],
        out_specs=[HBM, VMEM],
        out_shape=[
            jax.ShapeDtypeStruct((tokens, width), BF16),
            jax.ShapeDtypeStruct((heads, rows, DH), F32),
        ],
        scratch_shapes=[
            pltpu.VMEM((tokens, width), BF16),
            pltpu.VMEM((DH, DH), F32),
            dma(count),
        ],
        compiler_params=limit,
        cost_estimate=cost(2 * tokens * width, 6 * tokens * width),
        name="norm",
    )(got, gated)
    return attn_out, decode_state


def solution(mesh):
    return jax.shard_map(
        body,
        mesh=mesh,
        in_specs=(
            P("seq", "grp"),
            P("seq", "grp"),
            P("seq", "grp"),
            P("seq", "grp"),
            P("grp"),
            P(),
        ),
        out_specs=(P("seq", "grp"), P("grp", "seq", None)),
        check_vma=False,
    )
```

time: 59.7 us -> 51.8 us (0.87); the launches traced: 59.6 us -> 50.7 us
  blocking collectives: 25.8 us -> 17.6 us
  Pallas kernels: 22.5 us -> 17.5 us
  waiting for transfers between devices: 1.12 us -> 4.01 us
  starting transfers between devices: 9.32 us -> 10.9 us
    all_to_all x1, blocking collectives: 25.8 us -> 17.6 us  [body(): lax.all_to_all(send, 'grp', 0, 0, tiled=True, axis_index_groups=[places(g...]
    pallas_call x2 -> x3, Pallas kernels: 5.85 us -> 2.9 us  [the longest x1 2.04 us: body(): pl.pallas_call(functools.partial(carry_kernel, heads, block), in_specs=[V...]
    ppermute x0 -> x1, starting transfers between devices: none -> 2.88 us  [body(): handed = lax.ppermute(hand, ('seq', 'grp'), crossing)]
    ppermute x3, waiting for transfers between devices: 0.13 us -> 3.01 us  [on_x(): return lax.ppermute(x, 'seq', [(i, place(i)) for i in range(shards)])]
    pallas_call x2, Pallas kernels: 10.3 us -> 8.08 us  [inside(): pl.pallas_call(functools.partial(inside_kernel, first, heads, block), in_...]
    ppermute x3, starting transfers between devices: 3.15 us -> 1.94 us  [on_x(): return lax.ppermute(x, 'seq', [(i, place(i)) for i in range(shards)])]
  transfers between devices with their start and end apart: 6 -> 7, of which waited for: 2 -> 2; matrix products, arithmetic and copies ran while one was open for 0% -> 0% of each run, Pallas kernels for 20% -> 22%
where the time goes in v3:
time: 51.8 us; the launch traced here: 50.7 us
  blocking collectives  17.6 us (34%)
  Pallas kernels  17.5 us (34%)
  starting transfers between devices  10.9 us (21%)
  waiting for transfers between devices  4.01 us (8%)
  between operations  0.7 us (1%)
    all_to_all x1, blocking collectives, body(): lax.all_to_all(send, 'grp', 0, 0, tiled=True, axis_index_groups=[places(g...  17.6 us
    pallas_call x2, Pallas kernels, inside(): pl.pallas_call(functools.partial(inside_kernel, first, heads, block), in_...  8.08 us
    ppermute x3, starting transfers between devices, swap(): return lax.ppermute(x, 'seq', [(i, i ^ bit) for i in range(shards)])  6.05 us
    pallas_call x1, Pallas kernels, body(): pl.pallas_call(functools.partial(state_kernel, heads, chunk), in_specs=[H...  4.18 us
    ppermute x3, waiting for transfers between devices, on_x(): return lax.ppermute(x, 'seq', [(i, place(i)) for i in range(shards)])  3.01 us
    ppermute x1, starting transfers between devices, body(): handed = lax.ppermute(hand, ('seq', 'grp'), crossing)  2.88 us
    pallas_call x1, Pallas kernels, body(): pl.pallas_call(functools.partial(norm_kernel, heads, float(width * groups...  2.25 us
    pallas_call x1, Pallas kernels, body(): pl.pallas_call(functools.partial(carry_kernel, heads, block), in_specs=[V...  2.04 us
  transfers between devices with their start and end apart: 7, of which 2 were waited for; matrix products, arithmetic and copies ran while one was open for 0% of the time, Pallas kernels for 22%

profile of v3, /device:TPU:1, one launch (start us, length us, event | category | flops | bytes accessed | tf_op | source)
XLA Modules:
  0.0 50.7 jit_solution(11577250483010700277)
XLA Ops:
  0.6 4.2 %local_state.1 = (bf16[2048,512]{1,0:T(8,128)(2,1)S(1)}, bf16[2048,512]{1,0:T(8,128)(2,1)S(1)}, f32[2,128,128]{2,1,0:T(8,128)S(1)}, f32[2,128,128]{2,1,0:T(8,128...) custom-call(bf16[2048,512]{1,0:T(8,128)(2,1)} %k_hbm.1, ...), custom_call_target="tpu_custom_call" | custom-call | flops 268435456 | bytes 4194304 | tf_op jit(solution)/shard_map/local_state/pallas_call | solution.py:264
  4.8 3.3 %collective-permute-start = (f32[2,128,128]{2,1,0:T(8,128)S(1)}, f32[2,128,128]{2,1,0:T(8,128)S(1)}, u32[]{:S(2)}, u32[]{:S(2)}) collective-permute-start(f32[2,128,128]{2,1,0:T(8,128)S(1)} %get-tuple-element.37), channel_id=1, source_target_pairs={{0,16},{16,0},{32,48},{48,32},{64,80},{80,64},{96,112},{112,96},{1... | collective-permute-start | bytes 393224 | tf_op jit(solution)/shard_map/ppermute | solution.py:284
  8.1 1.0 %collective-permute-done.other_ref = f32[2,128,128]{2,1,0:T(8,128)S(1)} collective-permute-done((f32[2,128,128]{2,1,0:T(8,128)S(1)}, f32[2,128,128]{2,1,0:T(8,128)S(1)}, u32[]{:S(2)}, u32[]{:S(2)}) %collective-permute-start) | collective-permute-done | bytes 131104 | tf_op jit(solution)/shard_map/ppermute | solution.py:284
  9.2 0.8 %collective-permute-start.3 = (f32[2,128,128]{2,1,0:T(8,128)S(1)}, f32[2,128,128]{2,1,0:T(8,128)S(1)}, u32[]{:S(2)}, u32[]{:S(2)}) collective-permute-start(f32[2,128,128]{2,1,0:T(8,128)S(1)} %pair.1.own_ref), channel_id=1, source_target_pairs={{0,96},{16,112},{32,0},{48,16},{64,32},{80,48},{96,64},{112,80},{1... | collective-permute-start | bytes 393224 | tf_op jit(solution)/shard_map/ppermute | solution.py:288
  10.0 0.5 %collective-permute-start.2 = (f32[2,128,128]{2,1,0:T(8,128)S(1)}, f32[2,128,128]{2,1,0:T(8,128)S(1)}, u32[]{:S(2)}, u32[]{:S(2)}) collective-permute-start(f32[2,128,128]{2,1,0:T(8,128)S(1)} %pair.1.own_ref), channel_id=1, source_target_pairs={{0,64},{16,80},{32,96},{48,112},{64,0},{80,16},{96,32},{112,48},{1... | collective-permute-start | bytes 393224 | tf_op jit(solution)/shard_map/ppermute | solution.py:288
  10.5 0.6 %collective-permute-start.1 = (f32[2,128,128]{2,1,0:T(8,128)S(1)}, f32[2,128,128]{2,1,0:T(8,128)S(1)}, u32[]{:S(2)}, u32[]{:S(2)}) collective-permute-start(f32[2,128,128]{2,1,0:T(8,128)S(1)} %pair.1.own_ref), channel_id=1, source_target_pairs={{0,32},{16,48},{32,64},{48,80},{64,96},{80,112},{96,0},{112,16},{1... | collective-permute-start | bytes 393224 | tf_op jit(solution)/shard_map/ppermute | solution.py:288
  11.1 0.0 copy-start
  11.1 5.5 %inside0.1 = (f32[1536,512]{1,0:T(8,128)S(1)}, bf16[1536,512]{1,0:T(8,128)(2,1)S(1)}, f32[4,128,128]{2,1,0:T(8,128)S(1)}) custom-call(bf16[2048,512]{1,0:T(8,128)(2,1)S(1)} %get-tuple-element.33.q_ref, bf16[2048,512]{1,0:T(8,128)(2,1)S(1)} %get-tuple-element.38.ka_ref, bf16[2048,512]{1,0:T(8,128)(2,1)S(1)} %get-tuple-element.39.va_ref, ...), custom_call_target="tpu_custom_call" | custom-call | flops 1409286144 | bytes 9437184 | tf_op jit(solution)/shard_map/inside0/pallas_call | solution.py:292
  16.7 0.0 collective-permute-done.3.refs_2_
  16.7 0.0 collective-permute-done.2.refs_1_
  16.7 3.0 %collective-permute-done.1.refs_0_ = f32[2,128,128]{2,1,0:T(8,128)S(1)} collective-permute-done((f32[2,128,128]{2,1,0:T(8,128)S(1)}, f32[2,128,128]{2,1,0:T(8,128)S(1)}, u32[]{:S(2)}, u32[]{:S(2)}) %collective-permute-start.1) | collective-permute-done | bytes 131104 | tf_op jit(solution)/shard_map/ppermute | solution.py:288
  19.8 1.4 %collective-permute-start.4 = (f32[2,128,128]{2,1,0:T(8,128)S(1)}, f32[2,128,128]{2,1,0:T(8,128)S(1)}, u32[]{:S(2)}, u32[]{:S(2)}) collective-permute-start(f32[2,128,128]{2,1,0:T(8,128)S(1)} %get-tuple-element.46.all_ref), channel_id=1, source_target_pairs={{0,128},{16,144},{32,160},{48,176},{64,192},{80,208},{96,224},{112... | collective-permute-start | bytes 393224 | tf_op jit(solution)/shard_map/ppermute | solution.py:284
  21.1 0.0 copy-done
  21.1 0.8 %gate.1.gate_ref = f32[2048,512]{1,0:T(8,128)S(1)} custom-call(bf16[2048,512]{1,0:T(8,128)(2,1)S(1)} %get-tuple-element.50.gate_ref, f32[1,512]{1,0:T(1,128)S(1)} %bitcast.1), custom_call_target="tpu_custom_call" | custom-call | flops 4194304 | bytes 6291456 | tf_op jit(solution)/shard_map/gate/pallas_call | solution.py:325
  22.0 2.5 %inside6.1 = (f32[512,512]{1,0:T(8,128)S(1)}, bf16[512,512]{1,0:T(8,128)(2,1)S(1)}, f32[4,128,128]{2,1,0:T(8,128)}) custom-call(bf16[2048,512]{1,0:T(8,128)(2,1)S(1)} %get-tuple-element.33.q_ref, bf16[2048,512]{1,0:T(8,128)(2,1)S(1)} %get-tuple-element.38.ka_ref, bf16[2048,512]{1,0:T(8,128)(2,1)S(1)} %get-tuple-element.39.va_ref, ...), custom_call_target="tpu_custom_call" | custom-call | flops 469762048 | bytes 3145728 | tf_op jit(solution)/shard_map/inside6/pallas_call | solution.py:292
  24.5 0.0 collective-permute-done.4.over_ref
  24.6 1.3 %collective-permute-start.5 = (f32[2,136,128]{2,1,0:T(8,128)S(1)}, f32[2,136,128]{2,1,0:T(8,128)S(1)}, u32[]{:S(2)}, u32[]{:S(2)}) collective-permute-start(f32[2,136,128]{2,1,0:T(8,128)S(1)} %get-tuple-element.57), channel_id=1, source_target_pairs={{0,16},{16,0},{32,48},{48,32},{64,80},{80,64},{96,112},{112,96},{1... | collective-permute-start | bytes 417800 | tf_op jit(solution)/shard_map/ppermute | solution.py:284
  25.9 2.9 %collective-permute-start.6 = (f32[2,8,128]{2,1,0:T(8,128)S(1)}, f32[2,8,128]{2,1,0:T(8,128)S(1)}, u32[]{:S(2)}, u32[]{:S(2)}) collective-permute-start(f32[2,8,128]{2,1,0:T(8,128)S(1)} %get-tuple-element.60), channel_id=1, source_target_pairs={{0,17},{1,0},{2,19},{3,2},{4,21},{5,4},{6,23},{7,6},{8,25},{9,8},{... | collective-permute-start | bytes 24584 | tf_op jit(solution)/shard_map/ppermute | solution.py:349
  28.8 0.0 collective-permute-done.5.got_ref
  28.8 2.0 %carry.1 = (f32[2048,512]{1,0:T(8,128)S(1)}, f32[16,128]{1,0:T(8,128)S(1)}) custom-call(f32[1536,512]{1,0:T(8,128)S(1)} %get-tuple-element.41.base0_ref, f32[512,512]{1,0:T(8,128)S(1)} %get-tuple-element.51.base1_ref, bf16[1536,512]{1,0:T(8,128)(2,1)S(1)} %get-tuple-element.52.qa0_ref, bf16[512,512]{1,0:T(8,128)(2,1)S(1)} %get-tuple-element.53.qa1_ref, ...), custom_call_target="tpu_custom_call" | custom-call | flops 536870912 | bytes 10485760 | tf_op jit(solution)/shard_map/carry/pallas_call | solution.py:352
  30.8 0.0 collective-permute-done.6.handed_ref
  30.9 17.6 %all_to_all.5.got_ref = f32[16,32,128]{2,1,0:T(8,128)S(1)} all-to-all(f32[16,32,128]{2,1,0:T(8,128)S(1)} %pack.1), channel_id=1, replica_groups={{15,14,13,12,11,10,9,8,7,6,5,4,3,2,1,0},{31,30,29,28,27,26,25,24,23,22,..., dimensions={0} | all-to-all | bytes 524288 | tf_op jit(solution)/shard_map/all_to_all | solution.py:378
  48.5 2.3 %norm.1 = (bf16[2048,512]{1,0:T(8,128)(2,1)}, f32[4,8,128]{2,1,0:T(8,128)}) custom-call(f32[16,32,128]{2,1,0:T(8,128)S(1)} %all_to_all.5.got_ref, f32[2048,512]{1,0:T(8,128)S(1)} %get-tuple-element.61.gated_ref), custom_call_target="tpu_custom_call" | custom-call | flops 2097152 | bytes 6291456 | tf_op jit(solution)/shard_map/norm/pallas_call | solution.py:382
  (5 shorter events, 0.2 us)
Async XLA Ops:
  4.8 4.3 %collective-permute-start = (f32[2,128,128]{2,1,0:T(8,128)S(1)}, f32[2,128,128]{2,1,0:T(8,128)S(1)}, u32[]{:S(2)}, u32[]{:S(2)}) collective-permute-start(f32[2,128,128]{2,1,0:T(8,128)S(1)} %get-tuple-element.37), channel_id=1, source_target_pairs={{0,16},{16,0},{32,48},{48,32},{64,80},{80,64},{96,112},{112,96},{1... | collective-permute-start | bytes 393224 | tf_op jit(solution)/shard_map/ppermute | solution.py:284
  9.2 7.5 %collective-permute-start.3 = (f32[2,128,128]{2,1,0:T(8,128)S(1)}, f32[2,128,128]{2,1,0:T(8,128)S(1)}, u32[]{:S(2)}, u32[]{:S(2)}) collective-permute-start(f32[2,128,128]{2,1,0:T(8,128)S(1)} %pair.1.own_ref), channel_id=1, source_target_pairs={{0,96},{16,112},{32,0},{48,16},{64,32},{80,48},{96,64},{112,80},{1... | collective-permute-start | bytes 393224 | tf_op jit(solution)/shard_map/ppermute | solution.py:288
  10.0 6.7 %collective-permute-start.2 = (f32[2,128,128]{2,1,0:T(8,128)S(1)}, f32[2,128,128]{2,1,0:T(8,128)S(1)}, u32[]{:S(2)}, u32[]{:S(2)}) collective-permute-start(f32[2,128,128]{2,1,0:T(8,128)S(1)} %pair.1.own_ref), channel_id=1, source_target_pairs={{0,64},{16,80},{32,96},{48,112},{64,0},{80,16},{96,32},{112,48},{1... | collective-permute-start | bytes 393224 | tf_op jit(solution)/shard_map/ppermute | solution.py:288
  10.5 9.2 %collective-permute-start.1 = (f32[2,128,128]{2,1,0:T(8,128)S(1)}, f32[2,128,128]{2,1,0:T(8,128)S(1)}, u32[]{:S(2)}, u32[]{:S(2)}) collective-permute-start(f32[2,128,128]{2,1,0:T(8,128)S(1)} %pair.1.own_ref), channel_id=1, source_target_pairs={{0,32},{16,48},{32,64},{48,80},{64,96},{80,112},{96,0},{112,16},{1... | collective-permute-start | bytes 393224 | tf_op jit(solution)/shard_map/ppermute | solution.py:288
  11.1 10.0 %copy-start = (f32[512]{0:T(512)S(1)}, f32[512]{0:T(512)}, u32[]{:S(2)}) copy-start(f32[512]{0:T(512)} %param.10) | copy-start | bytes 6148
  19.8 4.7 %collective-permute-start.4 = (f32[2,128,128]{2,1,0:T(8,128)S(1)}, f32[2,128,128]{2,1,0:T(8,128)S(1)}, u32[]{:S(2)}, u32[]{:S(2)}) collective-permute-start(f32[2,128,128]{2,1,0:T(8,128)S(1)} %get-tuple-element.46.all_ref), channel_id=1, source_target_pairs={{0,128},{16,144},{32,160},{48,176},{64,192},{80,208},{96,224},{112... | collective-permute-start | bytes 393224 | tf_op jit(solution)/shard_map/ppermute | solution.py:284
  24.6 4.2 %collective-permute-start.5 = (f32[2,136,128]{2,1,0:T(8,128)S(1)}, f32[2,136,128]{2,1,0:T(8,128)S(1)}, u32[]{:S(2)}, u32[]{:S(2)}) collective-permute-start(f32[2,136,128]{2,1,0:T(8,128)S(1)} %get-tuple-element.57), channel_id=1, source_target_pairs={{0,16},{16,0},{32,48},{48,32},{64,80},{80,64},{96,112},{112,96},{1... | collective-permute-start | bytes 417800 | tf_op jit(solution)/shard_map/ppermute | solution.py:284
  25.9 4.9 %collective-permute-start.6 = (f32[2,8,128]{2,1,0:T(8,128)S(1)}, f32[2,8,128]{2,1,0:T(8,128)S(1)}, u32[]{:S(2)}, u32[]{:S(2)}) collective-permute-start(f32[2,8,128]{2,1,0:T(8,128)S(1)} %get-tuple-element.60), channel_id=1, source_target_pairs={{0,17},{1,0},{2,19},{3,2},{4,21},{5,4},{6,23},{7,6},{8,25},{9,8},{... | collective-permute-start | bytes 24584 | tf_op jit(solution)/shard_map/ppermute | solution.py:349

commit v4 on v3

--- a/solution.py
+++ b/solution.py
@@ -15,8 +15,8 @@
 HBM = pl.BlockSpec(memory_space=pltpu.HBM)
 
 
-def places(groups):
-    return list(range(groups))[::-1]
+def lines(groups):
+    return [list(range(groups - 2 + side, -1, -2)) for side in range(2)]
 
 
 def dot(a, b, dims):
@@ -103,14 +103,14 @@
     total = own_ref[...]
     before = jnp.zeros_like(total)
     for back in range(1, chips):
-        part = got[back - 1][...]
+        part = got[chips - 1 - back][...]
         total = total + part
         before = before + jnp.where(x >= back, part, 0.0)
     before_ref[...] = before
     all_ref[...] = total
 
 
-def along_y_kernel(chips, before_ref, all_ref, over_ref, mine_ref, other_ref, keep_ref, send_ref, hand_ref):
+def along_y_kernel(chips, before_ref, all_ref, over_ref, mine_ref, other_ref, keep_ref, send_ref):
     at = lax.axis_index("seq")
     core = lax.rem(at, 2)
     y = lax.div(at, 2 * chips)
@@ -119,14 +119,10 @@
     send_ref[:, :DH] = before + jnp.where(core > 0, 0.0, mine_ref[...])
     rows = keep_ref.shape[1] - DH
     partner = at + 1 - 2 * core
-    side = lax.rem(lax.axis_index("grp"), 2)
     for i in range(keep_ref.shape[0]):
-        finals = []
         for ref, place in ((keep_ref, at), (send_ref, partner)):
             some = pl.ds(pl.multiple_of(place * rows, 8), rows)
-            finals.append(all_ref[i, some] + over_ref[i, some])
-            ref[i, DH:] = finals[-1]
-        hand_ref[i] = jnp.where(side == 0, finals[1], finals[0])
+            ref[i, DH:] = all_ref[i, some] + over_ref[i, some]
 
 
 def inside_kernel(first, heads, block, q_ref, ka_ref, va_ref, run_in, base_ref, qa_ref, run_ref):
@@ -155,14 +151,14 @@
             run_ref[h] = state + dot(k, v, ((0,), (0,)))
 
 
-def gate_kernel(gate_ref, gain_ref, out_ref):
+def gate_kernel(attn_ref, gate_ref, gain_ref, out_ref):
     sigmoid = 0.5 + 0.5 * jnp.tanh(gate_ref[...].astype(F32) * 0.5)
-    out_ref[...] = gain_ref[...] * sigmoid
+    out_ref[...] = attn_ref[...] * (gain_ref[...] * sigmoid)
 
 
 def carry_kernel(
-    heads, block, base0_ref, base1_ref, qa0_ref, qa1_ref, keep_ref, got_ref, gate_ref,
-    gated_ref, mine_ref, states, squares,
+    heads, block, base0_ref, base1_ref, qa0_ref, qa1_ref, keep_ref, got_ref,
+    attn_ref, mine_ref, states, squares,
 ):
     half = heads // 2
     core = lax.rem(lax.axis_index("seq"), 2)
@@ -185,7 +181,7 @@
                 attn = base_ref[part, cols_of(h)] + dot(
                     jnp.concatenate([q, q], axis=1), states[h], ((1,), (0,))
                 )
-                gated_ref[whole, cols_of(h)] = attn * gate_ref[whole, cols_of(h)]
+                attn_ref[whole, cols_of(h)] = attn
                 sums = attn * attn if sums is None else sums + attn * attn
             hi = sums.astype(BF16)
             squares[whole, :DH] = hi
@@ -194,37 +190,40 @@
         first += base_ref.shape[0] // block
 
     across = dot(jnp.ones((16, 2 * DH), BF16), squares[...], ((1,), (1,)))
-    for c in range(squares.shape[0] // DH):
+    token_rows = squares.shape[0] // DH
+    for c in range(token_rows):
         mine_ref[c : c + 1] = across[:1, cols_of(c)]
-
-
-def pack_kernel(owners_ref, squares_ref, keep_ref, got_ref, handed_ref, send_ref):
+    rows = keep_ref.shape[1] - DH
+    for i in range(half):
+        for ref, h in ((keep_ref, core * half + i), (got_ref, (1 - core) * half + i)):
+            mine_ref[pl.ds(pl.multiple_of(token_rows + h * rows, 8), rows)] = ref[i, DH:]
+
+
+def pack_kernel(owners_ref, mine_ref, other_ref, send_ref):
     side = lax.rem(lax.axis_index("grp"), 2)
-    token_rows = squares_ref.shape[0]
-    half, rows, _ = handed_ref.shape
-    own, other = owners_ref[0], owners_ref[1]
-    for place, g in enumerate(places(send_ref.shape[0])):
-        send_ref[place, :token_rows] = squares_ref[...]
-        for i in range(half):
-            at = token_rows + i * rows
-            final = jnp.where(side == 0, keep_ref[i, DH:], got_ref[i, DH:])
-            send_ref[place, at : at + rows] = jnp.where(
-                own == g, final, jnp.where(other == g, handed_ref[i], 0.0)
+    rows = owners_ref.shape[1]
+    width = mine_ref.shape[0]
+    token_rows = width - 4 * rows
+    own, other = owners_ref[0] - side, owners_ref[1] - side
+    both = mine_ref[:token_rows] + other_ref[:token_rows]
+    for place, g in enumerate(lines(2 * send_ref.shape[0])[0]):
+        send_ref[place, :token_rows] = both
+        for at in range(token_rows, width, rows):
+            part = slice(at, at + rows)
+            send_ref[place, part] = jnp.where(
+                own == g, mine_ref[part], jnp.where(other == g, other_ref[part], 0.0)
             )
 
 
 def norm_kernel(heads, features, block, got_ref, gated_ref, out_hbm, state_ref, out, scales, sems):
-    sums = [None, None]
-    for place, g in enumerate(places(got_ref.shape[0])):
-        sums[g % 2] = got_ref[place] if sums[g % 2] is None else sums[g % 2] + got_ref[place]
-    even, odd = sums
+    total = got_ref[0]
+    for place in range(1, got_ref.shape[0]):
+        total = total + got_ref[place]
     rows = state_ref.shape[1]
     tokens = out.shape[0]
     token_rows = tokens // DH
     scales[...] = jnp.zeros_like(scales)
-    scales[:token_rows] = lax.rsqrt(
-        (even[:token_rows] + odd[:token_rows]) / features + 1e-6
-    )
+    scales[:token_rows] = lax.rsqrt(total[:token_rows] / features + 1e-6)
     columns = jnp.transpose(scales[...])
     copies = []
     for n in range(tokens // block):
@@ -234,12 +233,9 @@
         part = pl.ds(n * block, block)
         copies.append(pltpu.make_async_copy(out.at[part], out_hbm.at[part], sems.at[n]))
         copies[-1].start()
-    half = heads // 2
-    core = lax.rem(lax.axis_index("seq"), 2)
-    for i in range(half):
-        at = token_rows + i * rows
-        state_ref[core * half + i] = even[at : at + rows]
-        state_ref[(1 - core) * half + i] = odd[at : at + rows]
+    for h in range(heads):
+        at = token_rows + h * rows
+        state_ref[h] = total[at : at + rows]
     for copy in copies:
         copy.wait()
 
@@ -303,13 +299,13 @@
             name="inside%d" % first,
         )(q, ka, va, run)
 
-    cut = 6 * count // 8
+    cut = 5 * count // 8
     other = swap(give, 1)
     pair = pl.pallas_call(
         pair_kernel, in_specs=[VMEM] * 2, out_specs=VMEM, out_shape=pair_state,
         compiler_params=limit, name="pair",
     )(mine, other)
-    around = [on_x(pair, k) for k in range(1, chips)]
+    around = [on_x(pair, k) for k in range(chips - 1, 0, -1)]
     ka, va, _ = lax.optimization_barrier((ka, va, pair))
     base0, qa0, run = inside(0, cut, query, ka, va, jnp.zeros((heads, DH, DH), F32))
     base0, *around = lax.optimization_barrier((base0, *around))
@@ -321,41 +317,22 @@
     over = swap(all_x, 2 * chips)
     run, _ = lax.optimization_barrier((run, all_x))
     base1, qa1, _ = inside(cut, count - cut, query, ka, va, run)
-    gate, _ = lax.optimization_barrier((gate, all_x))
-    gate = pl.pallas_call(
-        gate_kernel,
-        in_specs=[VMEM, VMEM],
-        out_specs=VMEM,
-        out_shape=pltpu.VMEM((tokens, width), F32),
-        compiler_params=limit,
-        cost_estimate=cost(4 * tokens * width, 6 * tokens * width),
-        name="gate",
-    )(gate, norm_gain.reshape(1, width))
-
-    base1, gate, over = lax.optimization_barrier((base1, gate, over))
-    keep, send_core, hand = pl.pallas_call(
+    base1, over = lax.optimization_barrier((base1, over))
+    keep, send_core = pl.pallas_call(
         functools.partial(along_y_kernel, chips),
-        in_specs=[VMEM] * 5, out_specs=[VMEM] * 3,
-        out_shape=[pltpu.VMEM((half, DH + rows, DH), F32)] * 2
-        + [pltpu.VMEM((half, rows, DH), F32)],
+        in_specs=[VMEM] * 5, out_specs=[VMEM] * 2,
+        out_shape=[pltpu.VMEM((half, DH + rows, DH), F32)] * 2,
         compiler_params=limit, name="along_y",
     )(before_x, all_x, over, mine, other)
     got_core = swap(send_core, 1)
-    crossing = [
-        (i * groups + g, (i if g % 2 else i ^ 1) * groups + (g ^ 1))
-        for i in range(shards)
-        for g in range(groups)
-    ]
-    handed = lax.ppermute(hand, ("seq", "grp"), crossing)
-
-    payload = token_rows + half * rows
-    gated, squares = pl.pallas_call(
+    payload = token_rows + heads * rows
+    attn, own = pl.pallas_call(
         functools.partial(carry_kernel, heads, block),
-        in_specs=[VMEM] * 7,
+        in_specs=[VMEM] * 6,
         out_specs=[VMEM] * 2,
         out_shape=[
             pltpu.VMEM((tokens, width), F32),
-            pltpu.VMEM((token_rows, DH), F32),
+            pltpu.VMEM((payload, DH), F32),
         ],
         scratch_shapes=[
             pltpu.VMEM((heads, 2 * DH, DH), BF16),
@@ -364,19 +341,30 @@
         compiler_params=limit,
         cost_estimate=cost(4 * tokens * width * DH, 10 * tokens * width),
         name="carry",
-    )(base0, base1, qa0, qa1, keep, got_core, gate)
-
+    )(base0, base1, qa0, qa1, keep, got_core)
+
+    beside = lax.ppermute(own, "grp", [(g, g ^ 1) for g in range(groups)])
+    gated = pl.pallas_call(
+        gate_kernel,
+        in_specs=[VMEM] * 3,
+        out_specs=VMEM,
+        out_shape=pltpu.VMEM((tokens, width), F32),
+        compiler_params=limit,
+        cost_estimate=cost(4 * tokens * width, 10 * tokens * width),
+        name="gate",
+    )(attn, gate, norm_gain.reshape(1, width))
+    gated, beside = lax.optimization_barrier((gated, beside))
     send = pl.pallas_call(
         pack_kernel,
-        in_specs=[VMEM] * 5,
+        in_specs=[VMEM] * 3,
         out_specs=VMEM,
-        out_shape=pltpu.VMEM((groups, payload, DH), F32),
+        out_shape=pltpu.VMEM((groups // 2, payload, DH), F32),
         compiler_params=limit,
         name="pack",
-    )(owners, squares, keep, got_core, handed)
+    )(owners, own, beside)
 
     got = lax.all_to_all(
-        send, "grp", 0, 0, tiled=True, axis_index_groups=[places(groups)]
+        send, "grp", 0, 0, tiled=True, axis_index_groups=lines(groups)
     )
 
     attn_out, decode_state = pl.pallas_call(

time: 51.8 us -> 49 us (0.946)
  the two profiles are of different devices: /device:TPU:1 before, /device:TPU:16 now
where the time goes in v4:
time: 49 us; the launch traced here: 48.8 us
  Pallas kernels  17.3 us (35%)
  blocking collectives  15.9 us (32%)
  starting transfers between devices  8.97 us (18%)
  waiting for transfers between devices  5.88 us (12%)
  between operations  0.7 us (1%)
    all_to_all x1, blocking collectives, body(): lax.all_to_all(send, 'grp', 0, 0, tiled=True, axis_index_groups=lines(gro...  15.9 us
    pallas_call x2, Pallas kernels, inside(): pl.pallas_call(functools.partial(inside_kernel, first, heads, block), in_...  8.04 us
    ppermute x3, starting transfers between devices, on_x(): return lax.ppermute(x, 'seq', [(i, place(i)) for i in range(shards)])  5.73 us
    pallas_call x1, Pallas kernels, body(): pl.pallas_call(functools.partial(state_kernel, heads, chunk), in_specs=[H...  4.18 us
    ppermute x3, waiting for transfers between devices, swap(): return lax.ppermute(x, 'seq', [(i, i ^ bit) for i in range(shards)])  2.94 us
    ppermute x1, waiting for transfers between devices, body(): beside = lax.ppermute(own, 'grp', [(g, g ^ 1) for g in range(groups)])  2.7 us
    pallas_call x1, Pallas kernels, body(): pl.pallas_call(functools.partial(norm_kernel, heads, float(width * groups...  2.24 us
    pallas_call x1, Pallas kernels, body(): pl.pallas_call(functools.partial(carry_kernel, heads, block), in_specs=[V...  1.77 us
  transfers between devices with their start and end apart: 7, of which 5 were waited for; matrix products, arithmetic and copies ran while one was open for 0% of the time, Pallas kernels for 18%

profile of v4, /device:TPU:16, one launch (start us, length us, event | category | flops | bytes accessed | tf_op | source)
XLA Modules:
  0.0 48.8 jit_solution(1242540583187704403)
XLA Ops:
  0.6 4.2 %local_state.1 = (bf16[2048,512]{1,0:T(8,128)(2,1)S(1)}, bf16[2048,512]{1,0:T(8,128)(2,1)S(1)}, f32[2,128,128]{2,1,0:T(8,128)S(1)}, f32[2,128,128]{2,1,0:T(8,128...) custom-call(bf16[2048,512]{1,0:T(8,128)(2,1)} %k_hbm.1, ...), custom_call_target="tpu_custom_call" | custom-call | flops 268435456 | bytes 4194304 | tf_op jit(solution)/shard_map/local_state/pallas_call | solution.py:260
  4.8 0.1 collective-permute-start
  4.9 1.3 %collective-permute-done.other_ref = f32[2,128,128]{2,1,0:T(8,128)S(1)} collective-permute-done((f32[2,128,128]{2,1,0:T(8,128)S(1)}, f32[2,128,128]{2,1,0:T(8,128)S(1)}, u32[]{:S(2)}, u32[]{:S(2)}) %collective-permute-start) | collective-permute-done | bytes 131104 | tf_op jit(solution)/shard_map/ppermute | solution.py:280
  6.3 1.6 %collective-permute-start.3 = (f32[2,128,128]{2,1,0:T(8,128)S(1)}, f32[2,128,128]{2,1,0:T(8,128)S(1)}, u32[]{:S(2)}, u32[]{:S(2)}) collective-permute-start(f32[2,128,128]{2,1,0:T(8,128)S(1)} %pair.1.own_ref), channel_id=1, source_target_pairs={{0,32},{16,48},{32,64},{48,80},{64,96},{80,112},{96,0},{112,16},{1... | collective-permute-start | bytes 393224 | tf_op jit(solution)/shard_map/ppermute | solution.py:284
  7.8 2.7 %collective-permute-start.2 = (f32[2,128,128]{2,1,0:T(8,128)S(1)}, f32[2,128,128]{2,1,0:T(8,128)S(1)}, u32[]{:S(2)}, u32[]{:S(2)}) collective-permute-start(f32[2,128,128]{2,1,0:T(8,128)S(1)} %pair.1.own_ref), channel_id=1, source_target_pairs={{0,64},{16,80},{32,96},{48,112},{64,0},{80,16},{96,32},{112,48},{1... | collective-permute-start | bytes 393224 | tf_op jit(solution)/shard_map/ppermute | solution.py:284
  10.6 1.4 %collective-permute-start.1 = (f32[2,128,128]{2,1,0:T(8,128)S(1)}, f32[2,128,128]{2,1,0:T(8,128)S(1)}, u32[]{:S(2)}, u32[]{:S(2)}) collective-permute-start(f32[2,128,128]{2,1,0:T(8,128)S(1)} %pair.1.own_ref), channel_id=1, source_target_pairs={{0,96},{16,112},{32,0},{48,16},{64,32},{80,48},{96,64},{112,80},{1... | collective-permute-start | bytes 393224 | tf_op jit(solution)/shard_map/ppermute | solution.py:284
  12.0 4.6 %inside0.1 = (f32[1280,512]{1,0:T(8,128)S(1)}, bf16[1280,512]{1,0:T(8,128)(2,1)S(1)}, f32[4,128,128]{2,1,0:T(8,128)S(1)}) custom-call(bf16[2048,512]{1,0:T(8,128)(2,1)S(1)} %get-tuple-element.32.q_ref, bf16[2048,512]{1,0:T(8,128)(2,1)S(1)} %get-tuple-element.37.ka_ref, bf16[2048,512]{1,0:T(8,128)(2,1)S(1)} %get-tuple-element.38.va_ref, ...), custom_call_target="tpu_custom_call" | custom-call | flops 1174405120 | bytes 7864320 | tf_op jit(solution)/shard_map/inside0/pallas_call | solution.py:288
  16.6 0.0 collective-permute-done.3.refs_2_
  16.7 0.2 collective-permute-done.2.refs_1_
  16.9 0.0 collective-permute-done.1.refs_0_
  16.9 0.1 along_x.1
  17.0 1.4 %collective-permute-start.4 = (f32[2,128,128]{2,1,0:T(8,128)S(1)}, f32[2,128,128]{2,1,0:T(8,128)S(1)}, u32[]{:S(2)}, u32[]{:S(2)}) collective-permute-start(f32[2,128,128]{2,1,0:T(8,128)S(1)} %get-tuple-element.45.all_ref), channel_id=1, source_target_pairs={{0,128},{16,144},{32,160},{48,176},{64,192},{80,208},{96,224},{112... | collective-permute-start | bytes 393224 | tf_op jit(solution)/shard_map/ppermute | solution.py:280
  18.3 3.4 %inside5.1 = (f32[768,512]{1,0:T(8,128)S(1)}, bf16[768,512]{1,0:T(8,128)(2,1)S(1)}, f32[4,128,128]{2,1,0:T(8,128)}) custom-call(bf16[2048,512]{1,0:T(8,128)(2,1)S(1)} %get-tuple-element.32.q_ref, bf16[2048,512]{1,0:T(8,128)(2,1)S(1)} %get-tuple-element.37.ka_ref, bf16[2048,512]{1,0:T(8,128)(2,1)S(1)} %get-tuple-element.38.va_ref, ...), custom_call_target="tpu_custom_call" | custom-call | flops 704643072 | bytes 4718592 | tf_op jit(solution)/shard_map/inside5/pallas_call | solution.py:288
  21.8 0.3 collective-permute-done.4.over_ref
  22.1 0.1 collective-permute-start.5
  22.2 1.3 %collective-permute-done.5.got_ref = f32[2,136,128]{2,1,0:T(8,128)S(1)} collective-permute-done((f32[2,136,128]{2,1,0:T(8,128)S(1)}, f32[2,136,128]{2,1,0:T(8,128)S(1)}, u32[]{:S(2)}, u32[]{:S(2)}) %collective-permute-start.5) | collective-permute-done | bytes 139296 | tf_op jit(solution)/shard_map/ppermute | solution.py:280
  23.5 0.0 copy-start
  23.5 1.8 %carry.1 = (f32[2048,512]{1,0:T(8,128)S(1)}, f32[48,128]{1,0:T(8,128)S(1)}) custom-call(f32[1280,512]{1,0:T(8,128)S(1)} %get-tuple-element.40.base0_ref, f32[768,512]{1,0:T(8,128)S(1)} %get-tuple-element.48.base1_ref, bf16[1280,512]{1,0:T(8,128)(2,1)S(1)} %get-tuple-element.49.qa0_ref, bf16[768,512]{1,0:T(8,128)(2,1)S(1)} %get-tuple-element.50.qa1_ref, ...), custom_call_target="tpu_custom_call" | custom-call | flops 536870912 | bytes 10485760 | tf_op jit(solution)/shard_map/carry/pallas_call | solution.py:329
  25.3 1.7 %collective-permute-start.6 = (f32[48,128]{1,0:T(8,128)S(1)}, f32[48,128]{1,0:T(8,128)S(1)}, u32[]{:S(2)}, u32[]{:S(2)}) collective-permute-start(f32[48,128]{1,0:T(8,128)S(1)} %get-tuple-element.55.mine_ref), channel_id=1, source_target_pairs={{0,1},{1,0},{2,3},{3,2},{4,5},{5,4},{6,7},{7,6},{8,9},{9,8},{10,11... | collective-permute-start | bytes 73736 | tf_op jit(solution)/shard_map/ppermute | solution.py:346
  27.0 0.0 copy-done
  27.0 1.0 %gate.1.gated_ref = f32[2048,512]{1,0:T(8,128)S(1)} custom-call(f32[2048,512]{1,0:T(8,128)S(1)} %get-tuple-element.56.attn_ref, bf16[2048,512]{1,0:T(8,128)(2,1)S(1)} %get-tuple-element.57.gate_ref, f32[1,512]{1,0:T(1,128)S(1)} %bitcast.1), custom_call_target="tpu_custom_call" | custom-call | flops 4194304 | bytes 10485760 | tf_op jit(solution)/shard_map/gate/pallas_call | solution.py:347
  27.9 2.7 %collective-permute-done.6.other_ref = f32[48,128]{1,0:T(8,128)S(1)} collective-permute-done((f32[48,128]{1,0:T(8,128)S(1)}, f32[48,128]{1,0:T(8,128)S(1)}, u32[]{:S(2)}, u32[]{:S(2)}) %collective-permute-start.6) | collective-permute-done | bytes 24608 | tf_op jit(solution)/shard_map/ppermute | solution.py:346
  30.7 15.9 %all_to_all.5.got_ref = f32[8,48,128]{2,1,0:T(8,128)S(1)} all-to-all(f32[8,48,128]{2,1,0:T(8,128)S(1)} %pack.1), channel_id=1, replica_groups={{14,12,10,8,6,4,2,0},{15,13,11,9,7,5,3,1},{30,28,26,24,22,20,18,16},{31..., dimensions={0} | all-to-all | bytes 393216 | tf_op jit(solution)/shard_map/all_to_all | solution.py:366
  46.6 2.2 %norm.1 = (bf16[2048,512]{1,0:T(8,128)(2,1)}, f32[4,8,128]{2,1,0:T(8,128)}) custom-call(f32[8,48,128]{2,1,0:T(8,128)S(1)} %all_to_all.5.got_ref, f32[2048,512]{1,0:T(8,128)S(1)} %gate.1.gated_ref), custom_call_target="tpu_custom_call" | custom-call | flops 2097152 | bytes 6291456 | tf_op jit(solution)/shard_map/norm/pallas_call | solution.py:370
  (4 shorter events, 0.1 us)
Async XLA Ops:
  4.8 1.4 %collective-permute-start = (f32[2,128,128]{2,1,0:T(8,128)S(1)}, f32[2,128,128]{2,1,0:T(8,128)S(1)}, u32[]{:S(2)}, u32[]{:S(2)}) collective-permute-start(f32[2,128,128]{2,1,0:T(8,128)S(1)} %get-tuple-element.36), channel_id=1, source_target_pairs={{0,16},{16,0},{32,48},{48,32},{64,80},{80,64},{96,112},{112,96},{1... | collective-permute-start | bytes 393224 | tf_op jit(solution)/shard_map/ppermute | solution.py:280
  6.3 10.4 %collective-permute-start.3 = (f32[2,128,128]{2,1,0:T(8,128)S(1)}, f32[2,128,128]{2,1,0:T(8,128)S(1)}, u32[]{:S(2)}, u32[]{:S(2)}) collective-permute-start(f32[2,128,128]{2,1,0:T(8,128)S(1)} %pair.1.own_ref), channel_id=1, source_target_pairs={{0,32},{16,48},{32,64},{48,80},{64,96},{80,112},{96,0},{112,16},{1... | collective-permute-start | bytes 393224 | tf_op jit(solution)/shard_map/ppermute | solution.py:284
  7.8 9.1 %collective-permute-start.2 = (f32[2,128,128]{2,1,0:T(8,128)S(1)}, f32[2,128,128]{2,1,0:T(8,128)S(1)}, u32[]{:S(2)}, u32[]{:S(2)}) collective-permute-start(f32[2,128,128]{2,1,0:T(8,128)S(1)} %pair.1.own_ref), channel_id=1, source_target_pairs={{0,64},{16,80},{32,96},{48,112},{64,0},{80,16},{96,32},{112,48},{1... | collective-permute-start | bytes 393224 | tf_op jit(solution)/shard_map/ppermute | solution.py:284
  10.6 6.3 %collective-permute-start.1 = (f32[2,128,128]{2,1,0:T(8,128)S(1)}, f32[2,128,128]{2,1,0:T(8,128)S(1)}, u32[]{:S(2)}, u32[]{:S(2)}) collective-permute-start(f32[2,128,128]{2,1,0:T(8,128)S(1)} %pair.1.own_ref), channel_id=1, source_target_pairs={{0,96},{16,112},{32,0},{48,16},{64,32},{80,48},{96,64},{112,80},{1... | collective-permute-start | bytes 393224 | tf_op jit(solution)/shard_map/ppermute | solution.py:284
  17.0 5.1 %collective-permute-start.4 = (f32[2,128,128]{2,1,0:T(8,128)S(1)}, f32[2,128,128]{2,1,0:T(8,128)S(1)}, u32[]{:S(2)}, u32[]{:S(2)}) collective-permute-start(f32[2,128,128]{2,1,0:T(8,128)S(1)} %get-tuple-element.45.all_ref), channel_id=1, source_target_pairs={{0,128},{16,144},{32,160},{48,176},{64,192},{80,208},{96,224},{112... | collective-permute-start | bytes 393224 | tf_op jit(solution)/shard_map/ppermute | solution.py:280
  22.1 1.4 %collective-permute-start.5 = (f32[2,136,128]{2,1,0:T(8,128)S(1)}, f32[2,136,128]{2,1,0:T(8,128)S(1)}, u32[]{:S(2)}, u32[]{:S(2)}) collective-permute-start(f32[2,136,128]{2,1,0:T(8,128)S(1)} %get-tuple-element.54), channel_id=1, source_target_pairs={{0,16},{16,0},{32,48},{48,32},{64,80},{80,64},{96,112},{112,96},{1... | collective-permute-start | bytes 417800 | tf_op jit(solution)/shard_map/ppermute | solution.py:280
  23.5 3.5 %copy-start = (f32[512]{0:T(512)S(1)}, f32[512]{0:T(512)}, u32[]{:S(2)}) copy-start(f32[512]{0:T(512)} %param.10) | copy-start | bytes 6148
  25.3 5.3 %collective-permute-start.6 = (f32[48,128]{1,0:T(8,128)S(1)}, f32[48,128]{1,0:T(8,128)S(1)}, u32[]{:S(2)}, u32[]{:S(2)}) collective-permute-start(f32[48,128]{1,0:T(8,128)S(1)} %get-tuple-element.55.mine_ref), channel_id=1, source_target_pairs={{0,1},{1,0},{2,3},{3,2},{4,5},{5,4},{6,7},{7,6},{8,9},{9,8},{10,11... | collective-permute-start | bytes 73736 | tf_op jit(solution)/shard_map/ppermute | solution.py:346

commit v5 on v4

--- a/solution.py
+++ b/solution.py
@@ -16,7 +16,9 @@
 
 
 def lines(groups):
-    return [list(range(groups - 2 + side, -1, -2)) for side in range(2)]
+    count = groups // 2
+    order = [6, 5, 4, 7, 3, 2, 1, 0] if count == 8 else list(range(count))[::-1]
+    return [[2 * at + side for at in order] for side in range(2)]
 
 
 def dot(a, b, dims):
@@ -44,10 +46,22 @@
     return slice(h * DH, (h + 1) * DH)
 
 
-def state_kernel(
-    heads, chunk, k_hbm, v_hbm, q_hbm, gate_hbm, owner_hbm,
-    ka_ref, va_ref, give_ref, mine_ref, q_ref, gate_ref, owners_ref, k_in, v_in, acc, owner, sems, late,
-):
+def pair_start(width, own):
+    core = lax.rem(lax.axis_index("seq"), 2)
+    return pl.multiple_of((core if own else 1 - core) * (width // 2), width // 2)
+
+
+def add_states(first, part, k_in, v_in, ka_ref, va_ref, state_ref):
+    for i in range(state_ref.shape[0]):
+        wide = pl.ds(pl.multiple_of(first + i * DH, DH), DH)
+        k = silu(k_in[part, wide])
+        v = silu(v_in[part, wide])
+        ka_ref[part, cols_of(i)] = k
+        va_ref[part, cols_of(i)] = v
+        state_ref[i] += dot(k, v, ((0,), (0,)))
+
+
+def give_kernel(chunk, k_hbm, v_hbm, q_hbm, k_in, v_in, q_ref, ka_ref, va_ref, give_ref, sems, late):
     count = k_in.shape[0] // chunk
 
     def pair(c):
@@ -57,37 +71,36 @@
             pltpu.make_async_copy(v_hbm.at[part], v_in.at[part], sems.at[1, c]),
         ]
 
-    later = [
-        pltpu.make_async_copy(q_hbm, q_ref, late.at[0]),
-        pltpu.make_async_copy(gate_hbm, gate_ref, late.at[1]),
-        pltpu.make_async_copy(owner_hbm, owner, late.at[2]),
-    ]
+    later = pltpu.make_async_copy(q_hbm, q_ref, late)
     for c in range(count):
         for copy in pair(c):
             copy.start()
-    for copy in later:
-        copy.start()
-    acc[...] = jnp.zeros_like(acc)
+    later.start()
+    give_ref[...] = jnp.zeros_like(give_ref)
+    first = pair_start(k_in.shape[1], False)
 
     @pl.loop(0, count)
     def _(c):
         for copy in pair(c):
             copy.wait()
         part = pl.ds(pl.multiple_of(c * chunk, chunk), chunk)
-        for h in range(heads):
-            k = silu(k_in[part, cols_of(h)])
-            v = silu(v_in[part, cols_of(h)])
-            ka_ref[part, cols_of(h)] = k
-            va_ref[part, cols_of(h)] = v
-            acc[h] += dot(k, v, ((0,), (0,)))
-
-    half = heads // 2
-    core = lax.rem(lax.axis_index("seq"), 2)
-    for i in range(half):
-        give_ref[i] = acc[(1 - core) * half + i]
-        mine_ref[i] = acc[core * half + i]
-    for copy in later:
-        copy.wait()
+        add_states(first, part, k_in, v_in, ka_ref, va_ref, give_ref)
+
+    later.wait()
+
+
+def mine_kernel(chunk, k_in, v_in, owner_hbm, ka_ref, va_ref, mine_ref, owners_ref, owner, sem):
+    copy = pltpu.make_async_copy(owner_hbm, owner, sem)
+    copy.start()
+    mine_ref[...] = jnp.zeros_like(mine_ref)
+    first = pair_start(k_in.shape[1], True)
+
+    @pl.loop(0, k_in.shape[0] // chunk)
+    def _(c):
+        part = pl.ds(pl.multiple_of(c * chunk, chunk), chunk)
+        add_states(first, part, k_in, v_in, ka_ref, va_ref, mine_ref)
+
+    copy.wait()
     group = lax.axis_index("grp")
     for at, g in enumerate((group, group + 1 - 2 * lax.rem(group, 2))):
         owners_ref[at] = jnp.full(owners_ref.shape[1:], owner[g], jnp.int32)
@@ -125,8 +138,10 @@
             ref[i, DH:] = all_ref[i, some] + over_ref[i, some]
 
 
-def inside_kernel(first, heads, block, q_ref, ka_ref, va_ref, run_in, base_ref, qa_ref, run_ref):
+def inside_kernel(first, heads, block, q_ref, ka0_ref, va0_ref, ka1_ref, va1_ref, run_in, base_ref, qa_ref, run_ref):
     count = qa_ref.shape[0] // block
+    half = heads // 2
+    starts = [pair_start(q_ref.shape[1], own) for own in (True, False)]
     run_ref[...] = run_in[...]
     causal = lax.broadcasted_iota(jnp.int32, (block, block), 0) >= lax.broadcasted_iota(
         jnp.int32, (block, block), 1
@@ -137,9 +152,11 @@
         part = pl.ds(pl.multiple_of(n * block, block), block)
         whole = pl.ds(pl.multiple_of((first + n) * block, block), block)
         for h in range(heads):
-            q = silu(q_ref[whole, cols_of(h)])
-            k = ka_ref[whole, cols_of(h)]
-            v = va_ref[whole, cols_of(h)]
+            ka_ref, va_ref = (ka0_ref, va0_ref) if h < half else (ka1_ref, va1_ref)
+            i = h % half
+            q = silu(q_ref[whole, pl.ds(pl.multiple_of(starts[h // half] + i * DH, DH), DH)])
+            k = ka_ref[whole, cols_of(i)]
+            v = va_ref[whole, cols_of(i)]
             scores = jnp.where(causal, dot(q, k, ((1,), (1,))), 0.0).astype(BF16)
             state = run_ref[h]
             hi = state.astype(BF16)
@@ -151,49 +168,81 @@
             run_ref[h] = state + dot(k, v, ((0,), (0,)))
 
 
-def gate_kernel(attn_ref, gate_ref, gain_ref, out_ref):
-    sigmoid = 0.5 + 0.5 * jnp.tanh(gate_ref[...].astype(F32) * 0.5)
-    out_ref[...] = attn_ref[...] * (gain_ref[...] * sigmoid)
-
-
-def carry_kernel(
-    heads, block, base0_ref, base1_ref, qa0_ref, qa1_ref, keep_ref, got_ref,
-    attn_ref, mine_ref, states, squares,
-):
-    half = heads // 2
-    core = lax.rem(lax.axis_index("seq"), 2)
+def gate_kernel(block, own_ref, rest_ref, gate_hbm, gain_ref, out_ref, gate_in, sems):
+    count = gate_in.shape[0] // block
+    width = gate_in.shape[1]
+
+    def copy(n):
+        part = pl.ds(n * block, block)
+        return pltpu.make_async_copy(gate_hbm.at[part], gate_in.at[part], sems.at[n])
+
+    for n in range(count):
+        copy(n).start()
+    places = [pl.ds(pair_start(width, own), width // 2) for own in (True, False)]
+
+    @pl.loop(0, count)
+    def _(n):
+        copy(n).wait()
+        part = pl.ds(pl.multiple_of(n * block, block), block)
+        for attn_ref, cols in zip((own_ref, rest_ref), places):
+            sigmoid = 0.5 + 0.5 * jnp.tanh(gate_in[part, cols].astype(F32) * 0.5)
+            out_ref[part, cols] = attn_ref[part] * (gain_ref[:, cols] * sigmoid)
+
+
+def carry(pair, block, base_refs, qa_refs, state_ref, attn_ref, states, finish):
+    half = state_ref.shape[0]
     for i in range(half):
-        for ref, h in ((keep_ref, core * half + i), (got_ref, (1 - core) * half + i)):
-            state = ref[i, :DH]
-            hi = state.astype(BF16)
-            states[h, :DH] = hi
-            states[h, DH:] = (state - hi.astype(F32)).astype(BF16)
+        state = state_ref[i, :DH]
+        hi = state.astype(BF16)
+        states[i, :DH] = hi
+        states[i, DH:] = (state - hi.astype(F32)).astype(BF16)
     first = 0
-    for base_ref, qa_ref in ((base0_ref, qa0_ref), (base1_ref, qa1_ref)):
+    for base_ref, qa_ref in zip(base_refs, qa_refs):
 
         @pl.loop(0, base_ref.shape[0] // block, unroll=2)
         def _(n):
             part = pl.ds(pl.multiple_of(n * block, block), block)
             whole = pl.ds(pl.multiple_of((first + n) * block, block), block)
             sums = None
-            for h in range(heads):
-                q = qa_ref[part, cols_of(h)]
-                attn = base_ref[part, cols_of(h)] + dot(
-                    jnp.concatenate([q, q], axis=1), states[h], ((1,), (0,))
+            for i in range(half):
+                wide = cols_of(pair * half + i)
+                q = qa_ref[part, wide]
+                attn = base_ref[part, wide] + dot(
+                    jnp.concatenate([q, q], axis=1), states[i], ((1,), (0,))
                 )
-                attn_ref[whole, cols_of(h)] = attn
+                attn_ref[whole, cols_of(i)] = attn
                 sums = attn * attn if sums is None else sums + attn * attn
-            hi = sums.astype(BF16)
-            squares[whole, :DH] = hi
-            squares[whole, DH:] = (sums - hi.astype(F32)).astype(BF16)
+            finish(whole, sums)
 
         first += base_ref.shape[0] // block
 
+
+def carry_own_kernel(
+    block, base0_ref, base1_ref, qa0_ref, qa1_ref, keep_ref, attn_ref, sums_ref, states
+):
+    def finish(whole, sums):
+        sums_ref[whole] = sums
+
+    carry(0, block, (base0_ref, base1_ref), (qa0_ref, qa1_ref), keep_ref, attn_ref, states, finish)
+
+
+def carry_rest_kernel(
+    block, base0_ref, base1_ref, qa0_ref, qa1_ref, keep_ref, got_ref, sums_ref,
+    attn_ref, mine_ref, states, squares,
+):
+    def finish(whole, sums):
+        sums = sums + sums_ref[whole]
+        hi = sums.astype(BF16)
+        squares[whole, :DH] = hi
+        squares[whole, DH:] = (sums - hi.astype(F32)).astype(BF16)
+
+    carry(1, block, (base0_ref, base1_ref), (qa0_ref, qa1_ref), got_ref, attn_ref, states, finish)
     across = dot(jnp.ones((16, 2 * DH), BF16), squares[...], ((1,), (1,)))
     token_rows = squares.shape[0] // DH
     for c in range(token_rows):
         mine_ref[c : c + 1] = across[:1, cols_of(c)]
-    rows = keep_ref.shape[1] - DH
+    core = lax.rem(lax.axis_index("seq"), 2)
+    half, rows = keep_ref.shape[0], keep_ref.shape[1] - DH
     for i in range(half):
         for ref, h in ((keep_ref, core * half + i), (got_ref, (1 - core) * half + i)):
             mine_ref[pl.ds(pl.multiple_of(token_rows + h * rows, 8), rows)] = ref[i, DH:]
@@ -257,24 +306,17 @@
     dma = lambda *shape: pltpu.SemaphoreType.DMA(shape)
     limit = params(24)
 
-    ka, va, give, mine, query, gate, owners = pl.pallas_call(
-        functools.partial(state_kernel, heads, chunk),
-        in_specs=[HBM] * 5,
-        out_specs=[VMEM] * 7,
-        out_shape=[wide] * 2 + [pair_state] * 2 + [wide] * 2
-        + [pltpu.VMEM((2, rows, DH), jnp.int32)],
-        scratch_shapes=[
-            pltpu.VMEM((tokens, width), BF16),
-            pltpu.VMEM((tokens, width), BF16),
-            pltpu.VMEM((heads, DH, DH), F32),
-            pltpu.SMEM(head_owner.shape, jnp.int32),
-            dma(2, tokens // chunk),
-            dma(3),
-        ],
-        compiler_params=limit,
-        cost_estimate=cost(2 * tokens * width * DH, 4 * tokens * width),
-        name="local_state",
-    )(in_hbm(key_in), in_hbm(value_in), in_hbm(query_in), in_hbm(gate_in), in_hbm(head_owner))
+    half_wide = pltpu.VMEM((tokens, half * DH), BF16)
+    k_in, v_in, query, ka1, va1, give = pl.pallas_call(
+        functools.partial(give_kernel, chunk),
+        in_specs=[HBM] * 3,
+        out_specs=[VMEM] * 6,
+        out_shape=[wide] * 3 + [half_wide] * 2 + [pair_state],
+        scratch_shapes=[dma(2, tokens // chunk), pltpu.SemaphoreType.DMA],
+        compiler_params=limit,
+        cost_estimate=cost(tokens * width * DH, 6 * tokens * width),
+        name="give",
+    )(in_hbm(key_in), in_hbm(value_in), in_hbm(query_in))
 
     def swap(x, bit):
         return lax.ppermute(x, "seq", [(i, i ^ bit) for i in range(shards)])
@@ -283,11 +325,11 @@
         place = lambda i: i - i % (2 * chips) + (i + 2 * k) % (2 * chips)
         return lax.ppermute(x, "seq", [(i, place(i)) for i in range(shards)])
 
-    def inside(first, blocks, q, ka, va, run):
+    def inside(first, blocks, q, acts, run):
         part = blocks * block
         return pl.pallas_call(
             functools.partial(inside_kernel, first, heads, block),
-            in_specs=[VMEM] * 4,
+            in_specs=[VMEM] * 6,
             out_specs=[VMEM] * 3,
             out_shape=[
                 pltpu.VMEM((part, width), F32),
@@ -297,17 +339,29 @@
             compiler_params=limit,
             cost_estimate=cost(2 * part * width * (2 * block + 3 * DH), 12 * part * width),
             name="inside%d" % first,
-        )(q, ka, va, run)
+        )(q, *acts, run)
 
     cut = 5 * count // 8
     other = swap(give, 1)
+    k_in, _ = lax.optimization_barrier((k_in, give))
+    ka0, va0, mine, owners = pl.pallas_call(
+        functools.partial(mine_kernel, chunk),
+        in_specs=[VMEM, VMEM, HBM],
+        out_specs=[VMEM] * 4,
+        out_shape=[half_wide] * 2 + [pair_state, pltpu.VMEM((2, rows, DH), jnp.int32)],
+        scratch_shapes=[pltpu.SMEM(head_owner.shape, jnp.int32), pltpu.SemaphoreType.DMA],
+        compiler_params=limit,
+        cost_estimate=cost(tokens * width * DH, 3 * tokens * width),
+        name="mine",
+    )(k_in, v_in, in_hbm(head_owner))
+    other, mine = lax.optimization_barrier((other, mine))
     pair = pl.pallas_call(
         pair_kernel, in_specs=[VMEM] * 2, out_specs=VMEM, out_shape=pair_state,
         compiler_params=limit, name="pair",
     )(mine, other)
     around = [on_x(pair, k) for k in range(chips - 1, 0, -1)]
-    ka, va, _ = lax.optimization_barrier((ka, va, pair))
-    base0, qa0, run = inside(0, cut, query, ka, va, jnp.zeros((heads, DH, DH), F32))
+    acts = lax.optimization_barrier((ka0, va0, ka1, va1, pair))[:4]
+    base0, qa0, run = inside(0, cut, query, acts, jnp.zeros((heads, DH, DH), F32))
     base0, *around = lax.optimization_barrier((base0, *around))
     before_x, all_x = pl.pallas_call(
         functools.partial(along_x_kernel, chips),
@@ -316,7 +370,7 @@
     )(pair, *around)
     over = swap(all_x, 2 * chips)
     run, _ = lax.optimization_barrier((run, all_x))
-    base1, qa1, _ = inside(cut, count - cut, query, ka, va, run)
+    base1, qa1, _ = inside(cut, count - cut, query, acts, run)
     base1, over = lax.optimization_barrier((base1, over))
     keep, send_core = pl.pallas_call(
         functools.partial(along_y_kernel, chips),
@@ -326,33 +380,41 @@
     )(before_x, all_x, over, mine, other)
     got_core = swap(send_core, 1)
     payload = token_rows + heads * rows
-    attn, own = pl.pallas_call(
-        functools.partial(carry_kernel, heads, block),
-        in_specs=[VMEM] * 6,
+    half_attn = pltpu.VMEM((tokens, half * DH), F32)
+    states = pltpu.VMEM((half, 2 * DH, DH), BF16)
+    attn_own, sums = pl.pallas_call(
+        functools.partial(carry_own_kernel, block),
+        in_specs=[VMEM] * 5,
         out_specs=[VMEM] * 2,
-        out_shape=[
-            pltpu.VMEM((tokens, width), F32),
-            pltpu.VMEM((payload, DH), F32),
-        ],
-        scratch_shapes=[
-            pltpu.VMEM((heads, 2 * DH, DH), BF16),
-            pltpu.VMEM((tokens, 2 * DH), BF16),
-        ],
-        compiler_params=limit,
-        cost_estimate=cost(4 * tokens * width * DH, 10 * tokens * width),
-        name="carry",
-    )(base0, base1, qa0, qa1, keep, got_core)
+        out_shape=[half_attn, pltpu.VMEM((tokens, DH), F32)],
+        scratch_shapes=[states],
+        compiler_params=limit,
+        cost_estimate=cost(2 * tokens * width * DH, 5 * tokens * width),
+        name="carry_own",
+    )(base0, base1, qa0, qa1, keep)
+    sums, got_core = lax.optimization_barrier((sums, got_core))
+    attn_rest, own = pl.pallas_call(
+        functools.partial(carry_rest_kernel, block),
+        in_specs=[VMEM] * 7,
+        out_specs=[VMEM] * 2,
+        out_shape=[half_attn, pltpu.VMEM((payload, DH), F32)],
+        scratch_shapes=[states, pltpu.VMEM((tokens, 2 * DH), BF16)],
+        compiler_params=limit,
+        cost_estimate=cost(2 * tokens * width * DH, 5 * tokens * width),
+        name="carry_rest",
+    )(base0, base1, qa0, qa1, keep, got_core, sums)
 
     beside = lax.ppermute(own, "grp", [(g, g ^ 1) for g in range(groups)])
     gated = pl.pallas_call(
-        gate_kernel,
-        in_specs=[VMEM] * 3,
+        functools.partial(gate_kernel, block),
+        in_specs=[VMEM, VMEM, HBM, VMEM],
         out_specs=VMEM,
         out_shape=pltpu.VMEM((tokens, width), F32),
+        scratch_shapes=[pltpu.VMEM((tokens, width), BF16), dma(count)],
         compiler_params=limit,
         cost_estimate=cost(4 * tokens * width, 10 * tokens * width),
         name="gate",
-    )(attn, gate, norm_gain.reshape(1, width))
+    )(attn_own, attn_rest, in_hbm(gate_in), norm_gain.reshape(1, width))
     gated, beside = lax.optimization_barrier((gated, beside))
     send = pl.pallas_call(
         pack_kernel,

time: 49 us -> 47.5 us (0.969)
  the two profiles are of different devices: /device:TPU:16 before, /device:TPU:1 now
where the time goes in v5:
time: 47.5 us; the launch traced here: 47.4 us
  Pallas kernels  19.3 us (41%)
  blocking collectives  14.1 us (30%)
  starting transfers between devices  10.9 us (23%)
  waiting for transfers between devices  2.23 us (5%)
  between operations  0.73 us (2%)
    all_to_all x1, blocking collectives, body(): lax.all_to_all(send, 'grp', 0, 0, tiled=True, axis_index_groups=lines(gro...  14.1 us
    pallas_call x2, Pallas kernels, inside(): pl.pallas_call(functools.partial(inside_kernel, first, heads, block), in_...  8.06 us
    ppermute x3, starting transfers between devices, swap(): return lax.ppermute(x, 'seq', [(i, i ^ bit) for i in range(shards)])  6.05 us
    ppermute x3, starting transfers between devices, on_x(): return lax.ppermute(x, 'seq', [(i, place(i)) for i in range(shards)])  3.15 us
    pallas_call x1, Pallas kernels, body(): pl.pallas_call(functools.partial(give_kernel, chunk), in_specs=[HBM] * 3,...  2.96 us
    pallas_call x1, Pallas kernels, body(): pl.pallas_call(functools.partial(norm_kernel, heads, float(width * groups...  2.24 us
    pallas_call x1, Pallas kernels, body(): pl.pallas_call(functools.partial(gate_kernel, block), in_specs=[VMEM, VME...  2.04 us
    ppermute x1, starting transfers between devices, body(): beside = lax.ppermute(own, 'grp', [(g, g ^ 1) for g in range(groups)])  1.73 us
  transfers between devices with their start and end apart: 7, of which 4 were waited for; matrix products, arithmetic and copies ran while one was open for 0% of the time, Pallas kernels for 27%

profile of v5, /device:TPU:1, one launch (start us, length us, event | category | flops | bytes accessed | tf_op | source)
XLA Modules:
  0.0 47.4 jit_solution(7402244700012551147)
XLA Ops:
  0.6 3.0 %give.1 = (bf16[2048,512]{1,0:T(8,128)(2,1)S(1)}, bf16[2048,512]{1,0:T(8,128)(2,1)S(1)}, bf16[2048,512]{1,0:T(8,128)(2,1)S(1)}, bf16[2048,256]{1,0:T(8,128)(2,1)...) custom-call(bf16[2048,512]{1,0:T(8,128)(2,1)} %k_hbm.1, bf16[2048,512]{1,0:T(8,128)(2,1)} %v_hbm.1, ...), custom_call_target="tpu_custom_call" | custom-call | flops 134217728 | bytes 6291456 | tf_op jit(solution)/shard_map/give/pallas_call | solution.py:310
  3.6 3.3 %collective-permute-start = (f32[2,128,128]{2,1,0:T(8,128)S(1)}, f32[2,128,128]{2,1,0:T(8,128)S(1)}, u32[]{:S(2)}, u32[]{:S(2)}) collective-permute-start(f32[2,128,128]{2,1,0:T(8,128)S(1)} %get-tuple-element.44), channel_id=1, source_target_pairs={{0,16},{16,0},{32,48},{48,32},{64,80},{80,64},{96,112},{112,96},{1... | collective-permute-start | bytes 393224 | tf_op jit(solution)/shard_map/ppermute | solution.py:322
  6.9 1.7 %mine.1 = (bf16[2048,256]{1,0:T(8,128)(2,1)S(1)}, bf16[2048,256]{1,0:T(8,128)(2,1)S(1)}, f32[2,128,128]{2,1,0:T(8,128)S(1)}, s32[2,8,128]{2,1,0:T(8,128)S(1)}) custom-call(bf16[2048,512]{1,0:T(8,128)(2,1)S(1)} %get-tuple-element.45.k_in, bf16[2048,512]{1,0:T(8,128)(2,1)S(1)} %get-tuple-element.46.v_in, s32[16]{0:T(128)} %owner_hbm.1), custom_call_target="tpu_custom_call" | custom-call | flops 134217728 | bytes 3145728 | tf_op jit(solution)/shard_map/mine/pallas_call | solution.py:347
  8.6 0.0 collective-permute-done.other_ref
  8.6 0.1 collective-permute-start.3
  8.7 1.9 %collective-permute-start.2 = (f32[2,128,128]{2,1,0:T(8,128)S(1)}, f32[2,128,128]{2,1,0:T(8,128)S(1)}, u32[]{:S(2)}, u32[]{:S(2)}) collective-permute-start(f32[2,128,128]{2,1,0:T(8,128)S(1)} %pair.1.own_ref), channel_id=1, source_target_pairs={{0,64},{16,80},{32,96},{48,112},{64,0},{80,16},{96,32},{112,48},{1... | collective-permute-start | bytes 393224 | tf_op jit(solution)/shard_map/ppermute | solution.py:326
  10.6 1.2 %collective-permute-start.1 = (f32[2,128,128]{2,1,0:T(8,128)S(1)}, f32[2,128,128]{2,1,0:T(8,128)S(1)}, u32[]{:S(2)}, u32[]{:S(2)}) collective-permute-start(f32[2,128,128]{2,1,0:T(8,128)S(1)} %pair.1.own_ref), channel_id=1, source_target_pairs={{0,96},{16,112},{32,0},{48,16},{64,32},{80,48},{96,64},{112,80},{1... | collective-permute-start | bytes 393224 | tf_op jit(solution)/shard_map/ppermute | solution.py:326
  11.8 4.6 %inside0.1 = (f32[1280,512]{1,0:T(8,128)S(1)}, bf16[1280,512]{1,0:T(8,128)(2,1)S(1)}, f32[4,128,128]{2,1,0:T(8,128)S(1)}) custom-call(bf16[2048,512]{1,0:T(8,128)(2,1)S(1)} %get-tuple-element.48.q_ref, bf16[2048,256]{1,0:T(8,128)(2,1)S(1)} %get-tuple-element.56.ka0_ref, bf16[2048,256]{1,0:T(8,128)(2,1)S(1)} %get-tuple-element.57.va0_ref, ...), custom_call_target="tpu_custom_call" | custom-call | flops 1174405120 | bytes 7864320 | tf_op jit(solution)/shard_map/inside0/pallas_call | solution.py:330
  16.4 1.4 %collective-permute-done.3.refs_2_ = f32[2,128,128]{2,1,0:T(8,128)S(1)} collective-permute-done((f32[2,128,128]{2,1,0:T(8,128)S(1)}, f32[2,128,128]{2,1,0:T(8,128)S(1)}, u32[]{:S(2)}, u32[]{:S(2)}) %collective-permute-start.3) | collective-permute-done | bytes 131104 | tf_op jit(solution)/shard_map/ppermute | solution.py:326
  17.8 0.0 collective-permute-done.2.refs_1_
  17.8 0.3 collective-permute-done.1.refs_0_
  18.2 0.4 collective-permute-start.4
  18.5 3.4 %inside5.1 = (f32[768,512]{1,0:T(8,128)S(1)}, bf16[768,512]{1,0:T(8,128)(2,1)S(1)}, f32[4,128,128]{2,1,0:T(8,128)}) custom-call(bf16[2048,512]{1,0:T(8,128)(2,1)S(1)} %get-tuple-element.48.q_ref, bf16[2048,256]{1,0:T(8,128)(2,1)S(1)} %get-tuple-element.56.ka0_ref, bf16[2048,256]{1,0:T(8,128)(2,1)S(1)} %get-tuple-element.57.va0_ref, ...), custom_call_target="tpu_custom_call" | custom-call | flops 704643072 | bytes 4718592 | tf_op jit(solution)/shard_map/inside5/pallas_call | solution.py:330
  22.0 0.1 collective-permute-done.4.over_ref
  22.1 2.4 %collective-permute-start.5 = (f32[2,136,128]{2,1,0:T(8,128)S(1)}, f32[2,136,128]{2,1,0:T(8,128)S(1)}, u32[]{:S(2)}, u32[]{:S(2)}) collective-permute-start(f32[2,136,128]{2,1,0:T(8,128)S(1)} %get-tuple-element.76), channel_id=1, source_target_pairs={{0,16},{16,0},{32,48},{48,32},{64,80},{80,64},{96,112},{112,96},{1... | collective-permute-start | bytes 417800 | tf_op jit(solution)/shard_map/ppermute | solution.py:322
  24.5 1.0 %carry_own.1 = (f32[2048,256]{1,0:T(8,128)S(1)}, f32[2048,128]{1,0:T(8,128)S(1)}) custom-call(f32[1280,512]{1,0:T(8,128)S(1)} %get-tuple-element.61.base0_ref, f32[768,512]{1,0:T(8,128)S(1)} %get-tuple-element.69.base1_ref, bf16[1280,512]{1,0:T(8,128)(2,1)S(1)} %get-tuple-element.70.qa0_ref, bf16[768,512]{1,0:T(8,128)(2,1)S(1)} %get-tuple-element.71.qa1_ref, ...), custom_call_target="tpu_custom_call" | custom-call | flops 268435456 | bytes 5242880 | tf_op jit(solution)/shard_map/carry_own/pallas_call | solution.py:385
  25.5 0.0 collective-permute-done.5.got_ref
  25.5 0.0 copy-start
  25.5 1.2 %carry_rest.1 = (f32[2048,256]{1,0:T(8,128)S(1)}, f32[48,128]{1,0:T(8,128)S(1)}) custom-call(f32[1280,512]{1,0:T(8,128)S(1)} %get-tuple-element.61.base0_ref, f32[768,512]{1,0:T(8,128)S(1)} %get-tuple-element.69.base1_ref, bf16[1280,512]{1,0:T(8,128)(2,1)S(1)} %get-tuple-element.70.qa0_ref, bf16[768,512]{1,0:T(8,128)(2,1)S(1)} %get-tuple-element.71.qa1_ref, ...), custom_call_target="tpu_custom_call" | custom-call | flops 268435456 | bytes 5242880 | tf_op jit(solution)/shard_map/carry_rest/pallas_call | solution.py:396
  26.7 1.7 %collective-permute-start.6 = (f32[48,128]{1,0:T(8,128)S(1)}, f32[48,128]{1,0:T(8,128)S(1)}, u32[]{:S(2)}, u32[]{:S(2)}) collective-permute-start(f32[48,128]{1,0:T(8,128)S(1)} %get-tuple-element.79.mine_ref), channel_id=1, source_target_pairs={{0,1},{1,0},{2,3},{3,2},{4,5},{5,4},{6,7},{7,6},{8,9},{9,8},{10,11... | collective-permute-start | bytes 73736 | tf_op jit(solution)/shard_map/ppermute | solution.py:407
  28.5 0.0 copy-done
  28.5 2.0 %gate.1.gated_ref = f32[2048,512]{1,0:T(8,128)S(1)} custom-call(f32[2048,256]{1,0:T(8,128)S(1)} %get-tuple-element.80.own_ref, f32[2048,256]{1,0:T(8,128)S(1)} %get-tuple-element.81.rest_ref, bf16[2048,512]{1,0:T(8,128)(2,1)} %gate_hbm.1, f32[1,512]{1,0:T(1,128)S(1)} %bitcast.1), custom_call_target="tpu_custom_call" | custom-call | flops 4194304 | bytes 10485760 | tf_op jit(solution)/shard_map/gate/pallas_call | solution.py:408
  30.5 0.4 collective-permute-done.6.other_ref
  31.0 14.1 %all_to_all.5.got_ref = f32[8,48,128]{2,1,0:T(8,128)S(1)} all-to-all(f32[8,48,128]{2,1,0:T(8,128)S(1)} %pack.1), channel_id=1, replica_groups={{12,10,8,14,6,4,2,0},{13,11,9,15,7,5,3,1},{28,26,24,30,22,20,18,16},{29..., dimensions={0} | all-to-all | bytes 393216 | tf_op jit(solution)/shard_map/all_to_all | solution.py:428
  45.1 2.2 %norm.1 = (bf16[2048,512]{1,0:T(8,128)(2,1)}, f32[4,8,128]{2,1,0:T(8,128)}) custom-call(f32[8,48,128]{2,1,0:T(8,128)S(1)} %all_to_all.5.got_ref, f32[2048,512]{1,0:T(8,128)S(1)} %gate.1.gated_ref), custom_call_target="tpu_custom_call" | custom-call | flops 2097152 | bytes 6291456 | tf_op jit(solution)/shard_map/norm/pallas_call | solution.py:432
  (5 shorter events, 0.2 us)
Async XLA Ops:
  3.6 5.0 %collective-permute-start = (f32[2,128,128]{2,1,0:T(8,128)S(1)}, f32[2,128,128]{2,1,0:T(8,128)S(1)}, u32[]{:S(2)}, u32[]{:S(2)}) collective-permute-start(f32[2,128,128]{2,1,0:T(8,128)S(1)} %get-tuple-element.44), channel_id=1, source_target_pairs={{0,16},{16,0},{32,48},{48,32},{64,80},{80,64},{96,112},{112,96},{1... | collective-permute-start | bytes 393224 | tf_op jit(solution)/shard_map/ppermute | solution.py:322
  8.6 9.2 %collective-permute-start.3 = (f32[2,128,128]{2,1,0:T(8,128)S(1)}, f32[2,128,128]{2,1,0:T(8,128)S(1)}, u32[]{:S(2)}, u32[]{:S(2)}) collective-permute-start(f32[2,128,128]{2,1,0:T(8,128)S(1)} %pair.1.own_ref), channel_id=1, source_target_pairs={{0,32},{16,48},{32,64},{48,80},{64,96},{80,112},{96,0},{112,16},{1... | collective-permute-start | bytes 393224 | tf_op jit(solution)/shard_map/ppermute | solution.py:326
  8.7 9.1 %collective-permute-start.2 = (f32[2,128,128]{2,1,0:T(8,128)S(1)}, f32[2,128,128]{2,1,0:T(8,128)S(1)}, u32[]{:S(2)}, u32[]{:S(2)}) collective-permute-start(f32[2,128,128]{2,1,0:T(8,128)S(1)} %pair.1.own_ref), channel_id=1, source_target_pairs={{0,64},{16,80},{32,96},{48,112},{64,0},{80,16},{96,32},{112,48},{1... | collective-permute-start | bytes 393224 | tf_op jit(solution)/shard_map/ppermute | solution.py:326
  10.6 7.5 %collective-permute-start.1 = (f32[2,128,128]{2,1,0:T(8,128)S(1)}, f32[2,128,128]{2,1,0:T(8,128)S(1)}, u32[]{:S(2)}, u32[]{:S(2)}) collective-permute-start(f32[2,128,128]{2,1,0:T(8,128)S(1)} %pair.1.own_ref), channel_id=1, source_target_pairs={{0,96},{16,112},{32,0},{48,16},{64,32},{80,48},{96,64},{112,80},{1... | collective-permute-start | bytes 393224 | tf_op jit(solution)/shard_map/ppermute | solution.py:326
  18.2 3.9 %collective-permute-start.4 = (f32[2,128,128]{2,1,0:T(8,128)S(1)}, f32[2,128,128]{2,1,0:T(8,128)S(1)}, u32[]{:S(2)}, u32[]{:S(2)}) collective-permute-start(f32[2,128,128]{2,1,0:T(8,128)S(1)} %get-tuple-element.66.all_ref), channel_id=1, source_target_pairs={{0,128},{16,144},{32,160},{48,176},{64,192},{80,208},{96,224},{112... | collective-permute-start | bytes 393224 | tf_op jit(solution)/shard_map/ppermute | solution.py:322
  22.1 3.4 %collective-permute-start.5 = (f32[2,136,128]{2,1,0:T(8,128)S(1)}, f32[2,136,128]{2,1,0:T(8,128)S(1)}, u32[]{:S(2)}, u32[]{:S(2)}) collective-permute-start(f32[2,136,128]{2,1,0:T(8,128)S(1)} %get-tuple-element.76), channel_id=1, source_target_pairs={{0,16},{16,0},{32,48},{48,32},{64,80},{80,64},{96,112},{112,96},{1... | collective-permute-start | bytes 417800 | tf_op jit(solution)/shard_map/ppermute | solution.py:322
  25.5 3.0 %copy-start = (f32[512]{0:T(512)S(1)}, f32[512]{0:T(512)}, u32[]{:S(2)}) copy-start(f32[512]{0:T(512)} %param.10) | copy-start | bytes 6148
  26.7 4.2 %collective-permute-start.6 = (f32[48,128]{1,0:T(8,128)S(1)}, f32[48,128]{1,0:T(8,128)S(1)}, u32[]{:S(2)}, u32[]{:S(2)}) collective-permute-start(f32[48,128]{1,0:T(8,128)S(1)} %get-tuple-element.79.mine_ref), channel_id=1, source_target_pairs={{0,1},{1,0},{2,3},{3,2},{4,5},{5,4},{6,7},{7,6},{8,9},{9,8},{10,11... | collective-permute-start | bytes 73736 | tf_op jit(solution)/shard_map/ppermute | solution.py:407

commit v6 on v5

--- a/solution.py
+++ b/solution.py
@@ -8,6 +8,7 @@
 from jax.sharding import PartitionSpec as P
 
 DH = 128
+HOPS = (2, 3, 1)
 F32 = jnp.float32
 BF16 = jnp.bfloat16
 MIB = 1 << 20
@@ -51,7 +52,8 @@
     return pl.multiple_of((core if own else 1 - core) * (width // 2), width // 2)
 
 
-def add_states(first, part, k_in, v_in, ka_ref, va_ref, state_ref):
+def add_states(first, c, part, k_in, v_in, ka_ref, va_ref, state_ref, runs_ref):
+    runs_ref[c] = state_ref[...]
     for i in range(state_ref.shape[0]):
         wide = pl.ds(pl.multiple_of(first + i * DH, DH), DH)
         k = silu(k_in[part, wide])
@@ -61,46 +63,62 @@
         state_ref[i] += dot(k, v, ((0,), (0,)))
 
 
-def give_kernel(chunk, k_hbm, v_hbm, q_hbm, k_in, v_in, q_ref, ka_ref, va_ref, give_ref, sems, late):
-    count = k_in.shape[0] // chunk
+def give_kernel(
+    chunk, k_hbm, v_hbm, k_in, v_in, ka_ref, va_ref, give_ref, runs_ref, sems, late
+):
+    tokens, width = k_in.shape
+    count = tokens // chunk
+    first = pair_start(width, False)
 
     def pair(c):
-        part = pl.ds(c * chunk, chunk)
+        place = (pl.ds(c * chunk, chunk), pl.ds(first, width // 2))
         return [
-            pltpu.make_async_copy(k_hbm.at[part], k_in.at[part], sems.at[0, c]),
-            pltpu.make_async_copy(v_hbm.at[part], v_in.at[part], sems.at[1, c]),
+            pltpu.make_async_copy(k_hbm.at[place], k_in.at[place], sems.at[0, c]),
+            pltpu.make_async_copy(v_hbm.at[place], v_in.at[place], sems.at[1, c]),
         ]
 
-    later = pltpu.make_async_copy(q_hbm, q_ref, late)
+    own = (slice(None), pl.ds(pair_start(width, True), width // 2))
+    later = [
+        pltpu.make_async_copy(k_hbm.at[own], k_in.at[own], late.at[0]),
+        pltpu.make_async_copy(v_hbm.at[own], v_in.at[own], late.at[1]),
+    ]
     for c in range(count):
         for copy in pair(c):
             copy.start()
-    later.start()
+    for copy in later:
+        copy.start()
     give_ref[...] = jnp.zeros_like(give_ref)
-    first = pair_start(k_in.shape[1], False)
 
     @pl.loop(0, count)
     def _(c):
         for copy in pair(c):
             copy.wait()
         part = pl.ds(pl.multiple_of(c * chunk, chunk), chunk)
-        add_states(first, part, k_in, v_in, ka_ref, va_ref, give_ref)
-
-    later.wait()
-
-
-def mine_kernel(chunk, k_in, v_in, owner_hbm, ka_ref, va_ref, mine_ref, owners_ref, owner, sem):
-    copy = pltpu.make_async_copy(owner_hbm, owner, sem)
-    copy.start()
+        add_states(first, c, part, k_in, v_in, ka_ref, va_ref, give_ref, runs_ref)
+
+    for copy in later:
+        copy.wait()
+
+
+def mine_kernel(
+    chunk, k_in, v_in, q_hbm, owner_hbm, ka_ref, va_ref, mine_ref, runs_ref, q_ref, owners_ref, owner, sems
+):
+    copies = [
+        pltpu.make_async_copy(q_hbm, q_ref, sems.at[0]),
+        pltpu.make_async_copy(owner_hbm, owner, sems.at[1]),
+    ]
+    for copy in copies:
+        copy.start()
     mine_ref[...] = jnp.zeros_like(mine_ref)
     first = pair_start(k_in.shape[1], True)
 
     @pl.loop(0, k_in.shape[0] // chunk)
     def _(c):
         part = pl.ds(pl.multiple_of(c * chunk, chunk), chunk)
-        add_states(first, part, k_in, v_in, ka_ref, va_ref, mine_ref)
-
-    copy.wait()
+        add_states(first, c, part, k_in, v_in, ka_ref, va_ref, mine_ref, runs_ref)
+
+    for copy in copies:
+        copy.wait()
     group = lax.axis_index("grp")
     for at, g in enumerate((group, group + 1 - 2 * lax.rem(group, 2))):
         owners_ref[at] = jnp.full(owners_ref.shape[1:], owner[g], jnp.int32)
@@ -116,7 +134,7 @@
     total = own_ref[...]
     before = jnp.zeros_like(total)
     for back in range(1, chips):
-        part = got[chips - 1 - back][...]
+        part = got[HOPS.index(back)][...]
         total = total + part
         before = before + jnp.where(x >= back, part, 0.0)
     before_ref[...] = before
@@ -138,34 +156,42 @@
             ref[i, DH:] = all_ref[i, some] + over_ref[i, some]
 
 
-def inside_kernel(first, heads, block, q_ref, ka0_ref, va0_ref, ka1_ref, va1_ref, run_in, base_ref, qa_ref, run_ref):
+def inside_kernel(
+    first, heads, block, q_ref, ka0_ref, va0_ref, runs0_ref, ka1_ref, va1_ref, runs1_ref,
+    base_ref, qa_ref,
+):
     count = qa_ref.shape[0] // block
     half = heads // 2
     starts = [pair_start(q_ref.shape[1], own) for own in (True, False)]
-    run_ref[...] = run_in[...]
-    causal = lax.broadcasted_iota(jnp.int32, (block, block), 0) >= lax.broadcasted_iota(
-        jnp.int32, (block, block), 1
-    )
-
-    @pl.loop(0, count, unroll=2)
-    def _(n):
-        part = pl.ds(pl.multiple_of(n * block, block), block)
-        whole = pl.ds(pl.multiple_of((first + n) * block, block), block)
+    causal = (
+        lax.broadcasted_iota(jnp.int32, (block, block), 0)
+        >= lax.broadcasted_iota(jnp.int32, (block, block), 1)
+    ).astype(BF16)
+
+    @pl.loop(0, count // 2)
+    def _(c):
         for h in range(heads):
-            ka_ref, va_ref = (ka0_ref, va0_ref) if h < half else (ka1_ref, va1_ref)
+            ka_ref, va_ref, runs_ref = (
+                (ka0_ref, va0_ref, runs0_ref) if h < half else (ka1_ref, va1_ref, runs1_ref)
+            )
             i = h % half
-            q = silu(q_ref[whole, pl.ds(pl.multiple_of(starts[h // half] + i * DH, DH), DH)])
-            k = ka_ref[whole, cols_of(i)]
-            v = va_ref[whole, cols_of(i)]
-            scores = jnp.where(causal, dot(q, k, ((1,), (1,))), 0.0).astype(BF16)
-            state = run_ref[h]
-            hi = state.astype(BF16)
-            lo = (state - hi.astype(F32)).astype(BF16)
-            left = jnp.concatenate([scores, q, q], axis=1)
-            right = jnp.concatenate([v, hi, lo], axis=0)
-            base_ref[part, cols_of(h)] = dot(left, right, ((1,), (0,)))
-            qa_ref[part, cols_of(h)] = q
-            run_ref[h] = state + dot(k, v, ((0,), (0,)))
+            column = pl.ds(pl.multiple_of(starts[h // half] + i * DH, DH), DH)
+            state = runs_ref[first // 2 + c, i]
+            for odd in range(2):
+                part = pl.ds(pl.multiple_of((2 * c + odd) * block, block), block)
+                whole = pl.ds(pl.multiple_of((first + 2 * c + odd) * block, block), block)
+                q = silu(q_ref[whole, column])
+                k = ka_ref[whole, cols_of(i)]
+                v = va_ref[whole, cols_of(i)]
+                scores = dot(q, k, ((1,), (1,))).astype(BF16) * causal
+                hi = state.astype(BF16)
+                lo = (state - hi.astype(F32)).astype(BF16)
+                left = jnp.concatenate([scores, q, q], axis=1)
+                right = jnp.concatenate([v, hi, lo], axis=0)
+                base_ref[part, cols_of(h)] = dot(left, right, ((1,), (0,)))
+                qa_ref[part, cols_of(h)] = q
+                if not odd:
+                    state = state + dot(k, v, ((0,), (0,)))
 
 
 def gate_kernel(block, own_ref, rest_ref, gate_hbm, gain_ref, out_ref, gate_in, sems):
@@ -199,7 +225,7 @@
     first = 0
     for base_ref, qa_ref in zip(base_refs, qa_refs):
 
-        @pl.loop(0, base_ref.shape[0] // block, unroll=2)
+        @pl.loop(0, base_ref.shape[0] // block, unroll=True)
         def _(n):
             part = pl.ds(pl.multiple_of(n * block, block), block)
             whole = pl.ds(pl.multiple_of((first + n) * block, block), block)
@@ -307,16 +333,17 @@
     limit = params(24)
 
     half_wide = pltpu.VMEM((tokens, half * DH), BF16)
-    k_in, v_in, query, ka1, va1, give = pl.pallas_call(
+    runs = pltpu.VMEM((tokens // chunk, half, DH, DH), F32)
+    k_in, v_in, ka1, va1, give, runs1 = pl.pallas_call(
         functools.partial(give_kernel, chunk),
-        in_specs=[HBM] * 3,
+        in_specs=[HBM] * 2,
         out_specs=[VMEM] * 6,
-        out_shape=[wide] * 3 + [half_wide] * 2 + [pair_state],
-        scratch_shapes=[dma(2, tokens // chunk), pltpu.SemaphoreType.DMA],
+        out_shape=[wide] * 2 + [half_wide] * 2 + [pair_state, runs],
+        scratch_shapes=[dma(2, tokens // chunk), dma(2)],
         compiler_params=limit,
         cost_estimate=cost(tokens * width * DH, 6 * tokens * width),
         name="give",
-    )(in_hbm(key_in), in_hbm(value_in), in_hbm(query_in))
+    )(in_hbm(key_in), in_hbm(value_in))
 
     def swap(x, bit):
         return lax.ppermute(x, "seq", [(i, i ^ bit) for i in range(shards)])
@@ -325,43 +352,43 @@
         place = lambda i: i - i % (2 * chips) + (i + 2 * k) % (2 * chips)
         return lax.ppermute(x, "seq", [(i, place(i)) for i in range(shards)])
 
-    def inside(first, blocks, q, acts, run):
+    def inside(first, blocks, q, acts):
         part = blocks * block
         return pl.pallas_call(
             functools.partial(inside_kernel, first, heads, block),
-            in_specs=[VMEM] * 6,
-            out_specs=[VMEM] * 3,
+            in_specs=[VMEM] * 7,
+            out_specs=[VMEM] * 2,
             out_shape=[
                 pltpu.VMEM((part, width), F32),
                 pltpu.VMEM((part, width), BF16),
-                pltpu.VMEM((heads, DH, DH), F32),
             ],
             compiler_params=limit,
             cost_estimate=cost(2 * part * width * (2 * block + 3 * DH), 12 * part * width),
             name="inside%d" % first,
-        )(q, *acts, run)
-
-    cut = 5 * count // 8
+        )(q, *acts)
+
+    cut = 6 * count // 8
     other = swap(give, 1)
     k_in, _ = lax.optimization_barrier((k_in, give))
-    ka0, va0, mine, owners = pl.pallas_call(
+    ka0, va0, mine, runs0, query, owners = pl.pallas_call(
         functools.partial(mine_kernel, chunk),
-        in_specs=[VMEM, VMEM, HBM],
-        out_specs=[VMEM] * 4,
-        out_shape=[half_wide] * 2 + [pair_state, pltpu.VMEM((2, rows, DH), jnp.int32)],
-        scratch_shapes=[pltpu.SMEM(head_owner.shape, jnp.int32), pltpu.SemaphoreType.DMA],
+        in_specs=[VMEM, VMEM, HBM, HBM],
+        out_specs=[VMEM] * 6,
+        out_shape=[half_wide] * 2
+        + [pair_state, runs, wide, pltpu.VMEM((2, rows, DH), jnp.int32)],
+        scratch_shapes=[pltpu.SMEM(head_owner.shape, jnp.int32), dma(2)],
         compiler_params=limit,
         cost_estimate=cost(tokens * width * DH, 3 * tokens * width),
         name="mine",
-    )(k_in, v_in, in_hbm(head_owner))
+    )(k_in, v_in, in_hbm(query_in), in_hbm(head_owner))
     other, mine = lax.optimization_barrier((other, mine))
     pair = pl.pallas_call(
         pair_kernel, in_specs=[VMEM] * 2, out_specs=VMEM, out_shape=pair_state,
         compiler_params=limit, name="pair",
     )(mine, other)
-    around = [on_x(pair, k) for k in range(chips - 1, 0, -1)]
-    acts = lax.optimization_barrier((ka0, va0, ka1, va1, pair))[:4]
-    base0, qa0, run = inside(0, cut, query, acts, jnp.zeros((heads, DH, DH), F32))
+    around = [on_x(pair, k) for k in HOPS]
+    acts = lax.optimization_barrier((ka0, va0, runs0, ka1, va1, runs1, pair))[:6]
+    base0, qa0 = inside(0, cut, query, acts)
     base0, *around = lax.optimization_barrier((base0, *around))
     before_x, all_x = pl.pallas_call(
         functools.partial(along_x_kernel, chips),
@@ -369,8 +396,8 @@
         compiler_params=limit, name="along_x",
     )(pair, *around)
     over = swap(all_x, 2 * chips)
-    run, _ = lax.optimization_barrier((run, all_x))
-    base1, qa1, _ = inside(cut, count - cut, query, acts, run)
+    acts = lax.optimization_barrier((*acts, all_x))[:6]
+    base1, qa1 = inside(cut, count - cut, query, acts)
     base1, over = lax.optimization_barrier((base1, over))
     keep, send_core = pl.pallas_call(
         functools.partial(along_y_kernel, chips),

time: 47.5 us -> 46.9 us (0.987)
  Pallas kernels: 19.3 us -> 17 us
  starting transfers between devices: 10.9 us -> 12 us
    pallas_call x2, Pallas kernels: 8.06 us -> 6.57 us  [inside(): pl.pallas_call(functools.partial(inside_kernel, first, heads, block), in_...]
    ppermute x3, waiting for transfers between devices: 0.12 us -> 1.46 us  [swap(): return lax.ppermute(x, 'seq', [(i, i ^ bit) for i in range(shards)])]
    ppermute x3, starting transfers between devices: 6.05 us -> 7.11 us  [swap(): return lax.ppermute(x, 'seq', [(i, i ^ bit) for i in range(shards)])]
    ppermute x3, waiting for transfers between devices: 1.68 us -> 1 us  [on_x(): return lax.ppermute(x, 'seq', [(i, place(i)) for i in range(shards)])]
  transfers between devices with their start and end apart: 7 -> 7, of which waited for: 4 -> 4; matrix products, arithmetic and copies ran while one was open for 0% -> 0% of each run, Pallas kernels for 27% -> 23%
where the time goes in v6:
time: 46.9 us; the launch traced here: 46.8 us
  Pallas kernels  17 us (36%)
  blocking collectives  14.5 us (31%)
  starting transfers between devices  12 us (26%)
  waiting for transfers between devices  2.46 us (5%)
  between operations  0.74 us (2%)
    all_to_all x1, blocking collectives, body(): lax.all_to_all(send, 'grp', 0, 0, tiled=True, axis_index_groups=lines(gro...  14.5 us
    ppermute x3, starting transfers between devices, swap(): return lax.ppermute(x, 'seq', [(i, i ^ bit) for i in range(shards)])  7.11 us
    pallas_call x2, Pallas kernels, inside(): pl.pallas_call(functools.partial(inside_kernel, first, heads, block), in_...  6.57 us
    pallas_call x1, Pallas kernels, body(): pl.pallas_call(functools.partial(give_kernel, chunk), in_specs=[HBM] * 2,...  2.76 us
    ppermute x3, starting transfers between devices, on_x(): return lax.ppermute(x, 'seq', [(i, place(i)) for i in range(shards)])  2.75 us
    pallas_call x1, Pallas kernels, body(): pl.pallas_call(functools.partial(norm_kernel, heads, float(width * groups...  2.24 us
    ppermute x1, starting transfers between devices, body(): beside = lax.ppermute(own, 'grp', [(g, g ^ 1) for g in range(groups)])  2.16 us
    pallas_call x1, Pallas kernels, body(): pl.pallas_call(functools.partial(gate_kernel, block), in_specs=[VMEM, VME...  2.04 us
  transfers between devices with their start and end apart: 7, of which 4 were waited for; matrix products, arithmetic and copies ran while one was open for 0% of the time, Pallas kernels for 23%

profile of v6, /device:TPU:1, one launch (start us, length us, event | category | flops | bytes accessed | tf_op | source)
XLA Modules:
  0.0 46.8 jit_solution(8182617861460469062)
XLA Ops:
  0.6 2.8 %give.1 = (bf16[2048,512]{1,0:T(8,128)(2,1)S(1)}, bf16[2048,512]{1,0:T(8,128)(2,1)S(1)}, bf16[2048,256]{1,0:T(8,128)(2,1)S(1)}, bf16[2048,256]{1,0:T(8,128)(2,1)...) custom-call(bf16[2048,512]{1,0:T(8,128)(2,1)} %k_hbm.1, bf16[2048,512]{1,0:T(8,128)(2,1)} %v_hbm.1), custom_call_target="tpu_custom_call" | custom-call | flops 134217728 | bytes 6291456 | tf_op jit(solution)/shard_map/give/pallas_call | solution.py:337
  3.4 3.3 %collective-permute-start = (f32[2,128,128]{2,1,0:T(8,128)S(1)}, f32[2,128,128]{2,1,0:T(8,128)S(1)}, u32[]{:S(2)}, u32[]{:S(2)}) collective-permute-start(f32[2,128,128]{2,1,0:T(8,128)S(1)} %get-tuple-element.52), channel_id=1, source_target_pairs={{0,16},{16,0},{32,48},{48,32},{64,80},{80,64},{96,112},{112,96},{1... | collective-permute-start | bytes 393224 | tf_op jit(solution)/shard_map/ppermute | solution.py:349
  6.7 1.7 %mine.1 = (bf16[2048,256]{1,0:T(8,128)(2,1)S(1)}, bf16[2048,256]{1,0:T(8,128)(2,1)S(1)}, f32[2,128,128]{2,1,0:T(8,128)S(1)}, f32[4,2,128,128]{3,2,1,0:T(8,128)S(...) custom-call(bf16[2048,512]{1,0:T(8,128)(2,1)S(1)} %get-tuple-element.53.k_in, ...), custom_call_target="tpu_custom_call" | custom-call | flops 134217728 | bytes 3145728 | tf_op jit(solution)/shard_map/mine/pallas_call | solution.py:373
  8.4 0.0 collective-permute-done.other_ref
  8.4 0.1 collective-permute-start.3
  8.5 2.7 %collective-permute-start.2 = (f32[2,128,128]{2,1,0:T(8,128)S(1)}, f32[2,128,128]{2,1,0:T(8,128)S(1)}, u32[]{:S(2)}, u32[]{:S(2)}) collective-permute-start(f32[2,128,128]{2,1,0:T(8,128)S(1)} %pair.1.own_ref), channel_id=1, source_target_pairs={{0,96},{16,112},{32,0},{48,16},{64,32},{80,48},{96,64},{112,80},{1... | collective-permute-start | bytes 393224 | tf_op jit(solution)/shard_map/ppermute | solution.py:353
  11.2 0.0 collective-permute-start.1
  11.2 5.0 %inside0.1 = (f32[1536,512]{1,0:T(8,128)S(1)}, bf16[1536,512]{1,0:T(8,128)(2,1)S(1)}) custom-call(bf16[2048,512]{1,0:T(8,128)(2,1)S(1)} %get-tuple-element.56.q_ref, bf16[2048,256]{1,0:T(8,128)(2,1)S(1)} %get-tuple-element.78.ka0_ref, bf16[2048,256]{1,0:T(8,128)(2,1)S(1)} %get-tuple-element.79.va0_ref, f32[4,2,128,128]{3,2,1,0:T(8,128)S(1)} %get-tuple-element.80.runs0_ref, ...), custom_call_target="tpu_custom_call" | custom-call | flops 1409286144 | bytes 9437184 | tf_op jit(solution)/shard_map/inside0/pallas_call | solution.py:357
  16.2 0.0 collective-permute-done.3.refs_2_
  16.2 0.3 collective-permute-done.2.refs_1_
  16.5 0.7 %collective-permute-done.1.refs_0_ = f32[2,128,128]{2,1,0:T(8,128)S(1)} collective-permute-done((f32[2,128,128]{2,1,0:T(8,128)S(1)}, f32[2,128,128]{2,1,0:T(8,128)S(1)}, u32[]{:S(2)}, u32[]{:S(2)}) %collective-permute-start.1) | collective-permute-done | bytes 131104 | tf_op jit(solution)/shard_map/ppermute | solution.py:353
  17.2 1.1 %collective-permute-start.4 = (f32[2,128,128]{2,1,0:T(8,128)S(1)}, f32[2,128,128]{2,1,0:T(8,128)S(1)}, u32[]{:S(2)}, u32[]{:S(2)}) collective-permute-start(f32[2,128,128]{2,1,0:T(8,128)S(1)} %get-tuple-element.77.all_ref), channel_id=1, source_target_pairs={{0,128},{16,144},{32,160},{48,176},{64,192},{80,208},{96,224},{112... | collective-permute-start | bytes 393224 | tf_op jit(solution)/shard_map/ppermute | solution.py:349
  18.3 1.6 %inside6.1 = (f32[512,512]{1,0:T(8,128)S(1)}, bf16[512,512]{1,0:T(8,128)(2,1)S(1)}) custom-call(bf16[2048,512]{1,0:T(8,128)(2,1)S(1)} %get-tuple-element.56.q_ref, bf16[2048,256]{1,0:T(8,128)(2,1)S(1)} %get-tuple-element.78.ka0_ref, bf16[2048,256]{1,0:T(8,128)(2,1)S(1)} %get-tuple-element.79.va0_ref, f32[4,2,128,128]{3,2,1,0:T(8,128)S(1)} %get-tuple-element.80.runs0_ref, ...), custom_call_target="tpu_custom_call" | custom-call | flops 469762048 | bytes 3145728 | tf_op jit(solution)/shard_map/inside6/pallas_call | solution.py:357
  19.9 1.2 %collective-permute-done.4.over_ref = f32[2,128,128]{2,1,0:T(8,128)S(1)} collective-permute-done((f32[2,128,128]{2,1,0:T(8,128)S(1)}, f32[2,128,128]{2,1,0:T(8,128)S(1)}, u32[]{:S(2)}, u32[]{:S(2)}) %collective-permute-start.4) | collective-permute-done | bytes 131104 | tf_op jit(solution)/shard_map/ppermute | solution.py:349
  21.2 2.7 %collective-permute-start.5 = (f32[2,136,128]{2,1,0:T(8,128)S(1)}, f32[2,136,128]{2,1,0:T(8,128)S(1)}, u32[]{:S(2)}, u32[]{:S(2)}) collective-permute-start(f32[2,136,128]{2,1,0:T(8,128)S(1)} %get-tuple-element.92), channel_id=1, source_target_pairs={{0,16},{16,0},{32,48},{48,32},{64,80},{80,64},{96,112},{112,96},{1... | collective-permute-start | bytes 417800 | tf_op jit(solution)/shard_map/ppermute | solution.py:349
  23.9 0.7 %carry_own.1 = (f32[2048,256]{1,0:T(8,128)S(1)}, f32[2048,128]{1,0:T(8,128)S(1)}) custom-call(f32[1536,512]{1,0:T(8,128)S(1)} %get-tuple-element.73.base0_ref, f32[512,512]{1,0:T(8,128)S(1)} %get-tuple-element.85.base1_ref, bf16[1536,512]{1,0:T(8,128)(2,1)S(1)} %get-tuple-element.86.qa0_ref, bf16[512,512]{1,0:T(8,128)(2,1)S(1)} %get-tuple-element.87.qa1_ref, ...), custom_call_target="tpu_custom_call" | custom-call | flops 268435456 | bytes 5242880 | tf_op jit(solution)/shard_map/carry_own/pallas_call | solution.py:412
  24.6 0.3 collective-permute-done.5.got_ref
  24.9 0.0 copy-start
  24.9 0.9 %carry_rest.1 = (f32[2048,256]{1,0:T(8,128)S(1)}, f32[48,128]{1,0:T(8,128)S(1)}) custom-call(f32[1536,512]{1,0:T(8,128)S(1)} %get-tuple-element.73.base0_ref, f32[512,512]{1,0:T(8,128)S(1)} %get-tuple-element.85.base1_ref, bf16[1536,512]{1,0:T(8,128)(2,1)S(1)} %get-tuple-element.86.qa0_ref, bf16[512,512]{1,0:T(8,128)(2,1)S(1)} %get-tuple-element.87.qa1_ref, ...), custom_call_target="tpu_custom_call" | custom-call | flops 268435456 | bytes 5242880 | tf_op jit(solution)/shard_map/carry_rest/pallas_call | solution.py:423
  25.8 2.2 %collective-permute-start.6 = (f32[48,128]{1,0:T(8,128)S(1)}, f32[48,128]{1,0:T(8,128)S(1)}, u32[]{:S(2)}, u32[]{:S(2)}) collective-permute-start(f32[48,128]{1,0:T(8,128)S(1)} %get-tuple-element.95.mine_ref), channel_id=1, source_target_pairs={{0,1},{1,0},{2,3},{3,2},{4,5},{5,4},{6,7},{7,6},{8,9},{9,8},{10,11... | collective-permute-start | bytes 73736 | tf_op jit(solution)/shard_map/ppermute | solution.py:434
  27.9 0.0 copy-done
  27.9 2.0 %gate.1.gated_ref = f32[2048,512]{1,0:T(8,128)S(1)} custom-call(f32[2048,256]{1,0:T(8,128)S(1)} %get-tuple-element.96.own_ref, f32[2048,256]{1,0:T(8,128)S(1)} %get-tuple-element.97.rest_ref, bf16[2048,512]{1,0:T(8,128)(2,1)} %gate_hbm.1, f32[1,512]{1,0:T(1,128)S(1)} %bitcast.1), custom_call_target="tpu_custom_call" | custom-call | flops 4194304 | bytes 10485760 | tf_op jit(solution)/shard_map/gate/pallas_call | solution.py:435
  30.0 0.0 collective-permute-done.6.other_ref
  30.0 14.5 %all_to_all.5.got_ref = f32[8,48,128]{2,1,0:T(8,128)S(1)} all-to-all(f32[8,48,128]{2,1,0:T(8,128)S(1)} %pack.1), channel_id=1, replica_groups={{12,10,8,14,6,4,2,0},{13,11,9,15,7,5,3,1},{28,26,24,30,22,20,18,16},{29..., dimensions={0} | all-to-all | bytes 393216 | tf_op jit(solution)/shard_map/all_to_all | solution.py:455
  44.5 2.2 %norm.1 = (bf16[2048,512]{1,0:T(8,128)(2,1)}, f32[4,8,128]{2,1,0:T(8,128)}) custom-call(f32[8,48,128]{2,1,0:T(8,128)S(1)} %all_to_all.5.got_ref, f32[2048,512]{1,0:T(8,128)S(1)} %gate.1.gated_ref), custom_call_target="tpu_custom_call" | custom-call | flops 2097152 | bytes 6291456 | tf_op jit(solution)/shard_map/norm/pallas_call | solution.py:459
  (4 shorter events, 0.1 us)
Async XLA Ops:
  3.4 5.0 %collective-permute-start = (f32[2,128,128]{2,1,0:T(8,128)S(1)}, f32[2,128,128]{2,1,0:T(8,128)S(1)}, u32[]{:S(2)}, u32[]{:S(2)}) collective-permute-start(f32[2,128,128]{2,1,0:T(8,128)S(1)} %get-tuple-element.52), channel_id=1, source_target_pairs={{0,16},{16,0},{32,48},{48,32},{64,80},{80,64},{96,112},{112,96},{1... | collective-permute-start | bytes 393224 | tf_op jit(solution)/shard_map/ppermute | solution.py:349
  8.4 7.7 %collective-permute-start.3 = (f32[2,128,128]{2,1,0:T(8,128)S(1)}, f32[2,128,128]{2,1,0:T(8,128)S(1)}, u32[]{:S(2)}, u32[]{:S(2)}) collective-permute-start(f32[2,128,128]{2,1,0:T(8,128)S(1)} %pair.1.own_ref), channel_id=1, source_target_pairs={{0,32},{16,48},{32,64},{48,80},{64,96},{80,112},{96,0},{112,16},{1... | collective-permute-start | bytes 393224 | tf_op jit(solution)/shard_map/ppermute | solution.py:353
  8.5 7.9 %collective-permute-start.2 = (f32[2,128,128]{2,1,0:T(8,128)S(1)}, f32[2,128,128]{2,1,0:T(8,128)S(1)}, u32[]{:S(2)}, u32[]{:S(2)}) collective-permute-start(f32[2,128,128]{2,1,0:T(8,128)S(1)} %pair.1.own_ref), channel_id=1, source_target_pairs={{0,96},{16,112},{32,0},{48,16},{64,32},{80,48},{96,64},{112,80},{1... | collective-permute-start | bytes 393224 | tf_op jit(solution)/shard_map/ppermute | solution.py:353
  11.2 6.0 %collective-permute-start.1 = (f32[2,128,128]{2,1,0:T(8,128)S(1)}, f32[2,128,128]{2,1,0:T(8,128)S(1)}, u32[]{:S(2)}, u32[]{:S(2)}) collective-permute-start(f32[2,128,128]{2,1,0:T(8,128)S(1)} %pair.1.own_ref), channel_id=1, source_target_pairs={{0,64},{16,80},{32,96},{48,112},{64,0},{80,16},{96,32},{112,48},{1... | collective-permute-start | bytes 393224 | tf_op jit(solution)/shard_map/ppermute | solution.py:353
  17.2 3.9 %collective-permute-start.4 = (f32[2,128,128]{2,1,0:T(8,128)S(1)}, f32[2,128,128]{2,1,0:T(8,128)S(1)}, u32[]{:S(2)}, u32[]{:S(2)}) collective-permute-start(f32[2,128,128]{2,1,0:T(8,128)S(1)} %get-tuple-element.77.all_ref), channel_id=1, source_target_pairs={{0,128},{16,144},{32,160},{48,176},{64,192},{80,208},{96,224},{112... | collective-permute-start | bytes 393224 | tf_op jit(solution)/shard_map/ppermute | solution.py:349
  21.2 3.7 %collective-permute-start.5 = (f32[2,136,128]{2,1,0:T(8,128)S(1)}, f32[2,136,128]{2,1,0:T(8,128)S(1)}, u32[]{:S(2)}, u32[]{:S(2)}) collective-permute-start(f32[2,136,128]{2,1,0:T(8,128)S(1)} %get-tuple-element.92), channel_id=1, source_target_pairs={{0,16},{16,0},{32,48},{48,32},{64,80},{80,64},{96,112},{112,96},{1... | collective-permute-start | bytes 417800 | tf_op jit(solution)/shard_map/ppermute | solution.py:349
  24.9 3.1 %copy-start = (f32[512]{0:T(512)S(1)}, f32[512]{0:T(512)}, u32[]{:S(2)}) copy-start(f32[512]{0:T(512)} %param.10) | copy-start | bytes 6148
  25.8 4.2 %collective-permute-start.6 = (f32[48,128]{1,0:T(8,128)S(1)}, f32[48,128]{1,0:T(8,128)S(1)}, u32[]{:S(2)}, u32[]{:S(2)}) collective-permute-start(f32[48,128]{1,0:T(8,128)S(1)} %get-tuple-element.95.mine_ref), channel_id=1, source_target_pairs={{0,1},{1,0},{2,3},{3,2},{4,5},{5,4},{6,7},{7,6},{8,9},{9,8},{10,11... | collective-permute-start | bytes 73736 | tf_op jit(solution)/shard_map/ppermute | solution.py:434

commit v7 on v6

--- a/solution.py
+++ b/solution.py
@@ -290,17 +290,23 @@
             )
 
 
-def norm_kernel(heads, features, block, got_ref, gated_ref, out_hbm, state_ref, out, scales, sems):
+def norm_kernel(
+    heads, features, block, got_ref, gated_ref, out_hbm, state_hbm, out, scales, final, sems, state_sem
+):
     total = got_ref[0]
     for place in range(1, got_ref.shape[0]):
         total = total + got_ref[place]
-    rows = state_ref.shape[1]
+    rows = final.shape[1]
     tokens = out.shape[0]
     token_rows = tokens // DH
     scales[...] = jnp.zeros_like(scales)
     scales[:token_rows] = lax.rsqrt(total[:token_rows] / features + 1e-6)
     columns = jnp.transpose(scales[...])
-    copies = []
+    for h in range(heads):
+        at = token_rows + h * rows
+        final[h] = total[at : at + rows]
+    copies = [pltpu.make_async_copy(final, state_hbm, state_sem)]
+    copies[0].start()
     for n in range(tokens // block):
         for c in range(n * block // DH, (n + 1) * block // DH):
             part = slice(c * DH, (c + 1) * DH)
@@ -308,9 +314,6 @@
         part = pl.ds(n * block, block)
         copies.append(pltpu.make_async_copy(out.at[part], out_hbm.at[part], sems.at[n]))
         copies[-1].start()
-    for h in range(heads):
-        at = token_rows + h * rows
-        state_ref[h] = total[at : at + rows]
     for copy in copies:
         copy.wait()
 
@@ -459,7 +462,7 @@
     attn_out, decode_state = pl.pallas_call(
         functools.partial(norm_kernel, heads, float(width * groups), block),
         in_specs=[VMEM, VMEM],
-        out_specs=[HBM, VMEM],
+        out_specs=[HBM, HBM],
         out_shape=[
             jax.ShapeDtypeStruct((tokens, width), BF16),
             jax.ShapeDtypeStruct((heads, rows, DH), F32),
@@ -467,7 +470,9 @@
         scratch_shapes=[
             pltpu.VMEM((tokens, width), BF16),
             pltpu.VMEM((DH, DH), F32),
+            pltpu.VMEM((heads, rows, DH), F32),
             dma(count),
+            pltpu.SemaphoreType.DMA,
         ],
         compiler_params=limit,
         cost_estimate=cost(2 * tokens * width, 6 * tokens * width),

time: 46.9 us -> 46.3 us (0.987)
  Pallas kernels: 17 us -> 16.4 us
    pallas_call x1, Pallas kernels: 2.24 us -> 1.65 us  [body(): pl.pallas_call(functools.partial(norm_kernel, heads, float(width * groups...]
  transfers between devices with their start and end apart: 7 -> 7, of which waited for: 4 -> 4; matrix products, arithmetic and copies ran while one was open for 0% -> 0% of each run, Pallas kernels for 23% -> 24%
where the time goes in v7:
time: 46.3 us; the launch traced here: 46.2 us
  Pallas kernels  16.4 us (35%)
  blocking collectives  14.5 us (31%)
  starting transfers between devices  12 us (26%)
  waiting for transfers between devices  2.46 us (5%)
  between operations  0.74 us (2%)
    all_to_all x1, blocking collectives, body(): lax.all_to_all(send, 'grp', 0, 0, tiled=True, axis_index_groups=lines(gro...  14.5 us
    ppermute x3, starting transfers between devices, swap(): return lax.ppermute(x, 'seq', [(i, i ^ bit) for i in range(shards)])  7.11 us
    pallas_call x2, Pallas kernels, inside(): pl.pallas_call(functools.partial(inside_kernel, first, heads, block), in_...  6.57 us
    pallas_call x1, Pallas kernels, body(): pl.pallas_call(functools.partial(give_kernel, chunk), in_specs=[HBM] * 2,...  2.76 us
    ppermute x3, starting transfers between devices, on_x(): return lax.ppermute(x, 'seq', [(i, place(i)) for i in range(shards)])  2.75 us
    ppermute x1, starting transfers between devices, body(): beside = lax.ppermute(own, 'grp', [(g, g ^ 1) for g in range(groups)])  2.16 us
    pallas_call x1, Pallas kernels, body(): pl.pallas_call(functools.partial(gate_kernel, block), in_specs=[VMEM, VME...  2.04 us
    pallas_call x1, Pallas kernels, body(): pl.pallas_call(functools.partial(mine_kernel, chunk), in_specs=[VMEM, VME...  1.67 us
  transfers between devices with their start and end apart: 7, of which 4 were waited for; matrix products, arithmetic and copies ran while one was open for 0% of the time, Pallas kernels for 24%

profile of v7, /device:TPU:1, one launch (start us, length us, event | category | flops | bytes accessed | tf_op | source)
XLA Modules:
  0.0 46.2 jit_solution(12255296839990147693)
XLA Ops:
  0.6 2.8 %give.1 = (bf16[2048,512]{1,0:T(8,128)(2,1)S(1)}, bf16[2048,512]{1,0:T(8,128)(2,1)S(1)}, bf16[2048,256]{1,0:T(8,128)(2,1)S(1)}, bf16[2048,256]{1,0:T(8,128)(2,1)...) custom-call(bf16[2048,512]{1,0:T(8,128)(2,1)} %k_hbm.1, bf16[2048,512]{1,0:T(8,128)(2,1)} %v_hbm.1), custom_call_target="tpu_custom_call" | custom-call | flops 134217728 | bytes 6291456 | tf_op jit(solution)/shard_map/give/pallas_call | solution.py:340
  3.4 3.3 %collective-permute-start = (f32[2,128,128]{2,1,0:T(8,128)S(1)}, f32[2,128,128]{2,1,0:T(8,128)S(1)}, u32[]{:S(2)}, u32[]{:S(2)}) collective-permute-start(f32[2,128,128]{2,1,0:T(8,128)S(1)} %get-tuple-element.52), channel_id=1, source_target_pairs={{0,16},{16,0},{32,48},{48,32},{64,80},{80,64},{96,112},{112,96},{1... | collective-permute-start | bytes 393224 | tf_op jit(solution)/shard_map/ppermute | solution.py:352
  6.7 1.7 %mine.1 = (bf16[2048,256]{1,0:T(8,128)(2,1)S(1)}, bf16[2048,256]{1,0:T(8,128)(2,1)S(1)}, f32[2,128,128]{2,1,0:T(8,128)S(1)}, f32[4,2,128,128]{3,2,1,0:T(8,128)S(...) custom-call(bf16[2048,512]{1,0:T(8,128)(2,1)S(1)} %get-tuple-element.53.k_in, ...), custom_call_target="tpu_custom_call" | custom-call | flops 134217728 | bytes 3145728 | tf_op jit(solution)/shard_map/mine/pallas_call | solution.py:376
  8.4 0.0 collective-permute-done.other_ref
  8.4 0.1 collective-permute-start.3
  8.5 2.7 %collective-permute-start.2 = (f32[2,128,128]{2,1,0:T(8,128)S(1)}, f32[2,128,128]{2,1,0:T(8,128)S(1)}, u32[]{:S(2)}, u32[]{:S(2)}) collective-permute-start(f32[2,128,128]{2,1,0:T(8,128)S(1)} %pair.1.own_ref), channel_id=1, source_target_pairs={{0,96},{16,112},{32,0},{48,16},{64,32},{80,48},{96,64},{112,80},{1... | collective-permute-start | bytes 393224 | tf_op jit(solution)/shard_map/ppermute | solution.py:356
  11.2 0.0 collective-permute-start.1
  11.2 5.0 %inside0.1 = (f32[1536,512]{1,0:T(8,128)S(1)}, bf16[1536,512]{1,0:T(8,128)(2,1)S(1)}) custom-call(bf16[2048,512]{1,0:T(8,128)(2,1)S(1)} %get-tuple-element.56.q_ref, bf16[2048,256]{1,0:T(8,128)(2,1)S(1)} %get-tuple-element.78.ka0_ref, bf16[2048,256]{1,0:T(8,128)(2,1)S(1)} %get-tuple-element.79.va0_ref, f32[4,2,128,128]{3,2,1,0:T(8,128)S(1)} %get-tuple-element.80.runs0_ref, ...), custom_call_target="tpu_custom_call" | custom-call | flops 1409286144 | bytes 9437184 | tf_op jit(solution)/shard_map/inside0/pallas_call | solution.py:360
  16.2 0.0 collective-permute-done.3.refs_2_
  16.2 0.3 collective-permute-done.2.refs_1_
  16.5 0.7 %collective-permute-done.1.refs_0_ = f32[2,128,128]{2,1,0:T(8,128)S(1)} collective-permute-done((f32[2,128,128]{2,1,0:T(8,128)S(1)}, f32[2,128,128]{2,1,0:T(8,128)S(1)}, u32[]{:S(2)}, u32[]{:S(2)}) %collective-permute-start.1) | collective-permute-done | bytes 131104 | tf_op jit(solution)/shard_map/ppermute | solution.py:356
  17.2 1.1 %collective-permute-start.4 = (f32[2,128,128]{2,1,0:T(8,128)S(1)}, f32[2,128,128]{2,1,0:T(8,128)S(1)}, u32[]{:S(2)}, u32[]{:S(2)}) collective-permute-start(f32[2,128,128]{2,1,0:T(8,128)S(1)} %get-tuple-element.77.all_ref), channel_id=1, source_target_pairs={{0,128},{16,144},{32,160},{48,176},{64,192},{80,208},{96,224},{112... | collective-permute-start | bytes 393224 | tf_op jit(solution)/shard_map/ppermute | solution.py:352
  18.3 1.6 %inside6.1 = (f32[512,512]{1,0:T(8,128)S(1)}, bf16[512,512]{1,0:T(8,128)(2,1)S(1)}) custom-call(bf16[2048,512]{1,0:T(8,128)(2,1)S(1)} %get-tuple-element.56.q_ref, bf16[2048,256]{1,0:T(8,128)(2,1)S(1)} %get-tuple-element.78.ka0_ref, bf16[2048,256]{1,0:T(8,128)(2,1)S(1)} %get-tuple-element.79.va0_ref, f32[4,2,128,128]{3,2,1,0:T(8,128)S(1)} %get-tuple-element.80.runs0_ref, ...), custom_call_target="tpu_custom_call" | custom-call | flops 469762048 | bytes 3145728 | tf_op jit(solution)/shard_map/inside6/pallas_call | solution.py:360
  19.9 1.2 %collective-permute-done.4.over_ref = f32[2,128,128]{2,1,0:T(8,128)S(1)} collective-permute-done((f32[2,128,128]{2,1,0:T(8,128)S(1)}, f32[2,128,128]{2,1,0:T(8,128)S(1)}, u32[]{:S(2)}, u32[]{:S(2)}) %collective-permute-start.4) | collective-permute-done | bytes 131104 | tf_op jit(solution)/shard_map/ppermute | solution.py:352
  21.2 2.7 %collective-permute-start.5 = (f32[2,136,128]{2,1,0:T(8,128)S(1)}, f32[2,136,128]{2,1,0:T(8,128)S(1)}, u32[]{:S(2)}, u32[]{:S(2)}) collective-permute-start(f32[2,136,128]{2,1,0:T(8,128)S(1)} %get-tuple-element.92), channel_id=1, source_target_pairs={{0,16},{16,0},{32,48},{48,32},{64,80},{80,64},{96,112},{112,96},{1... | collective-permute-start | bytes 417800 | tf_op jit(solution)/shard_map/ppermute | solution.py:352
  23.9 0.7 %carry_own.1 = (f32[2048,256]{1,0:T(8,128)S(1)}, f32[2048,128]{1,0:T(8,128)S(1)}) custom-call(f32[1536,512]{1,0:T(8,128)S(1)} %get-tuple-element.73.base0_ref, f32[512,512]{1,0:T(8,128)S(1)} %get-tuple-element.85.base1_ref, bf16[1536,512]{1,0:T(8,128)(2,1)S(1)} %get-tuple-element.86.qa0_ref, bf16[512,512]{1,0:T(8,128)(2,1)S(1)} %get-tuple-element.87.qa1_ref, ...), custom_call_target="tpu_custom_call" | custom-call | flops 268435456 | bytes 5242880 | tf_op jit(solution)/shard_map/carry_own/pallas_call | solution.py:415
  24.6 0.3 collective-permute-done.5.got_ref
  24.9 0.0 copy-start
  24.9 0.9 %carry_rest.1 = (f32[2048,256]{1,0:T(8,128)S(1)}, f32[48,128]{1,0:T(8,128)S(1)}) custom-call(f32[1536,512]{1,0:T(8,128)S(1)} %get-tuple-element.73.base0_ref, f32[512,512]{1,0:T(8,128)S(1)} %get-tuple-element.85.base1_ref, bf16[1536,512]{1,0:T(8,128)(2,1)S(1)} %get-tuple-element.86.qa0_ref, bf16[512,512]{1,0:T(8,128)(2,1)S(1)} %get-tuple-element.87.qa1_ref, ...), custom_call_target="tpu_custom_call" | custom-call | flops 268435456 | bytes 5242880 | tf_op jit(solution)/shard_map/carry_rest/pallas_call | solution.py:426
  25.8 2.2 %collective-permute-start.6 = (f32[48,128]{1,0:T(8,128)S(1)}, f32[48,128]{1,0:T(8,128)S(1)}, u32[]{:S(2)}, u32[]{:S(2)}) collective-permute-start(f32[48,128]{1,0:T(8,128)S(1)} %get-tuple-element.95.mine_ref), channel_id=1, source_target_pairs={{0,1},{1,0},{2,3},{3,2},{4,5},{5,4},{6,7},{7,6},{8,9},{9,8},{10,11... | collective-permute-start | bytes 73736 | tf_op jit(solution)/shard_map/ppermute | solution.py:437
  27.9 0.0 copy-done
  27.9 2.0 %gate.1.gated_ref = f32[2048,512]{1,0:T(8,128)S(1)} custom-call(f32[2048,256]{1,0:T(8,128)S(1)} %get-tuple-element.96.own_ref, f32[2048,256]{1,0:T(8,128)S(1)} %get-tuple-element.97.rest_ref, bf16[2048,512]{1,0:T(8,128)(2,1)} %gate_hbm.1, f32[1,512]{1,0:T(1,128)S(1)} %bitcast.1), custom_call_target="tpu_custom_call" | custom-call | flops 4194304 | bytes 10485760 | tf_op jit(solution)/shard_map/gate/pallas_call | solution.py:438
  30.0 0.0 collective-permute-done.6.other_ref
  30.0 14.5 %all_to_all.5.got_ref = f32[8,48,128]{2,1,0:T(8,128)S(1)} all-to-all(f32[8,48,128]{2,1,0:T(8,128)S(1)} %pack.1), channel_id=1, replica_groups={{12,10,8,14,6,4,2,0},{13,11,9,15,7,5,3,1},{28,26,24,30,22,20,18,16},{29..., dimensions={0} | all-to-all | bytes 393216 | tf_op jit(solution)/shard_map/all_to_all | solution.py:458
  44.5 1.7 %norm.1 = (bf16[2048,512]{1,0:T(8,128)(2,1)}, f32[4,8,128]{2,1,0:T(8,128)}) custom-call(f32[8,48,128]{2,1,0:T(8,128)S(1)} %all_to_all.5.got_ref, f32[2048,512]{1,0:T(8,128)S(1)} %gate.1.gated_ref), custom_call_target="tpu_custom_call" | custom-call | flops 2097152 | bytes 6291456 | tf_op jit(solution)/shard_map/norm/pallas_call | solution.py:462
  (4 shorter events, 0.1 us)
Async XLA Ops:
  3.4 5.0 %collective-permute-start = (f32[2,128,128]{2,1,0:T(8,128)S(1)}, f32[2,128,128]{2,1,0:T(8,128)S(1)}, u32[]{:S(2)}, u32[]{:S(2)}) collective-permute-start(f32[2,128,128]{2,1,0:T(8,128)S(1)} %get-tuple-element.52), channel_id=1, source_target_pairs={{0,16},{16,0},{32,48},{48,32},{64,80},{80,64},{96,112},{112,96},{1... | collective-permute-start | bytes 393224 | tf_op jit(solution)/shard_map/ppermute | solution.py:352
  8.4 7.7 %collective-permute-start.3 = (f32[2,128,128]{2,1,0:T(8,128)S(1)}, f32[2,128,128]{2,1,0:T(8,128)S(1)}, u32[]{:S(2)}, u32[]{:S(2)}) collective-permute-start(f32[2,128,128]{2,1,0:T(8,128)S(1)} %pair.1.own_ref), channel_id=1, source_target_pairs={{0,32},{16,48},{32,64},{48,80},{64,96},{80,112},{96,0},{112,16},{1... | collective-permute-start | bytes 393224 | tf_op jit(solution)/shard_map/ppermute | solution.py:356
  8.5 7.9 %collective-permute-start.2 = (f32[2,128,128]{2,1,0:T(8,128)S(1)}, f32[2,128,128]{2,1,0:T(8,128)S(1)}, u32[]{:S(2)}, u32[]{:S(2)}) collective-permute-start(f32[2,128,128]{2,1,0:T(8,128)S(1)} %pair.1.own_ref), channel_id=1, source_target_pairs={{0,96},{16,112},{32,0},{48,16},{64,32},{80,48},{96,64},{112,80},{1... | collective-permute-start | bytes 393224 | tf_op jit(solution)/shard_map/ppermute | solution.py:356
  11.2 6.0 %collective-permute-start.1 = (f32[2,128,128]{2,1,0:T(8,128)S(1)}, f32[2,128,128]{2,1,0:T(8,128)S(1)}, u32[]{:S(2)}, u32[]{:S(2)}) collective-permute-start(f32[2,128,128]{2,1,0:T(8,128)S(1)} %pair.1.own_ref), channel_id=1, source_target_pairs={{0,64},{16,80},{32,96},{48,112},{64,0},{80,16},{96,32},{112,48},{1... | collective-permute-start | bytes 393224 | tf_op jit(solution)/shard_map/ppermute | solution.py:356
  17.2 3.9 %collective-permute-start.4 = (f32[2,128,128]{2,1,0:T(8,128)S(1)}, f32[2,128,128]{2,1,0:T(8,128)S(1)}, u32[]{:S(2)}, u32[]{:S(2)}) collective-permute-start(f32[2,128,128]{2,1,0:T(8,128)S(1)} %get-tuple-element.77.all_ref), channel_id=1, source_target_pairs={{0,128},{16,144},{32,160},{48,176},{64,192},{80,208},{96,224},{112... | collective-permute-start | bytes 393224 | tf_op jit(solution)/shard_map/ppermute | solution.py:352
  21.2 3.7 %collective-permute-start.5 = (f32[2,136,128]{2,1,0:T(8,128)S(1)}, f32[2,136,128]{2,1,0:T(8,128)S(1)}, u32[]{:S(2)}, u32[]{:S(2)}) collective-permute-start(f32[2,136,128]{2,1,0:T(8,128)S(1)} %get-tuple-element.92), channel_id=1, source_target_pairs={{0,16},{16,0},{32,48},{48,32},{64,80},{80,64},{96,112},{112,96},{1... | collective-permute-start | bytes 417800 | tf_op jit(solution)/shard_map/ppermute | solution.py:352
  24.9 3.1 %copy-start = (f32[512]{0:T(512)S(1)}, f32[512]{0:T(512)}, u32[]{:S(2)}) copy-start(f32[512]{0:T(512)} %param.10) | copy-start | bytes 6148
  25.8 4.2 %collective-permute-start.6 = (f32[48,128]{1,0:T(8,128)S(1)}, f32[48,128]{1,0:T(8,128)S(1)}, u32[]{:S(2)}, u32[]{:S(2)}) collective-permute-start(f32[48,128]{1,0:T(8,128)S(1)} %get-tuple-element.95.mine_ref), channel_id=1, source_target_pairs={{0,1},{1,0},{2,3},{3,2},{4,5},{5,4},{6,7},{7,6},{8,9},{9,8},{10,11... | collective-permute-start | bytes 73736 | tf_op jit(solution)/shard_map/ppermute | solution.py:437

commit v8 on v7

--- a/solution.py
+++ b/solution.py
@@ -293,20 +293,16 @@
 def norm_kernel(
     heads, features, block, got_ref, gated_ref, out_hbm, state_hbm, out, scales, final, sems, state_sem
 ):
-    total = got_ref[0]
-    for place in range(1, got_ref.shape[0]):
-        total = total + got_ref[place]
     rows = final.shape[1]
     tokens = out.shape[0]
     token_rows = tokens // DH
+    total = got_ref[0, :token_rows]
+    for place in range(1, got_ref.shape[0]):
+        total = total + got_ref[place, :token_rows]
     scales[...] = jnp.zeros_like(scales)
-    scales[:token_rows] = lax.rsqrt(total[:token_rows] / features + 1e-6)
+    scales[:token_rows] = lax.rsqrt(total / features + 1e-6)
     columns = jnp.transpose(scales[...])
-    for h in range(heads):
-        at = token_rows + h * rows
-        final[h] = total[at : at + rows]
-    copies = [pltpu.make_async_copy(final, state_hbm, state_sem)]
-    copies[0].start()
+    copies = []
     for n in range(tokens // block):
         for c in range(n * block // DH, (n + 1) * block // DH):
             part = slice(c * DH, (c + 1) * DH)
@@ -314,6 +310,15 @@
         part = pl.ds(n * block, block)
         copies.append(pltpu.make_async_copy(out.at[part], out_hbm.at[part], sems.at[n]))
         copies[-1].start()
+        if n == 0:
+            for h in range(heads):
+                part = slice(token_rows + h * rows, token_rows + (h + 1) * rows)
+                rest = got_ref[0, part]
+                for place in range(1, got_ref.shape[0]):
+                    rest = rest + got_ref[place, part]
+                final[h] = rest
+            copies.append(pltpu.make_async_copy(final, state_hbm, state_sem))
+            copies[-1].start()
     for copy in copies:
         copy.wait()
 

time: 46.3 us -> 46.3 us (level)
  no operation moved by 1% of the time
where the time goes in v8:
time: 46.3 us; the launch traced here: 46.2 us
  Pallas kernels  16.4 us (35%)
  blocking collectives  14.5 us (31%)
  starting transfers between devices  12 us (26%)
  waiting for transfers between devices  2.46 us (5%)
  between operations  0.74 us (2%)
    all_to_all x1, blocking collectives, body(): lax.all_to_all(send, 'grp', 0, 0, tiled=True, axis_index_groups=lines(gro...  14.5 us
    ppermute x3, starting transfers between devices, swap(): return lax.ppermute(x, 'seq', [(i, i ^ bit) for i in range(shards)])  7.11 us
    pallas_call x2, Pallas kernels, inside(): pl.pallas_call(functools.partial(inside_kernel, first, heads, block), in_...  6.57 us
    pallas_call x1, Pallas kernels, body(): pl.pallas_call(functools.partial(give_kernel, chunk), in_specs=[HBM] * 2,...  2.76 us
    ppermute x3, starting transfers between devices, on_x(): return lax.ppermute(x, 'seq', [(i, place(i)) for i in range(shards)])  2.75 us
    ppermute x1, starting transfers between devices, body(): beside = lax.ppermute(own, 'grp', [(g, g ^ 1) for g in range(groups)])  2.16 us
    pallas_call x1, Pallas kernels, body(): pl.pallas_call(functools.partial(gate_kernel, block), in_specs=[VMEM, VME...  2.04 us
    pallas_call x1, Pallas kernels, body(): pl.pallas_call(functools.partial(mine_kernel, chunk), in_specs=[VMEM, VME...  1.67 us
  transfers between devices with their start and end apart: 7, of which 4 were waited for; matrix products, arithmetic and copies ran while one was open for 0% of the time, Pallas kernels for 24%

profile of v8, /device:TPU:1, one launch (start us, length us, event | category | flops | bytes accessed | tf_op | source)
XLA Modules:
  0.0 46.2 jit_solution(16818497069767860038)
XLA Ops:
  0.6 2.8 %give.1 = (bf16[2048,512]{1,0:T(8,128)(2,1)S(1)}, bf16[2048,512]{1,0:T(8,128)(2,1)S(1)}, bf16[2048,256]{1,0:T(8,128)(2,1)S(1)}, bf16[2048,256]{1,0:T(8,128)(2,1)...) custom-call(bf16[2048,512]{1,0:T(8,128)(2,1)} %k_hbm.1, bf16[2048,512]{1,0:T(8,128)(2,1)} %v_hbm.1), custom_call_target="tpu_custom_call" | custom-call | flops 134217728 | bytes 6291456 | tf_op jit(solution)/shard_map/give/pallas_call | solution.py:345
  3.4 3.3 %collective-permute-start = (f32[2,128,128]{2,1,0:T(8,128)S(1)}, f32[2,128,128]{2,1,0:T(8,128)S(1)}, u32[]{:S(2)}, u32[]{:S(2)}) collective-permute-start(f32[2,128,128]{2,1,0:T(8,128)S(1)} %get-tuple-element.52), channel_id=1, source_target_pairs={{0,16},{16,0},{32,48},{48,32},{64,80},{80,64},{96,112},{112,96},{1... | collective-permute-start | bytes 393224 | tf_op jit(solution)/shard_map/ppermute | solution.py:357
  6.7 1.7 %mine.1 = (bf16[2048,256]{1,0:T(8,128)(2,1)S(1)}, bf16[2048,256]{1,0:T(8,128)(2,1)S(1)}, f32[2,128,128]{2,1,0:T(8,128)S(1)}, f32[4,2,128,128]{3,2,1,0:T(8,128)S(...) custom-call(bf16[2048,512]{1,0:T(8,128)(2,1)S(1)} %get-tuple-element.53.k_in, ...), custom_call_target="tpu_custom_call" | custom-call | flops 134217728 | bytes 3145728 | tf_op jit(solution)/shard_map/mine/pallas_call | solution.py:381
  8.4 0.0 collective-permute-done.other_ref
  8.4 0.1 collective-permute-start.3
  8.5 2.7 %collective-permute-start.2 = (f32[2,128,128]{2,1,0:T(8,128)S(1)}, f32[2,128,128]{2,1,0:T(8,128)S(1)}, u32[]{:S(2)}, u32[]{:S(2)}) collective-permute-start(f32[2,128,128]{2,1,0:T(8,128)S(1)} %pair.1.own_ref), channel_id=1, source_target_pairs={{0,96},{16,112},{32,0},{48,16},{64,32},{80,48},{96,64},{112,80},{1... | collective-permute-start | bytes 393224 | tf_op jit(solution)/shard_map/ppermute | solution.py:361
  11.2 0.0 collective-permute-start.1
  11.2 5.0 %inside0.1 = (f32[1536,512]{1,0:T(8,128)S(1)}, bf16[1536,512]{1,0:T(8,128)(2,1)S(1)}) custom-call(bf16[2048,512]{1,0:T(8,128)(2,1)S(1)} %get-tuple-element.56.q_ref, bf16[2048,256]{1,0:T(8,128)(2,1)S(1)} %get-tuple-element.78.ka0_ref, bf16[2048,256]{1,0:T(8,128)(2,1)S(1)} %get-tuple-element.79.va0_ref, f32[4,2,128,128]{3,2,1,0:T(8,128)S(1)} %get-tuple-element.80.runs0_ref, ...), custom_call_target="tpu_custom_call" | custom-call | flops 1409286144 | bytes 9437184 | tf_op jit(solution)/shard_map/inside0/pallas_call | solution.py:365
  16.2 0.0 collective-permute-done.3.refs_2_
  16.2 0.3 collective-permute-done.2.refs_1_
  16.5 0.7 %collective-permute-done.1.refs_0_ = f32[2,128,128]{2,1,0:T(8,128)S(1)} collective-permute-done((f32[2,128,128]{2,1,0:T(8,128)S(1)}, f32[2,128,128]{2,1,0:T(8,128)S(1)}, u32[]{:S(2)}, u32[]{:S(2)}) %collective-permute-start.1) | collective-permute-done | bytes 131104 | tf_op jit(solution)/shard_map/ppermute | solution.py:361
  17.2 1.1 %collective-permute-start.4 = (f32[2,128,128]{2,1,0:T(8,128)S(1)}, f32[2,128,128]{2,1,0:T(8,128)S(1)}, u32[]{:S(2)}, u32[]{:S(2)}) collective-permute-start(f32[2,128,128]{2,1,0:T(8,128)S(1)} %get-tuple-element.77.all_ref), channel_id=1, source_target_pairs={{0,128},{16,144},{32,160},{48,176},{64,192},{80,208},{96,224},{112... | collective-permute-start | bytes 393224 | tf_op jit(solution)/shard_map/ppermute | solution.py:357
  18.3 1.6 %inside6.1 = (f32[512,512]{1,0:T(8,128)S(1)}, bf16[512,512]{1,0:T(8,128)(2,1)S(1)}) custom-call(bf16[2048,512]{1,0:T(8,128)(2,1)S(1)} %get-tuple-element.56.q_ref, bf16[2048,256]{1,0:T(8,128)(2,1)S(1)} %get-tuple-element.78.ka0_ref, bf16[2048,256]{1,0:T(8,128)(2,1)S(1)} %get-tuple-element.79.va0_ref, f32[4,2,128,128]{3,2,1,0:T(8,128)S(1)} %get-tuple-element.80.runs0_ref, ...), custom_call_target="tpu_custom_call" | custom-call | flops 469762048 | bytes 3145728 | tf_op jit(solution)/shard_map/inside6/pallas_call | solution.py:365
  19.9 1.2 %collective-permute-done.4.over_ref = f32[2,128,128]{2,1,0:T(8,128)S(1)} collective-permute-done((f32[2,128,128]{2,1,0:T(8,128)S(1)}, f32[2,128,128]{2,1,0:T(8,128)S(1)}, u32[]{:S(2)}, u32[]{:S(2)}) %collective-permute-start.4) | collective-permute-done | bytes 131104 | tf_op jit(solution)/shard_map/ppermute | solution.py:357
  21.2 2.7 %collective-permute-start.5 = (f32[2,136,128]{2,1,0:T(8,128)S(1)}, f32[2,136,128]{2,1,0:T(8,128)S(1)}, u32[]{:S(2)}, u32[]{:S(2)}) collective-permute-start(f32[2,136,128]{2,1,0:T(8,128)S(1)} %get-tuple-element.92), channel_id=1, source_target_pairs={{0,16},{16,0},{32,48},{48,32},{64,80},{80,64},{96,112},{112,96},{1... | collective-permute-start | bytes 417800 | tf_op jit(solution)/shard_map/ppermute | solution.py:357
  23.9 0.7 %carry_own.1 = (f32[2048,256]{1,0:T(8,128)S(1)}, f32[2048,128]{1,0:T(8,128)S(1)}) custom-call(f32[1536,512]{1,0:T(8,128)S(1)} %get-tuple-element.73.base0_ref, f32[512,512]{1,0:T(8,128)S(1)} %get-tuple-element.85.base1_ref, bf16[1536,512]{1,0:T(8,128)(2,1)S(1)} %get-tuple-element.86.qa0_ref, bf16[512,512]{1,0:T(8,128)(2,1)S(1)} %get-tuple-element.87.qa1_ref, ...), custom_call_target="tpu_custom_call" | custom-call | flops 268435456 | bytes 5242880 | tf_op jit(solution)/shard_map/carry_own/pallas_call | solution.py:420
  24.6 0.3 collective-permute-done.5.got_ref
  24.9 0.0 copy-start
  24.9 0.9 %carry_rest.1 = (f32[2048,256]{1,0:T(8,128)S(1)}, f32[48,128]{1,0:T(8,128)S(1)}) custom-call(f32[1536,512]{1,0:T(8,128)S(1)} %get-tuple-element.73.base0_ref, f32[512,512]{1,0:T(8,128)S(1)} %get-tuple-element.85.base1_ref, bf16[1536,512]{1,0:T(8,128)(2,1)S(1)} %get-tuple-element.86.qa0_ref, bf16[512,512]{1,0:T(8,128)(2,1)S(1)} %get-tuple-element.87.qa1_ref, ...), custom_call_target="tpu_custom_call" | custom-call | flops 268435456 | bytes 5242880 | tf_op jit(solution)/shard_map/carry_rest/pallas_call | solution.py:431
  25.8 2.2 %collective-permute-start.6 = (f32[48,128]{1,0:T(8,128)S(1)}, f32[48,128]{1,0:T(8,128)S(1)}, u32[]{:S(2)}, u32[]{:S(2)}) collective-permute-start(f32[48,128]{1,0:T(8,128)S(1)} %get-tuple-element.95.mine_ref), channel_id=1, source_target_pairs={{0,1},{1,0},{2,3},{3,2},{4,5},{5,4},{6,7},{7,6},{8,9},{9,8},{10,11... | collective-permute-start | bytes 73736 | tf_op jit(solution)/shard_map/ppermute | solution.py:442
  27.9 0.0 copy-done
  27.9 2.0 %gate.1.gated_ref = f32[2048,512]{1,0:T(8,128)S(1)} custom-call(f32[2048,256]{1,0:T(8,128)S(1)} %get-tuple-element.96.own_ref, f32[2048,256]{1,0:T(8,128)S(1)} %get-tuple-element.97.rest_ref, bf16[2048,512]{1,0:T(8,128)(2,1)} %gate_hbm.1, f32[1,512]{1,0:T(1,128)S(1)} %bitcast.1), custom_call_target="tpu_custom_call" | custom-call | flops 4194304 | bytes 10485760 | tf_op jit(solution)/shard_map/gate/pallas_call | solution.py:443
  30.0 0.0 collective-permute-done.6.other_ref
  30.0 14.5 %all_to_all.5.got_ref = f32[8,48,128]{2,1,0:T(8,128)S(1)} all-to-all(f32[8,48,128]{2,1,0:T(8,128)S(1)} %pack.1), channel_id=1, replica_groups={{12,10,8,14,6,4,2,0},{13,11,9,15,7,5,3,1},{28,26,24,30,22,20,18,16},{29..., dimensions={0} | all-to-all | bytes 393216 | tf_op jit(solution)/shard_map/all_to_all | solution.py:463
  44.5 1.7 %norm.1 = (bf16[2048,512]{1,0:T(8,128)(2,1)}, f32[4,8,128]{2,1,0:T(8,128)}) custom-call(f32[8,48,128]{2,1,0:T(8,128)S(1)} %all_to_all.5.got_ref, f32[2048,512]{1,0:T(8,128)S(1)} %gate.1.gated_ref), custom_call_target="tpu_custom_call" | custom-call | flops 2097152 | bytes 6291456 | tf_op jit(solution)/shard_map/norm/pallas_call | solution.py:467
  (4 shorter events, 0.1 us)
Async XLA Ops:
  3.4 5.0 %collective-permute-start = (f32[2,128,128]{2,1,0:T(8,128)S(1)}, f32[2,128,128]{2,1,0:T(8,128)S(1)}, u32[]{:S(2)}, u32[]{:S(2)}) collective-permute-start(f32[2,128,128]{2,1,0:T(8,128)S(1)} %get-tuple-element.52), channel_id=1, source_target_pairs={{0,16},{16,0},{32,48},{48,32},{64,80},{80,64},{96,112},{112,96},{1... | collective-permute-start | bytes 393224 | tf_op jit(solution)/shard_map/ppermute | solution.py:357
  8.4 7.7 %collective-permute-start.3 = (f32[2,128,128]{2,1,0:T(8,128)S(1)}, f32[2,128,128]{2,1,0:T(8,128)S(1)}, u32[]{:S(2)}, u32[]{:S(2)}) collective-permute-start(f32[2,128,128]{2,1,0:T(8,128)S(1)} %pair.1.own_ref), channel_id=1, source_target_pairs={{0,32},{16,48},{32,64},{48,80},{64,96},{80,112},{96,0},{112,16},{1... | collective-permute-start | bytes 393224 | tf_op jit(solution)/shard_map/ppermute | solution.py:361
  8.5 7.9 %collective-permute-start.2 = (f32[2,128,128]{2,1,0:T(8,128)S(1)}, f32[2,128,128]{2,1,0:T(8,128)S(1)}, u32[]{:S(2)}, u32[]{:S(2)}) collective-permute-start(f32[2,128,128]{2,1,0:T(8,128)S(1)} %pair.1.own_ref), channel_id=1, source_target_pairs={{0,96},{16,112},{32,0},{48,16},{64,32},{80,48},{96,64},{112,80},{1... | collective-permute-start | bytes 393224 | tf_op jit(solution)/shard_map/ppermute | solution.py:361
  11.2 6.0 %collective-permute-start.1 = (f32[2,128,128]{2,1,0:T(8,128)S(1)}, f32[2,128,128]{2,1,0:T(8,128)S(1)}, u32[]{:S(2)}, u32[]{:S(2)}) collective-permute-start(f32[2,128,128]{2,1,0:T(8,128)S(1)} %pair.1.own_ref), channel_id=1, source_target_pairs={{0,64},{16,80},{32,96},{48,112},{64,0},{80,16},{96,32},{112,48},{1... | collective-permute-start | bytes 393224 | tf_op jit(solution)/shard_map/ppermute | solution.py:361
  17.2 3.9 %collective-permute-start.4 = (f32[2,128,128]{2,1,0:T(8,128)S(1)}, f32[2,128,128]{2,1,0:T(8,128)S(1)}, u32[]{:S(2)}, u32[]{:S(2)}) collective-permute-start(f32[2,128,128]{2,1,0:T(8,128)S(1)} %get-tuple-element.77.all_ref), channel_id=1, source_target_pairs={{0,128},{16,144},{32,160},{48,176},{64,192},{80,208},{96,224},{112... | collective-permute-start | bytes 393224 | tf_op jit(solution)/shard_map/ppermute | solution.py:357
  21.2 3.7 %collective-permute-start.5 = (f32[2,136,128]{2,1,0:T(8,128)S(1)}, f32[2,136,128]{2,1,0:T(8,128)S(1)}, u32[]{:S(2)}, u32[]{:S(2)}) collective-permute-start(f32[2,136,128]{2,1,0:T(8,128)S(1)} %get-tuple-element.92), channel_id=1, source_target_pairs={{0,16},{16,0},{32,48},{48,32},{64,80},{80,64},{96,112},{112,96},{1... | collective-permute-start | bytes 417800 | tf_op jit(solution)/shard_map/ppermute | solution.py:357
  24.9 3.1 %copy-start = (f32[512]{0:T(512)S(1)}, f32[512]{0:T(512)}, u32[]{:S(2)}) copy-start(f32[512]{0:T(512)} %param.10) | copy-start | bytes 6148
  25.8 4.2 %collective-permute-start.6 = (f32[48,128]{1,0:T(8,128)S(1)}, f32[48,128]{1,0:T(8,128)S(1)}, u32[]{:S(2)}, u32[]{:S(2)}) collective-permute-start(f32[48,128]{1,0:T(8,128)S(1)} %get-tuple-element.95.mine_ref), channel_id=1, source_target_pairs={{0,1},{1,0},{2,3},{3,2},{4,5},{5,4},{6,7},{7,6},{8,9},{9,8},{10,11... | collective-permute-start | bytes 73736 | tf_op jit(solution)/shard_map/ppermute | solution.py:442
